TPU v7x, 32 devices: a whole 2x2x4 slice. The times are simulated.
32 devices in a mesh: wide: 32 (over z, y, x, core).
Axes of the slice: x: 2, y: 2, z: 4, core: 2. Of those that a mesh axis runs over, the one named last changes fastest.
Arguments:
- tokens: bfloat16 [16384, 768], P('wide'), may hold values from -6 to 6
- cotangent: bfloat16 [16384, 768], P('wide'), may hold values from -6 to 6
- cond: bfloat16 [96, 768], replicated, may hold values from -6 to 6
- kept: int32 [96, 128], replicated, may hold values from 0 to 255, as said below
- counts: int32 [32], replicated, may hold values from 256 to 512, as said below
- ada_w: bfloat16 [768, 4608], P('wide'), may hold values from -0.21875 to 0.21875
- ada_bias: bfloat16 [4608], P('wide'), may hold values from -3 to 3
- qkv_w: bfloat16 [768, 2304], P('wide'), may hold values from -0.21875 to 0.21875
- q_bias: bfloat16 [768], P('wide'), may hold values from -3 to 3
- v_bias: bfloat16 [768], P('wide'), may hold values from -3 to 3
- proj_w: bfloat16 [768, 768], P('wide'), may hold values from -0.875 to 0.875
- proj_bias: bfloat16 [768], P('wide'), may hold values from -3 to 3
- fc1_w: bfloat16 [768, 3072], P('wide'), may hold values from -0.21875 to 0.21875
- fc1_bias: bfloat16 [3072], P('wide'), may hold values from -3 to 3
- fc2_w: bfloat16 [3072, 768], P('wide'), may hold values from -0.109375 to 0.109375
- fc2_bias: bfloat16 [768], P('wide'), may hold values from -3 to 3
Outputs:
- out: bfloat16 [16384, 768], P('wide')
- tokens_grad: float32 [16384, 768], P('wide')
- cond_grad: float32 [96, 768], replicated
- ada_w_grad: float32 [768, 4608], P('wide')
- ada_bias_grad: float32 [4608], P('wide')
- qkv_w_grad: float32 [768, 2304], P('wide')
- q_bias_grad: float32 [768], P('wide')
- v_bias_grad: float32 [768], P('wide')
- proj_w_grad: float32 [768, 768], P('wide')
- proj_bias_grad: float32 [768], P('wide')
- fc1_w_grad: float32 [768, 3072], P('wide')
- fc1_bias_grad: float32 [3072], P('wide')
- fc2_w_grad: float32 [3072, 768], P('wide')
- fc2_bias_grad: float32 [768], P('wide')
Inputs may be any that keep to these rules, and one draw needn't show every extreme that they name: Each image's kept positions are distinct and increasing. The counts sum to 12288; in every draw some device has all its rows used and some device has 256 used rows.
All inputs are finite; a program needn't handle non-finite values.
Results may differ from a plain program's by a relative error of at most 0.013.
The roundings to bfloat16 on the way count: a program that leaves them out, or rounds other values in their place, can miss the bound.
Values may be sent and summed in bfloat16 or wider, within the bound.
No kernel may reach another device: no remote copies, remote signals or barrier semaphores. Data moves between devices by JAX's collectives and lax.ppermute only.
A program may use at most 192 MiB of HBM per device.

v0:
```python
import functools
import math

import jax
import jax.numpy as jnp
from jax import lax
from jax.experimental import pallas as pl
from jax.experimental.pallas import tpu as pltpu
from jax.sharding import PartitionSpec as P

D = 768
HEADS = 12
HD = 64
GRID = 16
LEN = 128
TOK_DEV = 512
SLOTS = TOK_DEV // LEN
F = 3072
BLOCKS = 16
NEAR_FIRST, FAR_FIRST = (0, 1, 2, 3), (0, 2, 1, 3)

NORM_EPS = 1e-06
GELU_COEF = 0.7978845608028654

f32 = jnp.float32
bf16 = jnp.bfloat16

VM = pl.BlockSpec(memory_space=pltpu.VMEM)
SM = pl.BlockSpec(memory_space=pltpu.SMEM)
ANY = pl.BlockSpec(memory_space=pl.ANY)
HBM = pl.BlockSpec(memory_space=pltpu.HBM)


def params(mib):
    return pltpu.CompilerParams(vmem_limit_bytes=mib * 1024 * 1024)


def cost(us):
    return pl.CostEstimate(flops=max(1, int(us * 1e9)), bytes_accessed=1, transcendentals=0)


def dot(left, right):
    return jnp.dot(left, right, preferred_element_type=f32)


def dot_nt(left, right):
    return lax.dot_general(left, right, (((1,), (1,)), ((), ())), preferred_element_type=f32)


def dot_tn(left, right):
    return lax.dot_general(left, right, (((0,), (0,)), ((), ())), preferred_element_type=f32)


def silu(values):
    return values / (1.0 + jnp.exp(-values))


def norm_parts(values):
    centred = values - jnp.mean(values, axis=-1, keepdims=True)
    spread = jnp.mean(centred * centred, axis=-1, keepdims=True)
    inverse = lax.rsqrt(spread + NORM_EPS)
    return centred * inverse, inverse


def norm_back(normed, inverse, scale_part, grad):
    t = grad * (1.0 + scale_part)
    mean_t = jnp.mean(t, axis=-1, keepdims=True)
    mean_tn = jnp.mean(t * normed, axis=-1, keepdims=True)
    return (t - mean_t - normed * mean_tn) * inverse


def rows_from(ref, start):
    base = pl.multiple_of(start // 8 * 8, 8)
    shift = start - base
    tall = LEN + 8
    turned = pltpu.roll(ref[pl.ds(base, tall), :], jnp.where(shift == 0, 0, tall - shift), 0)
    return turned[:LEN]


def slot_rows(slot):
    return slice(slot * LEN, (slot + 1) * LEN)


def mod_part(mod_ref, slot, part):
    return mod_ref[slot : slot + 1, part * D : (part + 1) * D]


def place_of(block, chip):
    rel = jnp.bitwise_xor(block, chip)
    return jnp.bitwise_and(rel, 3) * 4 + lax.shift_right_logical(rel, 2)


def lay_out(where_ref, halves, rows, targets, z_order, split_rows=False):
    chip, core = where_ref[0], where_ref[1]
    for side in range(2):
        half = core if side == 0 else 1 - core
        place = 0
        for ref in halves[side]:
            for spot in range(ref.shape[0] // rows):
                block = jnp.bitwise_xor(z_order[place % 4] * 4 + place // 4, chip)
                place += 1
                for target, first, width in targets:
                    if split_rows:
                        to_row, to_col = (2 * block + half) * rows, 0
                    else:
                        to_row, to_col = block * rows, pl.multiple_of(half * width, 128)
                    to_row = pl.multiple_of(to_row, 16)
                    target[pl.ds(to_row, rows), pl.ds(to_col, width)] = ref[
                        spot * rows : (spot + 1) * rows, first : first + width
                    ]


def start_all(copies):
    for copy in copies:
        copy.start()
    return copies


def fetch(pairs, sems, first=0):
    return start_all(
        [pltpu.make_async_copy(a, b, sems.at[first + i]) for i, (a, b) in enumerate(pairs)]
    )


def wait_all(copies):
    for copy in copies:
        copy.wait()


def begin_kernel(
    where_ref, counts_ref, cond_in, ada_in, tok_in, cot_in, qkv_in, proj_in, fc1_in,
    mine_ref, send_ref, edge_ref, place_ref, starts_ref, slots_ref, parts_ref,
    wide, cond, ada, sems,
):
    devices = counts_ref.shape[0]
    images = cond.shape[0]
    core, me = where_ref[1], where_ref[2]
    copies = []
    first = 0
    for ref in (qkv_in, proj_in, fc1_in):
        half = ref.shape[1] // 2
        for out, at in ((send_ref, 1 - core), (mine_ref, core)):
            copies.append(
                (
                    ref.at[:, pl.ds(pl.multiple_of(at * half, 128), half)],
                    out.at[:, pl.ds(first, half)],
                )
            )
        first += half
    copies.append((tok_in.at[pl.ds(0, LEN), :], edge_ref.at[pl.ds(0, LEN), :]))
    copies.append((cot_in.at[pl.ds(0, LEN), :], edge_ref.at[pl.ds(LEN, LEN), :]))
    copies = fetch([*copies, (cond_in, cond), (ada_in, ada)], sems)

    def step(d, first_row):
        count = counts_ref[d]
        begin = (first_row + LEN - 1) // LEN
        starts_ref[d] = begin

        @pl.when(d == me)
        def _():
            lead = begin * LEN - first_row
            place_ref[0] = lead
            place_ref[1] = count
            place_ref[2] = (first_row + count + LEN - 1) // LEN - begin
            place_ref[3] = count - lead
            place_ref[4] = begin

        return first_row + count

    lax.fori_loop(0, devices, step, jnp.int32(0))
    sub = lax.broadcasted_iota(jnp.int32, (8, images), 0)
    lane = lax.broadcasted_iota(jnp.int32, (8, images), 1)

    @pl.loop(0, devices)
    def _(d):
        hit = (lane == starts_ref[d] + sub) & (sub < SLOTS)
        wide[pl.ds(pl.multiple_of(d * 8, 8), 8), :] = jnp.where(hit, 1.0, 0.0)

    wait_all(copies)
    span = parts_ref.shape[2]
    for d in range(devices):
        parts_ref[d] = ada[:, d * span : (d + 1) * span]
    act = silu(cond[...].astype(f32)).astype(bf16)
    slots_ref[...] = dot(wide[...].astype(bf16), act).astype(bf16)


def ada_kernel(
    where_ref, starts_ref, early_ref, late_ref, ada_ref, cond_ref,
    qkv_sum_ref, proj_sum_ref, fc2_sum_ref, fc1_sum_ref,
    grad_ref, colsum_ref, last_ref, wide, packed,
):
    devices = early_ref.shape[0]
    images, own = cond_ref.shape[0], ada_ref.shape[0]
    me = where_ref[2]
    row = lax.broadcasted_iota(jnp.int32, (own, D), 0)
    lane = lax.broadcasted_iota(jnp.int32, (own, D), 1)
    chosen = jnp.where(lane == me * own + row, 1.0, 0.0).astype(bf16)
    act = silu(cond_ref[...].astype(f32)).astype(bf16)
    act_own = dot_nt(act, chosen).astype(bf16)
    cond_own = dot_nt(chosen, cond_ref[...])
    total = jnp.zeros((own, images), f32)
    for ref, parts in ((early_ref, (2, 3, 4, 5)), (late_ref, (0, 1))):
        many = len(parts)
        high = many * SLOTS
        tall = devices * high
        sub = lax.broadcasted_iota(jnp.int32, (high, images), 0)
        lane = lax.broadcasted_iota(jnp.int32, (high, images), 1)

        @pl.loop(0, devices)
        def _(d):
            hit = lane == starts_ref[d] + sub % SLOTS
            wide[pl.ds(pl.multiple_of(d * high, high), high), :] = jnp.where(hit, 1.0, 0.0)

        picker = wide[0:tall, :]
        act_rows = dot(picker.astype(bf16), act_own)
        part_down = lax.broadcasted_iota(jnp.int32, (tall, 1), 0) % high // SLOTS
        part_across = lax.broadcasted_iota(jnp.int32, (1, tall), 1) % high // SLOTS
        act_parts = jnp.concatenate(
            [jnp.where(part_down == i, act_rows, 0.0) for i in range(many)], axis=1
        ).astype(bf16)
        ours = lax.broadcasted_iota(jnp.int32, (8, tall), 0) == part_across
        ours = jnp.where(ours, 1.0, 0.0).astype(bf16)
        sums = ref[...].reshape(tall, D)
        grads = dot_tn(act_parts, sums)
        colsums = dot(ours, sums)
        back = jnp.zeros((own, tall), f32)
        for i, part in enumerate(parts):
            cols = slice(part * D, (part + 1) * D)
            grad_ref[:, cols] = grads[i * own : (i + 1) * own]
            colsum_ref[:, cols] = colsums[i : i + 1]
            back += jnp.where(part_across == i, dot_nt(ada_ref[:, cols], sums), 0.0)
        total += jnp.dot(back, picker, precision=lax.Precision.HIGHEST)
    gate = 1.0 / (1.0 + jnp.exp(-cond_own))
    total = total * (gate * (1.0 + cond_own * (1.0 - gate)))
    lanes = last_ref.shape[2]
    fc1_sum = fc1_sum_ref[...]
    both = qkv_sum_ref[...]
    vectors = [both[:, :D], both[:, 2 * D :], proj_sum_ref[...], fc2_sum_ref[...]]
    for d in range(devices):
        packed[...] = jnp.zeros(packed.shape, f32)
        packed[0:own, 0:images] = total
        for j in range(8):
            if j < 4:
                value = vectors[j][:, d * own : (d + 1) * own]
            else:
                at = (4 * d + j - 4) * own
                value = fc1_sum[:, at : at + own]
            packed[own + j : own + j + 1, 0:own] = value
        last_ref[d] = packed[...].astype(bf16)


def finish_kernel(got_ref, cond_ref, bias_ref, tall):
    devices, rows, _ = got_ref.shape
    own = rows - 8
    total = None
    for d in range(devices):
        got = got_ref[d].astype(f32)
        tall[d * own : (d + 1) * own, :] = got[0:own]
        total = got[own:rows] if total is None else total + got[own:rows]
    cond_ref[...] = tall[...].T[0 : cond_ref.shape[0], :]
    bias_ref[...] = total


def mod_kernel(slots_ref, cols_ref, addend_ref, out_ref):
    value = dot(slots_ref[...], cols_ref[...])
    for d in range(out_ref.shape[0]):
        out_ref[d] = value[d * 8 : (d + 1) * 8, :] + addend_ref[...]


def prep_kernel(
    place_ref, got_ref, tok_in, cot_in, halo_in, kept_in, table_in,
    res_ref, gc_ref, mod_ref, qkv_bias_ref, proj_bias_ref, fc2_bias_ref, fc1_bias_ref,
    tok, cot, halo, kept, table, sems,
):
    copies = fetch(
        [(table_in, table), (kept_in, kept), (halo_in, halo), (tok_in, tok), (cot_in, cot)], sems
    )
    devices, _, span = got_ref.shape
    width = D // devices
    qkv_bias_ref[:, D : 2 * D] = jnp.zeros((1, D), f32)
    for d in range(devices):
        got = got_ref[d]
        mod_ref[:, d * span : (d + 1) * span] = got[0:SLOTS]
        cols = slice(d * width, (d + 1) * width)
        qkv_bias_ref[:, cols] = got[4:5, 0:width]
        qkv_bias_ref[:, 2 * D + d * width : 2 * D + (d + 1) * width] = got[4:5, width : 2 * width]
        proj_bias_ref[:, cols] = got[4:5, 2 * width : 3 * width]
        fc2_bias_ref[:, cols] = got[4:5, 3 * width : 4 * width]
        fc1_bias_ref[:, d * 4 * width : (d + 1) * 4 * width] = got[5:6, 0 : 4 * width]
    lead, count, slots, begin = place_ref[0], place_ref[1], place_ref[2], place_ref[4]
    wait_all(copies)
    angles = table[...]
    high = angles.astype(bf16)
    rest = angles - high.astype(f32)
    middle = rest.astype(bf16)
    lowest = (rest - middle.astype(f32)).astype(bf16)
    images = kept.shape[0]
    sub = lax.broadcasted_iota(jnp.int32, (8, images), 0)
    lane = lax.broadcasted_iota(jnp.int32, (8, images), 1)
    picker = jnp.where(lane == begin + sub, 1.0, 0.0).astype(bf16)
    patches = dot(picker, kept[...].astype(f32).astype(bf16)).astype(jnp.int32)
    for slot in range(SLOTS):
        row = lax.broadcasted_iota(jnp.int32, (LEN, TOK_DEV), 0) + slot * LEN
        source = row + lead
        live = slot < slots
        column = lax.broadcasted_iota(jnp.int32, (LEN, TOK_DEV), 1)
        own = jnp.where((column == source) & (source < count) & live, 1.0, 0.0).astype(bf16)
        far = source[:, :LEN] - count
        spill = jnp.where((column[:, :LEN] == far) & live, 1.0, 0.0).astype(bf16)
        taken = dot(own, tok[...]) + dot(spill, halo[0:LEN, :])
        grad = dot(own, cot[...]) + dot(spill, halo[LEN : 2 * LEN, :])
        gc_ref[slot_rows(slot), :] = grad.astype(bf16)
        patch = patches[slot : slot + 1, :]
        index = lax.broadcasted_iota(jnp.int32, (GRID, LEN), 0)
        line = jnp.where((index == patch // GRID) & live, 1.0, 0.0).astype(bf16)
        across = jnp.where((index == patch % GRID) & live, 1.0, 0.0).astype(bf16)
        half = D // 2
        for start, picked in ((0, line), (half, across)):
            spot = dot_tn(picked, high) + (dot_tn(picked, middle) + dot_tn(picked, lowest))
            res_ref[slot_rows(slot), start : start + half] = taken[:, start : start + half] + spot


def head_masks():
    lane = lax.broadcasted_iota(jnp.int32, (1, 2 * HD), 1)
    first = jnp.where(lane < HD, 1.0, 0.0).astype(bf16)
    return first, (1.0 - first.astype(f32)).astype(bf16)


def both_heads(pair, masks):
    return jnp.concatenate([pair * masks[0], pair * masks[1]], axis=0)


def side_by_side(stacked):
    return jnp.concatenate([stacked[:LEN], stacked[LEN:]], axis=1)


def pair_probs(queries, keys):
    scores = dot_nt(queries, keys) * (1.0 / math.sqrt(HD))
    exp_terms = jnp.exp(scores - jnp.max(scores, axis=1, keepdims=True))
    return exp_terms * (1.0 / jnp.sum(exp_terms, axis=1, keepdims=True))


def qkv_kernel(
    where_ref, res_ref, mod_ref, bias_ref, near_ref, far_ref, ain_out, qkv_ref, weight_out, ain_ref, weight, sems
):
    for slot in range(SLOTS):
        normed, _ = norm_parts(res_ref[slot_rows(slot), :])
        ain_ref[slot_rows(slot), :] = (
            normed * (1.0 + mod_part(mod_ref, slot, 1)) + mod_part(mod_ref, slot, 0)
        ).astype(bf16)
    out = fetch([(ain_ref, ain_out)], sems)
    lay_out(where_ref, ([near_ref], [far_ref]), D // BLOCKS, [(weight, 0, 3 * D // 2)], NEAR_FIRST)
    out += fetch([(weight, weight_out)], sems, 1)

    @pl.loop(0, 3 * D // 256)
    def _(j):
        cols = pl.ds(pl.multiple_of(j * 256, 256), 256)
        qkv_ref[:, cols] = (dot(ain_ref[...], weight[:, cols]) + bias_ref[:, cols]).astype(bf16)

    wait_all(out)


def attend_kernel(qkv_ref, att_ref, att_out, sems):
    masks = head_masks()

    @pl.loop(0, SLOTS)
    def _(slot):
        rows = pl.ds(pl.multiple_of(slot * LEN, LEN), LEN)
        for pair in range(HEADS // 2):
            at = pair * 2 * HD
            probs = pair_probs(
                both_heads(qkv_ref[rows, at : at + 2 * HD], masks),
                qkv_ref[rows, D + at : D + at + 2 * HD],
            )
            values = both_heads(qkv_ref[rows, 2 * D + at : 2 * D + at + 2 * HD], masks)
            att_ref[rows, at : at + 2 * HD] = dot(
                side_by_side(probs.astype(bf16)), values
            ).astype(bf16)

    wait_all(fetch([(att_ref, att_out)], sems))


def join_kernel(*refs):
    *parts, both, sems = refs
    pairs, first = [], 0
    for ref in parts:
        rows = ref.shape[0]
        pairs.append((ref, both.at[pl.ds(first, rows), :]))
        first += rows
    wait_all(fetch(pairs, sems))


def cut_kernel(near_ref, x_ref, y_ref, most_ref, low_ref, high_ref, sems):
    rows = near_ref.shape[0]
    half = rows // 2
    pairs = [(y_ref.at[pl.ds(0, half), :], low_ref), (x_ref.at[pl.ds(half, half), :], high_ref)]
    for i, ref in enumerate((near_ref, x_ref, y_ref)):
        pairs.append((ref, most_ref.at[pl.ds(i * rows, rows), :]))
    wait_all(fetch(pairs, sems))


def flip(where_ref, lhs_ref, ordered, split_rows):
    chip, core = where_ref[0], where_ref[1]
    depth = ordered.shape[0]
    size = depth // BLOCKS
    if split_rows:
        size //= 2
    step = 384
    for m in range(depth // step):
        turned = lhs_ref[:, m * step : (m + 1) * step].T
        for i in range(step // size):
            block = m * (step // size) + i
            side = block % 2
            to = place_of(block // 2 if split_rows else block, chip) * size
            if split_rows:
                to = to + jnp.where(core == side, depth // 2, 0)
            ordered[pl.ds(pl.multiple_of(to, 16), size), :] = turned[i * size : (i + 1) * size, :]


def hidden_kernel(
    where_ref, res_ref, att_ref, mod_ref, gc_ref, proj_bias_ref, bias_ref, *rest
):
    mine, more, theirs, rest_far = rest[:4]
    branch_ref, mid_ref, min_ref, gmo_ref, colsum_ref, act_out, slope_out, send_out, keep_out, mid_out = rest[4:14]
    proj, weight, act, slope, ordered, made, out_sems = rest[14:]
    total = jnp.zeros((1, D), f32)
    for slot in range(SLOTS):
        rows = slot_rows(slot)
        grad = (mod_part(mod_ref, slot, 5) * gc_ref[rows, :].astype(f32)).astype(bf16)
        gmo_ref[rows, :] = grad
        total += jnp.sum(grad.astype(f32), axis=0, keepdims=True)
    colsum_ref[...] = total
    lay_out(
        where_ref,
        ([mine, more], [theirs, rest_far]),
        D // BLOCKS,
        [(proj, 0, D // 2), (weight, D // 2, F // 2)],
        NEAR_FIRST,
    )
    for j in range(D // 256):
        cols = slice(j * 256, (j + 1) * 256)
        branch_ref[:, cols] = dot(att_ref[...], proj[:, cols]) + proj_bias_ref[:, cols]
    for slot in range(SLOTS):
        rows = slot_rows(slot)
        mid = res_ref[rows, :] + mod_part(mod_ref, slot, 2) * branch_ref[rows, :]
        mid_ref[rows, :] = mid
        normed, _ = norm_parts(mid)
        min_ref[rows, :] = (
            normed * (1.0 + mod_part(mod_ref, slot, 4)) + mod_part(mod_ref, slot, 3)
        ).astype(bf16)

    @pl.loop(0, F // 256)
    def _(j):
        cols = pl.ds(pl.multiple_of(j * 256, 256), 256)
        u = dot(min_ref[...], weight[:, cols]) + bias_ref[:, cols]
        square = u * u
        bend = jnp.tanh(GELU_COEF * (u + 0.044715 * square * u))
        left = 0.5 * (1.0 + bend)
        act[:, cols] = (u * left).astype(bf16)
        slope[:, cols] = (
            left
            + 0.5 * u * (1.0 - bend * bend) * (GELU_COEF * (1.0 + 3.0 * 0.044715 * square))
        ).astype(bf16)

    out = fetch([(act, act_out), (slope, slope_out)], out_sems)
    out += fetch([(mid_ref, mid_out)], out_sems, 8)
    flip(where_ref, act, ordered, True)
    step = 512
    for j in range(F // step):
        made[j * step : (j + 1) * step, :] = dot(
            ordered[j * step : (j + 1) * step, :], gmo_ref[...]
        ).astype(bf16)
        to, at = (send_out, j) if j < F // step // 2 else (keep_out, j - F // step // 2)
        out += fetch(
            [(made.at[pl.ds(j * step, step), :], to.at[pl.ds(at * step, step), :])],
            out_sems,
            2 + j,
        )
    wait_all(out)


def flips_kernel(where_ref, first_ref, second_in, third_in, flipped_ref, second_out, third_out, second, third, turned, sems):
    copies = fetch([(second_in, second), (third_in, third)], sems)
    flip(where_ref, first_ref, flipped_ref, False)
    out = []
    for i, (ref, to) in enumerate(((second, second_out), (third, third_out))):
        wait_all([copies[i]])
        flip(where_ref, ref, turned.at[i], False)
        out += fetch([(turned.at[i], to)], sems, 2 + i)
    wait_all(out)


def wgrad_kernel(count, where_ref, *rest):
    lhs, rhs = rest[:count], rest[count : 2 * count]
    send_out, keep_out, send, keep, sems, *late = rest[2 * count :]
    core = where_ref[1]
    if late:
        *bufs, in_sems = late
        ins = fetch([(lhs[0], bufs[0]), (rhs[0], bufs[1]), (lhs[1], bufs[2])], in_sems)
        lhs, rhs = (bufs[0], bufs[2]), (bufs[1], rhs[1])
    step = 384
    first = 0
    out = []
    for ordered, rhs_ref in zip(lhs, rhs):
        if late:
            wait_all(ins[2:] if first else ins[:2])
        width = rhs_ref.shape[1] // 2
        for buf, to, half in ((send, send_out, 1 - core), (keep, keep_out, core)):
            cols = pl.ds(pl.multiple_of(half * width, 128), width)
            for j in range(D // step):
                rows = slice(j * step, (j + 1) * step)
                buf[rows, first : first + width] = dot(
                    ordered[rows, :], rhs_ref[:, cols]
                ).astype(bf16)
                here = (pl.ds(j * step, step), pl.ds(first, width))
                out += fetch([(buf.at[here], to.at[here])], sems, len(out))
        first += width
    wait_all(out)


def pair_sums(keep_in, got_ref, rows, spans, keep, sems, got=None):
    copies = []
    for i, first in enumerate(spans):
        here, there = pl.ds(i * rows, rows), pl.ds(first, rows)
        pairs = [(keep_in.at[there, :], keep.at[here, :])]
        if got is not None:
            pairs.append((got_ref.at[there, :], got.at[here, :]))
        copies.append(fetch(pairs, sems, 2 * i))

    def total(i):
        wait_all(copies[i])
        here = slice(i * rows, (i + 1) * rows)
        other = got_ref[spans[i] : spans[i] + rows, :] if got is None else got[here, :]
        return keep[here, :].astype(f32) + other.astype(f32)

    return total


def first_kernel(keep_in, got_ref, x_ref, y_ref, keep, sems, *got):
    rows = x_ref.shape[0] // 2
    total = pair_sums(keep_in, got_ref, rows, [2 * rows, 6 * rows, 5 * rows, 7 * rows], keep, sems, *got)
    for i in range(4):
        ref = (x_ref, y_ref)[i // 2]
        ref[i % 2 * rows : (i % 2 + 1) * rows, :] = total(i).astype(bf16)


def second_kernel(keep_in, got_ref, x_got_ref, y_got_ref, x_ref, y_ref, keep, sems, *got):
    rows = x_ref.shape[0]
    total = pair_sums(keep_in, got_ref, rows, [3 * rows, 4 * rows], keep, sems, *got)
    x_ref[...] = (total(0) + y_got_ref[rows:, :].astype(f32)).astype(bf16)
    y_ref[...] = (total(1) + x_got_ref[rows:, :].astype(f32)).astype(bf16)


def near_kernel(direct, keep_in, got_ref, x_one_ref, y_one_ref, x_two_ref, y_two_ref, *rest):
    if direct:
        outs, (keep, sems, *got) = rest[:4], rest[4:]
    else:
        send_ref, own_out, beyond_out, keep, sems, own, beyond, out_sems = rest
        got = ()
        outs = (send_ref, own, beyond)
    half = x_two_ref.shape[0]
    rows = half // 2
    total = pair_sums(keep_in, got_ref, half, [0, half], keep, sems, *got)
    for i, (one_ref, two_ref) in enumerate(((x_one_ref, y_two_ref), (y_one_ref, x_two_ref))):
        both = total(i) + one_ref[0:half, :].astype(f32) + two_ref[...].astype(f32)
        for j in range(2):
            z = 2 * i + j
            value = both[j * rows : (j + 1) * rows]
            if direct:
                outs[z][...] = value.astype(outs[z].dtype)
            elif j:
                outs[0][i * rows : (i + 1) * rows, :] = value.astype(bf16)
            else:
                outs[1 + i][...] = value
    if not direct:
        wait_all(fetch([(own, own_out), (beyond, beyond_out)], out_sems))


def beyond_kernel(got_ref, own_in, beyond_in, send_ref, total_out, own, beyond, sems):
    wait_all(fetch([(own_in, own), (beyond_in, beyond)], sems))
    rows = own.shape[0]
    send_ref[...] = (beyond[...] + got_ref[rows:, :].astype(f32)).astype(bf16)
    own[...] = own[...] + got_ref[0:rows, :].astype(f32)
    wait_all(fetch([(own, total_out)], sems, 2))


def lay_out_fc2(where_ref, near_ref, far_ref, fc2):
    lay_out(where_ref, ([near_ref], [far_ref]), F // (2 * BLOCKS), [(fc2, 0, D)], FAR_FIRST, True)


def fc2_back_kernel(
    where_ref, gmo_ref, slope_in, near_ref, far_ref, gh_ref, colsum_ref, fc2, slope, in_sems
):
    step = 512
    parts = [pl.ds(j * step, step) for j in range(F // step)]
    late = fetch([(slope_in.at[:, part], slope.at[:, part]) for part in parts], in_sems)
    lay_out_fc2(where_ref, near_ref, far_ref, fc2)
    for j in range(F // step):
        wait_all([late[j]])
        for half in range(2):
            cols = slice(j * step + half * 256, j * step + (half + 1) * 256)
            grad = dot_nt(gmo_ref[...], fc2[cols, :])
            value = (slope[:, cols].astype(f32) * grad).astype(bf16)
            gh_ref[:, cols] = value
            colsum_ref[:, cols] = jnp.sum(value.astype(f32), axis=0, keepdims=True)


def fc2_out_kernel(
    where_ref, place_ref, mod_ref, gc_ref, bias_ref, mid_in, act_in, near_ref, far_ref,
    tail_ref, gate_ref, out_out, mid_ref, act, fc2, mlp, made, in_sems,
):
    last = fetch([(act_in, act), (mid_in, mid_ref)], in_sems)
    lay_out_fc2(where_ref, near_ref, far_ref, fc2)
    wait_all(last)
    for j in range(D // 256):
        cols = slice(j * 256, (j + 1) * 256)
        mlp[0:TOK_DEV, cols] = dot(act[...], fc2[:, cols]) + bias_ref[:, cols]
    for slot in range(SLOTS):
        rows = slot_rows(slot)
        value = mlp[rows, :]
        gate_ref[slot : slot + 1, :] = jnp.sum(
            value * gc_ref[rows, :].astype(f32), axis=0, keepdims=True
        )
        value = mid_ref[rows, :] + mod_part(mod_ref, slot, 5) * value
        mlp[rows, :] = value
        made[rows, :] = value.astype(bf16)
    out = fetch([(made, out_out)], in_sems, 2)
    mlp[TOK_DEV:, :] = jnp.zeros((LEN + 8, D), f32)
    tail_ref[...] = rows_from(mlp, place_ref[3]).astype(bf16)
    wait_all(out)


def keep_sum(sums, part, slot, values):
    at = part * SLOTS + slot
    sums[at : at + 1, :] = jnp.sum(values, axis=0, keepdims=True)


def spread_sums(sums, spread_ref):
    value = sums[...].astype(bf16)
    for d in range(spread_ref.shape[0]):
        spread_ref[d] = value


def mid_back_kernel(
    where_ref, gh_ref, mid_ref, branch_ref, mod_ref, gc_ref, gate_ref, mine, more, theirs, rest_far,
    ga_ref, proj_sum_ref, gm_out, gb_out, spread_out,
    gm_ref, gb_ref, spread_ref, proj, weight, grads, sums, out_sems,
):
    lay_out(
        where_ref,
        ([mine, more], [theirs, rest_far]),
        D // BLOCKS,
        [(proj, 0, D // 2), (weight, D // 2, F // 2)],
        NEAR_FIRST,
    )
    for j in range(D // 256):
        cols = slice(j * 256, (j + 1) * 256)
        grads[:, cols] = dot_nt(gh_ref[...], weight[cols, :])
    total = jnp.zeros((1, D), f32)
    for slot in range(SLOTS):
        rows = slot_rows(slot)
        normed, inverse = norm_parts(mid_ref[rows, :])
        e = grads[rows, :]
        keep_sum(sums, 1, slot, e)
        keep_sum(sums, 2, slot, e * normed)
        grad_mid = gc_ref[rows, :].astype(f32) + norm_back(
            normed, inverse, mod_part(mod_ref, slot, 4), e
        )
        gm_ref[rows, :] = grad_mid
        keep_sum(sums, 0, slot, branch_ref[rows, :] * grad_mid)
        value = (mod_part(mod_ref, slot, 2) * grad_mid).astype(bf16)
        gb_ref[rows, :] = value
        total += jnp.sum(value.astype(f32), axis=0, keepdims=True)
    proj_sum_ref[...] = total
    sums[3 * SLOTS :, :] = gate_ref[...]
    spread_sums(sums, spread_ref)
    out = fetch([(gm_ref, gm_out), (gb_ref, gb_out), (spread_ref, spread_out)], out_sems)
    for j in range(D // 256):
        cols = slice(j * 256, (j + 1) * 256)
        ga_ref[:, cols] = dot_nt(gb_ref[...], proj[cols, :]).astype(bf16)
    wait_all(out)


def probs_kernel(qk_in, probs_out, qk, probs, sems):
    masks = head_masks()
    copies = fetch(
        [
            (qk_in.at[pl.ds(slot * LEN, LEN), pl.ds(0, 2 * D)], qk.at[pl.ds(slot * LEN, LEN), :])
            for slot in range(SLOTS)
        ],
        sems,
    )
    out = []
    for slot in range(SLOTS):
        wait_all([copies[slot]])
        rows = slot_rows(slot)
        tall = HEADS // 2 * LEN
        for pair in range(HEADS // 2):
            at = pair * 2 * HD
            queries = both_heads(qk[rows, at : at + 2 * HD], masks)
            scores = dot_nt(qk[rows, D + at : D + at + 2 * HD], queries) * (1.0 / math.sqrt(HD))
            exp_terms = jnp.exp(scores - jnp.max(scores, axis=0, keepdims=True))
            first = slot * tall + pair * LEN
            probs[first : first + LEN, :] = exp_terms * (
                1.0 / jnp.sum(exp_terms, axis=0, keepdims=True)
            )
        here = pl.ds(slot * tall, tall)
        out += fetch([(probs.at[here, :], probs_out.at[here, :])], sems, SLOTS + slot)
    wait_all(out)


def attend_back_kernel(qkv_in, probs_in, ga_ref, gqkv_ref, colsum_ref, qkv, probs, sems):
    masks = head_masks()
    first_head = lax.broadcasted_iota(jnp.int32, (1, 2 * HD), 1) < HD
    scale = 1.0 / math.sqrt(HD)
    tall = HEADS // 2 * LEN
    copies = []
    for slot in range(SLOTS):
        here, there = pl.ds(slot * LEN, LEN), pl.ds(slot * tall, tall)
        copies += fetch(
            [
                (qkv_in.at[here, :], qkv.at[here, :]),
                (probs_in.at[there, :], probs.at[there, :]),
            ],
            sems,
            2 * slot,
        )
    for first in range(0, SLOTS, 2):
        wait_all(copies[2 * first : 2 * first + 4])

        @pl.loop(first, first + 2)
        def _(slot):
            rows = pl.ds(pl.multiple_of(slot * LEN, LEN), LEN)
            for pair in range(HEADS // 2):
                at = pair * 2 * HD
                q_cols, k_cols, v_cols = (
                    slice(part * D + at, part * D + at + 2 * HD) for part in range(3)
                )
                chances = probs[pl.ds(pl.multiple_of(slot * tall + pair * LEN, LEN), LEN), :]
                grads = both_heads(ga_ref[rows, q_cols], masks)
                weighed = chances * dot_nt(qkv[rows, v_cols], grads)
                inner = jnp.sum(weighed, axis=0, keepdims=True)
                grad_scores = (weighed - chances * inner).astype(bf16)
                grad_queries = dot_tn(grad_scores, qkv[rows, k_cols]) * scale
                gqkv_ref[rows, q_cols] = jnp.where(
                    first_head, grad_queries[:LEN], grad_queries[LEN:]
                ).astype(bf16)
                queries = both_heads(qkv[rows, q_cols], masks)
                gqkv_ref[rows, k_cols] = (dot(grad_scores, queries) * scale).astype(bf16)
                gqkv_ref[rows, v_cols] = dot(chances.astype(bf16), grads).astype(bf16)

    for j in range(3 * D // 256):
        cols = slice(j * 256, (j + 1) * 256)
        colsum_ref[:, cols] = jnp.sum(gqkv_ref[:, cols].astype(f32), axis=0, keepdims=True)


def start_back_kernel(
    place_ref, gqkv_ref, mod_ref, out_tail_ref, res_in, gm_in, weight_in,
    tg_out, tail_out, spread_out, weight, grads, res, gm, sums, tail_ref, spread_ref, in_sems, out_sems,
):
    step = 256
    parts = [pl.ds(j * step, step) for j in range(D // step)]
    copies = fetch([(weight_in.at[part, :], weight.at[part, :]) for part in parts], in_sems)
    late = fetch([(res_in, res), (gm_in, gm)], in_sems, len(parts))
    for j in range(D // step):
        wait_all([copies[j]])
        cols = slice(j * step, (j + 1) * step)
        grads[0:TOK_DEV, cols] = dot_nt(gqkv_ref[...], weight[cols, :])
    wait_all(late)
    out = []
    for slot in range(SLOTS):
        rows = slot_rows(slot)
        normed, inverse = norm_parts(res[rows, :])
        e = grads[rows, :]
        keep_sum(sums, 0, slot, e)
        keep_sum(sums, 1, slot, e * normed)
        grads[rows, :] = gm[rows, :] + norm_back(normed, inverse, mod_part(mod_ref, slot, 1), e)
        here = pl.ds(slot * LEN, LEN)
        out += fetch([(grads.at[here, :], tg_out.at[here, :])], out_sems, slot)
    spread_sums(sums, spread_ref)
    out += fetch([(spread_ref, spread_out)], out_sems, SLOTS)
    grads[TOK_DEV:, :] = jnp.zeros((LEN + 8, D), f32)
    tail = rows_from(grads, place_ref[3])
    high = tail.astype(bf16)
    tail_ref[0:LEN, :] = out_tail_ref[...]
    tail_ref[LEN : 2 * LEN, :] = high
    tail_ref[2 * LEN :, :] = (tail - high.astype(f32)).astype(bf16)
    wait_all(out + fetch([(tail_ref, tail_out)], out_sems, SLOTS + 1))


def place_kernel(
    place_ref, tail_ref, tok_in, cot_in, out_in, tg_in,
    final_out, final_tg, out_rows, tg_rows, tok, cot, out, made_out, made_tg, sems,
):
    lead, count = place_ref[0], place_ref[1]
    copies = fetch(
        [(out_in, out), (tok_in, tok), (tg_in, tg_rows.at[pl.ds(LEN, TOK_DEV), :]), (cot_in, cot)],
        sems,
    )
    for rows in (out_rows, tg_rows):
        rows[0:LEN, :] = jnp.zeros((LEN, D), f32)
        rows[LEN + TOK_DEV :, :] = jnp.zeros((8, D), f32)
    wait_all(copies[:2])
    out_rows[LEN : LEN + TOK_DEV, :] = out[...].astype(f32)
    last = []
    out_tail = tail_ref[0:LEN, :].astype(f32)
    tg_tail = tail_ref[LEN : 2 * LEN, :].astype(f32) + tail_ref[2 * LEN :, :].astype(f32)
    for k, (rows, tail, pad, made, final) in enumerate(
        ((out_rows, out_tail, tok, made_out, final_out), (tg_rows, tg_tail, cot, made_tg, final_tg))
    ):
        if k:
            wait_all(copies[2:])
        for slot in range(SLOTS):
            here = slot_rows(slot)
            row = lax.broadcasted_iota(jnp.int32, (LEN, 1), 0) + slot * LEN
            value = rows_from(rows, LEN - lead + slot * LEN)
            if slot == 0:
                value = jnp.where(row < lead, tail, value)
            value = jnp.where(row < count, value, pad[here, :].astype(f32))
            made[here, :] = value.astype(made.dtype)
        last += fetch([(made, final)], sems, 4 + k)
    wait_all(last)


def shape(*dims, dtype=f32):
    return jax.ShapeDtypeStruct(dims, dtype)


def call(kernel, outs, scratch, mib, ins, spaces, after=(), out_specs=None, us=0, zeros=False):
    taken, held, made = len(ins), len(after), len(outs)
    out_specs = out_specs or [VM] * made

    def body(*refs):
        first = taken + held
        kernel(*refs[:taken], *refs[first : first + made], *refs[first + made + 1 :])
        if zeros:
            refs[first + made][...] = jnp.zeros((8, 128), f32)

    def settled(item):
        is_token = item.shape == (8, 128) and item.dtype == f32
        return pltpu.with_memory_space_constraint(item, pltpu.HBM) if is_token else item

    def placed(item, spec):
        return pltpu.with_memory_space_constraint(item, pltpu.HBM) if spec is HBM else item

    out_specs = [*out_specs, VM if zeros else HBM]
    out_shape = [
        pltpu.HBM(item.shape, item.dtype) if spec is HBM else item
        for item, spec in zip([*outs, shape(8, 128)], out_specs)
    ]
    *results, token = pl.pallas_call(
        body,
        out_shape=out_shape,
        in_specs=list(spaces) + [ANY] * held,
        out_specs=out_specs,
        scratch_shapes=scratch,
        compiler_params=params(mib),
        cost_estimate=cost(us),
        name=getattr(kernel, "func", kernel).__name__,
    )(*[placed(item, spec) for item, spec in zip(ins, spaces)], *[settled(item) for item in after])
    return results, token


def tie(value, token):
    return jnp.where(token[0, 0] == 0.0, value, jnp.zeros_like(value))


def join(parts, after=(), us=0, zeros=False):
    rows = sum(part.shape[0] for part in parts)
    (both,), token = call(
        join_kernel,
        [shape(rows, parts[0].shape[1], dtype=parts[0].dtype)],
        [pltpu.SemaphoreType.DMA((len(parts),))],
        8,
        parts,
        [ANY] * len(parts),
        after=after,
        out_specs=[ANY],
        us=us,
        zeros=zeros,
    )
    return both, token


def tie(value, token):
    return jnp.where(token[0, 0] == 0.0, value, jnp.zeros_like(value))


def low(value):
    return value.astype(bf16)


class Links:
    def __init__(self, devices):
        self.devices = devices
        self.cube = devices == 32
        self.me = lax.axis_index("wide").astype(jnp.int32)
        self.core = self.me % 2 if self.cube else jnp.int32(0)
        self.chip = self.me // 2 if self.cube else jnp.int32(0)
        self.where = jnp.stack([self.chip, self.core, self.me])

    def swap(self, array, bits):
        return lax.ppermute(array, "wide", [(i, i ^ bits) for i in range(self.devices)])

    def by_core(self, first, second):
        return jnp.where(self.core == 0, first, second)

    def pair(self, mine, got):
        return self.by_core(
            jnp.concatenate([mine, got], axis=0), jnp.concatenate([got, mine], axis=0)
        )

    def along_z(self, pair):
        return jnp.concatenate(
            [pair, self.swap(pair, 8), self.swap(pair, 16), self.swap(pair, 24)], axis=0
        )

    def doubled_z(self, pair):
        two = jnp.concatenate([pair, self.swap(pair, 8)], axis=0)
        return jnp.concatenate([two, self.swap(two, 16)], axis=0)

    def gathered(self, shards):
        halves = [[], []]
        for shard in shards:
            whole = lax.all_gather(shard, "wide", axis=0, tiled=True)
            rows, width = whole.shape[0], whole.shape[1] // 2
            whole = whole.reshape(4, 4, rows // BLOCKS, -1).transpose(1, 0, 2, 3)
            whole = whole.reshape(rows, -1)
            halves[0].append(whole[:, :width])
            halves[1].append(whole[:, width:])
        return [jnp.concatenate(half, axis=1) for half in halves]

    def scattered(self, send, keep, widths):
        outs, first = [], 0
        rows = keep.shape[0]
        for width in widths:
            cols = slice(first, first + width)
            whole = jnp.concatenate([keep[:, cols], send[:, cols]], axis=1)
            whole = whole.reshape(4, 4, rows // BLOCKS, -1).transpose(1, 0, 2, 3)
            whole = whole.reshape(rows, -1).astype(f32)
            outs.append(lax.psum_scatter(whole, "wide", scatter_dimension=0, tiled=True))
            first += width
        return outs

    def scattered_rows(self, send, keep):
        whole = jnp.stack([keep, send]).reshape(2, 4, 4, -1, D)
        whole = whole.transpose(2, 1, 0, 3, 4).reshape(-1, D)
        return lax.psum_scatter(whole.astype(f32), "wide", scatter_dimension=0, tiled=True)

    def gathered_rows(self, shard):
        whole = lax.all_gather(shard, "wide", axis=0, tiled=True).reshape(4, 4, 2, -1, D)
        whole = jnp.stack([whole[z] for z in FAR_FIRST], axis=1)
        return [whole[:, :, half].reshape(-1, D) for half in range(2)]

    def first(self, keep, got, after, copied=False):
        rows, width = keep.shape[0] // 4, keep.shape[1]
        (x, y), token = call(
            first_kernel,
            [shape(rows, width, dtype=bf16)] * 2,
            [pltpu.VMEM((2 * rows, width), bf16), pltpu.SemaphoreType.DMA((8,))]
            + [pltpu.VMEM((2 * rows, width), bf16)] * copied,
            16,
            [keep, got],
            [HBM, HBM if copied else VM],
            after=after,
        )
        return [self.swap(x, 2), self.swap(y, 4)], token

    def second(self, keep, got, ones, after, copied=False):
        rows, width = keep.shape[0] // 8, keep.shape[1]
        (x, y), token = call(
            second_kernel,
            [shape(rows, width, dtype=bf16)] * 2,
            [pltpu.VMEM((2 * rows, width), bf16), pltpu.SemaphoreType.DMA((4,))]
            + [pltpu.VMEM((2 * rows, width), bf16)] * copied,
            16,
            [keep, got, *ones],
            [HBM, HBM if copied else VM, VM, VM],
            after=after,
            us=100,
        )
        return [self.swap(x, 2), self.swap(y, 4)], token

    def near_sum(self, keep, got, ones, twos, direct, after):
        tall, width = keep.shape[0] // 4, keep.shape[1]
        rows = tall // 4
        if direct:
            outs = [shape(rows, width)] + [shape(rows, width, dtype=bf16)] * 3
        else:
            outs = [shape(2 * rows, width, dtype=bf16)] + [shape(rows, width)] * 2
        scratch = [pltpu.VMEM((tall, width), bf16), pltpu.SemaphoreType.DMA((4,))]
        scratch += [pltpu.VMEM((tall, width), bf16)] * direct
        if not direct:
            scratch += [pltpu.VMEM((rows, width), f32)] * 2 + [pltpu.SemaphoreType.DMA((2,))]
        return call(
            functools.partial(near_kernel, direct),
            outs,
            scratch,
            16,
            [keep, got, *ones, *twos],
            [HBM, HBM if direct else VM] + [VM] * 4,
            after=after,
            out_specs=[VM] * 4 if direct else [VM, HBM, HBM],
            us=100,
        )

    def z_sum(self, token, own, *parts):
        own = tie(own, token)
        for part, bits in zip(parts, (8, 16, 24)):
            own = own + self.swap(part, bits).astype(f32)
        return own

    def halved_z(self, send, own, beyond, after):
        (send, total), token = call(
            beyond_kernel,
            [shape(*own.shape, dtype=bf16), shape(*own.shape)],
            [pltpu.VMEM(own.shape, f32)] * 2 + [pltpu.SemaphoreType.DMA((3,))],
            8,
            [self.swap(send, 8), own, beyond],
            [VM, HBM, HBM],
            after=after,
            out_specs=[VM, HBM],
        )
        return total, self.swap(send, 16), token

    def own_rows(self, own, widths):
        rows = own.shape[0] // 2
        mine = self.by_core(own[:rows], own[rows:])
        got = self.swap(self.by_core(own[rows:], own[:rows]), 1)
        outs, first = [], 0
        for width in widths:
            a, b = mine[:, first : first + width], got[:, first : first + width]
            outs.append(
                self.by_core(jnp.concatenate([a, b], axis=1), jnp.concatenate([b, a], axis=1))
            )
            first += width
        return outs


def on_device(
    tokens,
    cotangent,
    cond,
    kept,
    counts,
    ada_w,
    ada_bias,
    qkv_w,
    q_bias,
    v_bias,
    proj_w,
    proj_bias,
    fc1_w,
    fc1_bias,
    fc2_w,
    fc2_bias,
):
    devices = lax.axis_size("wide")
    images = cond.shape[0]
    span = ada_bias.shape[0]
    own_dim = ada_w.shape[0]
    links = Links(devices)
    me, where, cube = links.me, links.where, links.cube
    rows = TOK_DEV
    dma = pltpu.SemaphoreType.DMA
    half_sum = (qkv_w.shape[1] + proj_w.shape[1] + fc1_w.shape[1]) // 2

    (mine, send, edge, place, starts, cond_slots, ada_parts), _ = call(
        begin_kernel,
        [
            shape(own_dim, half_sum, dtype=bf16),
            shape(own_dim, half_sum, dtype=bf16),
            shape(2 * LEN, D, dtype=bf16),
            shape(8, dtype=jnp.int32),
            shape(devices, dtype=jnp.int32),
            shape(devices * 8, D, dtype=bf16),
            shape(devices, own_dim, span, dtype=bf16),
        ],
        [
            pltpu.VMEM((devices * 8, images), f32),
            pltpu.VMEM(cond.shape, bf16),
            pltpu.VMEM(ada_w.shape, bf16),
            dma((10,)),
        ],
        16,
        [where, counts, cond, ada_w, tokens, cotangent, qkv_w, proj_w, fc1_w],
        [SM, SM] + [HBM] * 7,
        out_specs=[VM, VM, VM, SM, SM, VM, VM],
    )
    if cube:
        pair = links.pair(mine, links.swap(send, 1))
        near_one = links.along_z(pair[:, : 3 * D // 2])
        before_mod = [pair]
    else:
        before_mod = []
    halo = lax.ppermute(edge, "wide", [(i + 1, i) for i in range(devices - 1)])

    ada_cols = lax.all_to_all(ada_parts, "wide", 0, 0, tiled=True)
    ada_cols = ada_cols.reshape(D, span)
    lanes = lambda items: jnp.pad(
        jnp.concatenate(items), (0, span - sum(i.shape[0] for i in items))
    ).reshape(1, span)
    addend = jnp.concatenate(
        [
            jnp.broadcast_to(ada_bias.reshape(1, span), (SLOTS, span)),
            lanes([q_bias, v_bias, proj_bias, fc2_bias]),
            lanes([fc1_bias]),
            jnp.zeros((2, span), bf16),
        ],
        axis=0,
    ).astype(f32)
    (mod_cols,), mod_ran = call(
        mod_kernel,
        [shape(devices, 8, span)],
        [],
        16,
        [cond_slots, ada_cols, addend],
        [VM] * 3,
        after=before_mod,
        zeros=True,
    )
    mixed = lax.all_to_all(mod_cols, "wide", 0, 0, tiled=True)

    quarter = D // 4
    frequency = jnp.exp(-math.log(10000.0) * jnp.arange(quarter).astype(f32) / quarter)
    angle = jnp.arange(GRID).astype(f32)[:, None] * frequency[None, :]
    table = jnp.concatenate([jnp.sin(angle), jnp.cos(angle)], axis=1)
    if cube:
        near_one = tie(near_one, mod_ran)
        over = [links.swap(near_one, bits) for bits in (2, 4, 6)]
        pair_two = tie(pair[:, 3 * D // 2 :], mod_ran)
        two = jnp.concatenate([pair_two, links.swap(pair_two, 8)], axis=0)
        before_prep = [near_one, two]
    else:
        before_prep = []
    (residual, grad_out, mod, qkv_bias, proj_bias_all, fc2_bias_all, fc1_bias_all), prepared = call(
        prep_kernel,
        [
            shape(rows, D),
            shape(rows, D, dtype=bf16),
            shape(SLOTS, 6 * D),
            shape(1, 3 * D),
            shape(1, D),
            shape(1, D),
            shape(1, F),
        ],
        [
            pltpu.VMEM((rows, D), bf16),
            pltpu.VMEM((rows, D), bf16),
            pltpu.VMEM((2 * LEN, D), bf16),
            pltpu.VMEM(kept.shape, jnp.int32),
            pltpu.VMEM(table.shape, f32),
            dma((5,)),
        ],
        16,
        [place, mixed, tokens, cotangent, halo, kept, table],
        [SM, VM, HBM, HBM, ANY, HBM, ANY],
        after=before_prep,
        us=10,
    )

    if cube:
        near_two = jnp.concatenate([two, links.swap(two, 16)], axis=0)
        qkv_near, joined = join([near_one, *over], [prepared, near_two])
        qkv_far = links.swap(qkv_near, 1)
        over_x, over_y = links.swap(near_two, 2), links.swap(near_two, 4)
        before_qkv = []
    else:
        qkv_near, qkv_far = links.gathered([qkv_w])
        before_qkv = []

    (attn_in, qkv, qkv_laid), qkv_ran = call(
        qkv_kernel,
        [
            shape(rows, D, dtype=bf16),
            shape(rows, 3 * D, dtype=bf16),
            shape(D, 3 * D, dtype=bf16),
        ],
        [pltpu.VMEM((rows, D), bf16), pltpu.VMEM((D, 3 * D), bf16), dma((2,))],
        16,
        [where, residual, mod, qkv_bias, qkv_near, qkv_far],
        [SM] + [VM] * 5,
        after=before_qkv,
        out_specs=[HBM, VM, HBM],
        zeros=True,
    )
    before_attend = [qkv_ran]
    if cube:
        two, _ = join([fc2_w, links.swap(fc2_w, 16)], [qkv_ran])
        before_attend.append(two)
        near_three = jnp.concatenate([two, links.swap(two, 8)], axis=0)
    (attended, attended_kept), attend_ran = call(
        attend_kernel,
        [shape(rows, D, dtype=bf16)] * 2,
        [dma((1,))],
        16,
        [qkv],
        [VM],
        after=before_attend,
        out_specs=[VM, HBM],
        zeros=True,
    )
    if cube:
        half = near_two.shape[0] // 2
        width = near_two.shape[1]
        (most, low_half, high_half), _ = call(
            cut_kernel,
            [
                shape(6 * half, width, dtype=bf16),
                shape(half, width, dtype=bf16),
                shape(half, width, dtype=bf16),
            ],
            [dma((5,))],
            8,
            [near_two, over_x, over_y],
            [ANY] * 3,
            after=[attend_ran],
            out_specs=[ANY] * 3,
        )
        most_far = links.swap(most, 1)
        diag = [links.swap(low_half, 2), links.swap(high_half, 4)]
        diag, _ = join(diag)
        mid_halves = [most, diag, most_far, links.swap(diag, 1)]
        over = [links.swap(near_three, bits) for bits in (2, 4, 6)]
    else:
        mid_near, mid_far = links.gathered([proj_w, fc1_w])
        cut = 3 * D // 4
        mid_halves = [mid_near[:cut], mid_near[cut:], mid_far[:cut], mid_far[cut:]]
        fc2_near, fc2_far = links.gathered_rows(fc2_w)

    (
        branch, middle, mlp_in, grad_mlp_out, fc2_bias_sum, activated, slope, fc2_send, fc2_keep,
        middle_kept,
    ), hidden_ran = call(
        hidden_kernel,
        [
            shape(rows, D),
            shape(rows, D),
            shape(rows, D, dtype=bf16),
            shape(rows, D, dtype=bf16),
            shape(1, D),
            shape(rows, F, dtype=bf16),
            shape(rows, F, dtype=bf16),
            shape(F // 2, D, dtype=bf16),
            shape(F // 2, D, dtype=bf16),
            shape(rows, D),
        ],
        [
            pltpu.VMEM((D, D), bf16),
            pltpu.VMEM((D, F), bf16),
            pltpu.VMEM((rows, F), bf16),
            pltpu.VMEM((rows, F), bf16),
            pltpu.VMEM((F, rows), bf16),
            pltpu.VMEM((F, D), bf16),
            dma((9,)),
        ],
        32,
        [where, residual, attended, mod, grad_out, proj_bias_all, fc1_bias_all, *mid_halves],
        [SM] + [VM] * 10,
        out_specs=[VM] * 5 + [HBM] * 5,
    )
    def weight_grad(*pairs, after=()):
        half = sum(right.shape[1] for _, right in pairs) // 2
        scratch = [pltpu.VMEM((D, half), bf16), pltpu.VMEM((D, half), bf16), dma((8,))]
        spaces = [VM, VM]
        if len(pairs) == 2:
            scratch += [
                pltpu.VMEM((D, rows), bf16),
                pltpu.VMEM((rows, D), bf16),
                pltpu.VMEM((D, rows), bf16),
                dma((3,)),
            ]
            spaces = [HBM, HBM, HBM, VM]
        return call(
            functools.partial(wgrad_kernel, len(pairs)),
            [shape(D, half, dtype=bf16)] * 2,
            scratch,
            20,
            [where, *[left for left, _ in pairs], *[right for _, right in pairs]],
            [SM, *spaces],
            after=after,
            out_specs=[HBM] * 2,
        )

    (mlp_flipped, attended_flipped, attn_flipped), flipped = call(
        flips_kernel,
        [shape(D, rows, dtype=bf16)] * 3,
        [pltpu.VMEM((rows, D), bf16)] * 2 + [pltpu.VMEM((2, D, rows), bf16), dma((4,))],
        16,
        [where, mlp_in, attended_kept, attn_in],
        [SM, VM, HBM, HBM],
        after=[hidden_ran],
        out_specs=[VM, HBM, HBM],
    )
    (probs,), probs_ran = call(
        probs_kernel,
        [shape(SLOTS * HEADS // 2 * LEN, 2 * LEN)],
        [
            pltpu.VMEM((rows, 2 * D), bf16),
            pltpu.VMEM((SLOTS * HEADS // 2 * LEN, 2 * LEN), f32),
            dma((2 * SLOTS,)),
        ],
        16,
        [qkv],
        [HBM],
        after=[flipped],
        out_specs=[HBM],
    )
    if cube:
        fc2_got = links.swap(fc2_send, 1)
        fc2_near, gathered = join([near_three, *over], [probs_ran], us=100)
        fc2_far = links.swap(fc2_near, 1)
        fc2_ones, fc2_first = links.first(fc2_keep, fc2_got, [gathered])
        before_fc2 = [fc2_first]
    else:
        before_fc2 = []
    (grad_hidden, fc1_bias_sum), _ = call(
        fc2_back_kernel,
        [shape(rows, F, dtype=bf16), shape(1, F)],
        [pltpu.VMEM((F, D), bf16), pltpu.VMEM((rows, F), bf16), dma((6,))],
        20,
        [where, grad_mlp_out, slope, fc2_near, fc2_far],
        [SM, VM, HBM, VM, VM],
        after=before_fc2,
    )
    (fc1_send, fc1_keep), fc1_ran = weight_grad((mlp_flipped, grad_hidden))
    (out_tail, gate_two_sum, result), out_ran = call(
        fc2_out_kernel,
        [shape(LEN, D, dtype=bf16), shape(SLOTS, D), shape(rows, D, dtype=bf16)],
        [
            pltpu.VMEM((rows, D), f32),
            pltpu.VMEM((rows, F), bf16),
            pltpu.VMEM((F, D), bf16),
            pltpu.VMEM((rows + LEN + 8, D), f32),
            pltpu.VMEM((rows, D), bf16),
            dma((3,)),
        ],
        20,
        [where, place, mod, grad_out, fc2_bias_all, middle_kept, activated, fc2_near, fc2_far],
        [SM] * 2 + [VM] * 3 + [HBM] * 2 + [VM] * 2,
        after=[fc1_ran],
        out_specs=[VM] * 2 + [HBM],
    )
    if cube:
        fc1_got = links.swap(fc1_send, 1)
        fc2_twos, fc2_second = links.second(fc2_keep, fc2_got, fc2_ones, [out_ran])
        fc1_ones, fc1_first = links.first(fc1_keep, fc1_got, [fc2_second])
        before_mid = [fc1_first]
    else:
        before_mid = [out_ran]
    (grad_attended, proj_bias_sum, grad_middle, grad_branch, early), mid_ran = call(
        mid_back_kernel,
        [
            shape(rows, D, dtype=bf16),
            shape(1, D),
            shape(rows, D),
            shape(rows, D, dtype=bf16),
            shape(devices, 16, D, dtype=bf16),
        ],
        [
            pltpu.VMEM((rows, D), f32),
            pltpu.VMEM((rows, D), bf16),
            pltpu.VMEM((devices, 16, D), bf16),
            pltpu.VMEM((D, D), bf16),
            pltpu.VMEM((D, F), bf16),
            pltpu.VMEM((rows, D), f32),
            pltpu.VMEM((16, D), f32),
            dma((3,)),
        ],
        20,
        [where, grad_hidden, middle, branch, mod, grad_out, gate_two_sum, *mid_halves],
        [SM] + [VM] * 10,
        out_specs=[VM] * 2 + [HBM] * 3,
        after=before_mid,
    )
    early = lax.all_to_all(early, "wide", 0, 0, tiled=True)
    if cube:
        fc2_near_sum, fc2_summed = links.near_sum(
            fc2_keep, fc2_got, fc2_ones, fc2_twos, False, [mid_ran]
        )
        before_back = [fc2_summed]
    else:
        before_back = []
    (grad_qkv, qkv_bias_sum), back_ran = call(
        attend_back_kernel,
        [shape(rows, 3 * D, dtype=bf16), shape(1, 3 * D)],
        [
            pltpu.VMEM((rows, 3 * D), bf16),
            pltpu.VMEM(probs.shape, f32),
            dma((2 * SLOTS,)),
        ],
        16,
        [qkv, probs, grad_attended],
        [HBM, HBM, VM],
        after=before_back,
    )
    before_qkv = []
    if cube:
        fc2_own, fc2_beyond, fc2_halved = links.halved_z(*fc2_near_sum, [back_ran])
        fc1_twos, fc1_second = links.second(fc1_keep, fc1_got, fc1_ones, [fc2_halved])
        before_qkv.append(fc1_second)
    (qkv_send, qkv_keep), qkv_grad_ran = weight_grad(
        (attended_flipped, grad_branch), (attn_flipped, grad_qkv), after=before_qkv
    )
    if cube:
        qkv_got = links.swap(qkv_send, 1)
    if cube:
        fc1_near_sum, fc1_summed = links.near_sum(
            fc1_keep, fc1_got, fc1_ones, fc1_twos, False, [qkv_grad_ran]
        )
        qkv_ones, qkv_first = links.first(qkv_keep, qkv_got, [fc1_summed])
        before_start = [qkv_first, early]
    else:
        before_start = [qkv_grad_ran]
    (tokens_back, tail, late), start_ran = call(
        start_back_kernel,
        [shape(rows, D), shape(3 * LEN, D, dtype=bf16), shape(devices, 2 * SLOTS, D, dtype=bf16)],
        [
            pltpu.VMEM((D, 3 * D), bf16),
            pltpu.VMEM((rows + LEN + 8, D), f32),
            pltpu.VMEM((rows, D), f32),
            pltpu.VMEM((rows, D), f32),
            pltpu.VMEM((2 * SLOTS, D), f32),
            pltpu.VMEM((3 * LEN, D), bf16),
            pltpu.VMEM((devices, 2 * SLOTS, D), bf16),
            dma((5,)),
            dma((SLOTS + 2,)),
        ],
        24,
        [place, grad_qkv, mod, out_tail, residual, grad_middle, qkv_laid],
        [SM] + [VM] * 3 + [HBM] * 3,
        after=before_start,
        out_specs=[HBM] * 3,
    )
    late = lax.all_to_all(late, "wide", 0, 0, tiled=True)

    if cube:
        fc1_own, fc1_beyond, fc1_halved = links.halved_z(*fc1_near_sum, [start_ran])
        qkv_twos, qkv_second = links.second(qkv_keep, qkv_got, qkv_ones, [fc1_halved], True)
        before_ada = [qkv_second]
    else:
        before_ada = [start_ran]

    onward = [(i, i + 1) for i in range(devices - 1)]
    tail = lax.ppermute(tail, "wide", onward)
    wide_images = -(-images // 128) * 128
    (ada_grad, ada_bias_sum, last), ada_ran = call(
        ada_kernel,
        [
            shape(own_dim, 6 * D),
            shape(1, 6 * D),
            shape(devices, own_dim + 8, wide_images, dtype=bf16),
        ],
        [pltpu.VMEM((devices * 16, images), f32), pltpu.VMEM((own_dim + 8, wide_images), f32)],
        24,
        [where, starts, early, late, ada_w, cond, qkv_bias_sum, proj_bias_sum, fc2_bias_sum, fc1_bias_sum],
        [SM] * 2 + [VM] * 8,
        after=before_ada,
        zeros=True,
    )
    last = lax.all_to_all(last, "wide", 0, 0, tiled=True)
    if cube:
        qkv_near_sum, qkv_summed = links.near_sum(
            qkv_keep, qkv_got, qkv_ones, qkv_twos, True, [ada_ran]
        )
        before_place = [qkv_summed]
    else:
        before_place = [ada_ran]
    (out, tokens_grad), placed = call(
        place_kernel,
        [shape(rows, D, dtype=bf16), shape(rows, D)],
        [
            pltpu.VMEM((rows + LEN + 8, D), f32),
            pltpu.VMEM((rows + LEN + 8, D), f32),
            pltpu.VMEM((rows, D), bf16),
            pltpu.VMEM((rows, D), bf16),
            pltpu.VMEM((rows, D), bf16),
            pltpu.VMEM((rows, D), bf16),
            pltpu.VMEM((rows, D), f32),
            dma((6,)),
        ],
        16,
        [place, tail, tokens, cotangent, result, tokens_back],
        [SM, VM] + [HBM] * 4,
        after=before_place,
        out_specs=[HBM] * 2,
    )


    (cond_grad, bias_grads), finished = call(
        finish_kernel,
        [shape(images, D), shape(8, wide_images)],
        [pltpu.VMEM((D, wide_images), f32)],
        16,
        [last],
        [VM],
        after=[placed],
        zeros=True,
    )
    fc1_widths, qkv_widths = [F // 2], [D // 2, 3 * D // 2]
    if cube:
        fc2_grad = tie(fc2_own, finished) + fc2_beyond.astype(f32)
        (fc1_grad,) = links.own_rows(
            tie(fc1_own, ada_ran) + fc1_beyond.astype(f32), fc1_widths
        )
        proj_grad, qkv_grad = links.own_rows(links.z_sum(finished, *qkv_near_sum), qkv_widths)
    else:
        fc2_grad = links.scattered_rows(fc2_send, fc2_keep)
        (fc1_grad,) = links.scattered(fc1_send, fc1_keep, fc1_widths)
        proj_grad, qkv_grad = links.scattered(qkv_send, qkv_keep, qkv_widths)
    bias_grads = bias_grads[:, :own_dim]
    ada_bias_grad = lax.dynamic_slice_in_dim(ada_bias_sum[0], me * span, span, 0)
    return (
        out,
        tokens_grad,
        cond_grad,
        ada_grad,
        ada_bias_grad,
        qkv_grad,
        bias_grads[0],
        bias_grads[1],
        proj_grad,
        bias_grads[2],
        fc1_grad,
        bias_grads[4:].reshape(-1),
        fc2_grad,
        bias_grads[3],
    )


def solution(mesh):
    row, flat = P("wide", None), P("wide")
    return jax.shard_map(
        on_device,
        mesh=mesh,
        in_specs=(row, row, P(), P(), P(), row, flat, row, flat, flat, row, flat, row, flat, row, flat),
        out_specs=(row, row, P(), row, flat, row, flat, flat, row, flat, row, flat, row, flat),
        check_vma=False,
    )
```

profile of v0, /device:TPU:9, one launch (start us, length us, event | category | flops | bytes accessed | tf_op | source)
XLA Modules:
  0.0 278.9 jit_solution(15570962654238239546)
XLA Ops:
  1.5 3.0 %begin_kernel.1 = (bf16[24,3072]{1,0:T(8,128)(2,1)S(1)}, bf16[24,3072]{1,0:T(8,128)(2,1)S(1)}, bf16[256,768]{1,0:T(8,128)(2,1)S(1)}, s32[8]{0:T(128)S(1)}, s32[3...) custom-call(s32[3]{0:T(128)S(1)} %pad_add_fusion.refs_0_, ...), custom_call_target="tpu_custom_call" | custom-call | flops 1 | bytes 1 | tf_op jit(solution)/shard_map/begin_kernel/pallas_call | solution.py:851
  4.5 6.4 %all-to-all-start = ((bf16[32,24,144]{2,1,0:T(8,128)(2,1)}), bf16[32,24,144]{2,1,0:T(8,128)(2,1)S(1)}, u32[]{:S(2)}, u32[]{:S(2)}) async-start(bf16[32,24,144]{2,1,0:T(8,128)(2,1)} %get-tuple-element.137), calls=%async_computation | async-start | bytes 786432 | tf_op jit(solution)/shard_map/all_to_all | solution.py:1098
  11.3 2.0 collective-permute-start.1
  17.4 10.3 %all-to-all-done = bf16[32,24,144]{2,1,0:T(8,128)(2,1)S(1)} async-done(((bf16[32,24,144]{2,1,0:T(8,128)(2,1)}), bf16[32,24,144]{2,1,0:T(8,128)(2,1)S(1)}, u32[]{:S(2)}, u32[]{:S(2)}) %all-to-all-start) | async-done | bytes 221216 | tf_op jit(solution)/shard_map/all_to_all | solution.py:1098
  29.1 3.9 %all-to-all-start.1 = ((f32[32,8,144]{2,1,0:T(8,128)}), f32[32,8,144]{2,1,0:T(8,128)S(1)}, u32[]{:S(2)}, u32[]{:S(2)}) async-start(f32[32,8,144]{2,1,0:T(8,128)} %get-tuple-element.140), calls=%async_computation.1 | async-start | bytes 524288 | tf_op jit(solution)/shard_map/all_to_all | solution.py:1122
  34.0 2.4 collective-permute-start.8
  36.7 5.9 %collective-permute-done.5 = bf16[48,1920]{1,0:T(8,128)(2,1)S(1)} collective-permute-done((bf16[48,1920]{1,0:T(8,128)(2,1)S(1)}, bf16[48,1920]{1,0:T(8,128)(2,1)S(1)}, u32[]{:S(2)}, u32[]{:S(2)}) %collective-permute-start.5) | collective-permute-done | bytes 184352 | tf_op jit(solution)/shard_map/ppermute | solution.py:903
  42.6 2.1 collective-permute-start.9
  44.7 4.4 %prep_kernel.1 = (f32[512,768]{1,0:T(8,128)S(1)}, bf16[512,768]{1,0:T(8,128)(2,1)S(1)}, f32[4,4608]{1,0:T(4,128)S(1)}, f32[1,2304]{1,0:T(1,128)S(1)}, f32[1,768]...) custom-call(s32[8]{0:T(128)S(1)} %get-tuple-element.135.refs_0_.refs_1_, ...), custom_call_target="tpu_custom_call" | custom-call | flops 10000000000 | bytes 1 | tf_op jit(solution)/shard_map/prep_kernel/pallas_call | solution.py:851
  49.1 11.0 %collective-permute-done.9 = bf16[96,1920]{1,0:T(8,128)(2,1)} collective-permute-done((bf16[96,1920]{1,0:T(8,128)(2,1)S(1)}, bf16[96,1920]{1,0:T(8,128)(2,1)}, u32[]{:S(2)}, u32[]{:S(2)}) %collective-permute-start.9) | collective-permute-done | bytes 368672 | tf_op jit(solution)/shard_map/ppermute | solution.py:903
  66.0 3.2 %collective-permute-start.11 = (bf16[96,768]{1,0:T(8,128)(2,1)S(1)}, bf16[96,768]{1,0:T(8,128)(2,1)S(1)}, u32[]{:S(2)}, u32[]{:S(2)}) collective-permute-start(bf16[96,768]{1,0:T(8,128)(2,1)S(1)} %copy-done.13), channel_id=1, source_target_pairs={{0,16},{1,17},{2,18},{3,19},{4,20},{5,21},{6,22},{7,23},{8,24},{9,... | collective-permute-start | bytes 442376 | tf_op jit(solution)/shard_map/ppermute | solution.py:903
  69.3 4.7 %qkv_kernel.1 = (bf16[512,768]{1,0:T(8,128)(2,1)}, bf16[512,2304]{1,0:T(8,128)(2,1)S(1)}, bf16[768,2304]{1,0:T(8,128)(2,1)}, f32[8,128]{1,0:T(8,128)S(1)}) custom-call(s32[3]{0:T(128)S(1)} %pad_add_fusion.refs_0_, f32[512,768]{1,0:T(8,128)S(1)} %get-tuple-element.143.refs_1_.refs_4_, f32[4,4608]{1,0:T(4,128)S(1)} %get-tuple-element.144.refs_2_.refs_3_.refs_4_, ...), custom_call_target="tpu_custom_call" | custom-call | flops 1 | bytes 1 | tf_op jit(solution)/shard_map/qkv_kernel/pallas_call | solution.py:851
  74.9 5.1 %attend_kernel.1 = (bf16[512,768]{1,0:T(8,128)(2,1)S(1)}, bf16[512,768]{1,0:T(8,128)(2,1)}, f32[8,128]{1,0:T(8,128)S(1)}) custom-call(bf16[512,2304]{1,0:T(8,128)(2,1)S(1)} %get-tuple-element.148.refs_0_, f32[8,128]{1,0:T(8,128)} %copy-done.17, bf16[192,768]{1,0:T(8,128)(2,1)S(1)} %get-tuple-element.150.refs_2_), custom_call_target="tpu_custom_call" | custom-call | flops 1 | bytes 1 | tf_op jit(solution)/shard_map/attend_kernel/pallas_call | solution.py:851
  86.6 2.1 collective-permute-start.18
  88.7 6.6 %collective-permute-done.14.refs_0_ = bf16[96,1920]{1,0:T(8,128)(2,1)S(1)} collective-permute-done((bf16[96,1920]{1,0:T(8,128)(2,1)S(1)}, bf16[96,1920]{1,0:T(8,128)(2,1)S(1)}, u32[]{:S(2)}, u32[]{:S(2)}) %collective-permute-start.14) | collective-permute-done | bytes 368672 | tf_op jit(solution)/shard_map/ppermute | solution.py:903
  100.5 15.6 %hidden_kernel.1 = (f32[512,768]{1,0:T(8,128)S(1)}, f32[512,768]{1,0:T(8,128)S(1)}, bf16[512,768]{1,0:T(8,128)(2,1)S(1)}, bf16[512,768]{1,0:T(8,128)(2,1)S(1)}, ...) custom-call(s32[3]{0:T(128)S(1)} %pad_add_fusion.refs_0_, ...), custom_call_target="tpu_custom_call" | custom-call | flops 1 | bytes 1 | tf_op jit(solution)/shard_map/hidden_kernel/pallas_call | solution.py:851
  117.1 3.3 %flips_kernel.1 = (bf16[768,512]{1,0:T(8,128)(2,1)S(1)}, bf16[768,512]{1,0:T(8,128)(2,1)}, bf16[768,512]{1,0:T(8,128)(2,1)}, f32[8,128]{1,0:T(8,128)}) custom-call(s32[3]{0:T(128)S(1)} %pad_add_fusion.refs_0_, bf16[512,768]{1,0:T(8,128)(2,1)S(1)} %get-tuple-element.160.refs_1_, bf16[512,768]{1,0:T(8,128)(2,1)} %get-tuple-element.161.refs_2_, ...), custom_call_target="tpu_custom_call" | custom-call | flops 1 | bytes 1 | tf_op jit(solution)/shard_map/flips_kernel/pallas_call | solution.py:851
  120.4 3.8 %probs_kernel.1 = (f32[3072,256]{1,0:T(8,128)}, f32[8,128]{1,0:T(8,128)}) custom-call(bf16[512,2304]{1,0:T(8,128)(2,1)} %copy-done, f32[8,128]{1,0:T(8,128)} %get-tuple-element.164.refs_1_), custom_call_target="tpu_custom_call" | custom-call | flops 1 | bytes 1 | tf_op jit(solution)/shard_map/probs_kernel/pallas_call | solution.py:851
  129.8 1.4 collective-permute-done.22.refs_4_.refs_8_
  131.2 5.8 %fc2_back_kernel.1 = (bf16[512,3072]{1,0:T(8,128)(2,1)S(1)}, f32[1,3072]{1,0:T(1,128)S(1)}, f32[8,128]{1,0:T(8,128)}) custom-call(s32[3]{0:T(128)S(1)} %pad_add_fusion.refs_0_, bf16[512,768]{1,0:T(8,128)(2,1)S(1)} %get-tuple-element.166.refs_1_, bf16[512,3072]{1,0:T(8,128)(2,1)} %get-tuple-element.167.refs_2_, ...), custom_call_target="tpu_custom_call" | custom-call | flops 1 | bytes 1 | tf_op jit(solution)/shard_map/fc2_back_kernel/pallas_call | solution.py:851
  137.0 4.2 %wgrad_kernel.2 = (bf16[768,1536]{1,0:T(8,128)(2,1)}, bf16[768,1536]{1,0:T(8,128)(2,1)}, f32[8,128]{1,0:T(8,128)}) custom-call(s32[3]{0:T(128)S(1)} %pad_add_fusion.refs_0_, bf16[768,512]{1,0:T(8,128)(2,1)S(1)} %get-tuple-element.180.refs_1_, bf16[512,3072]{1,0:T(8,128)(2,1)S(1)} %get-tuple-element.174.refs_2_.refs_1_), custom_call_target="tpu_custom_call" | custom-call | flops 1 | bytes 1 | tf_op jit(solution)/shard_map/wgrad_kernel/pallas_call | solution.py:851
  141.7 6.7 %fc2_out_kernel.1 = (bf16[128,768]{1,0:T(8,128)(2,1)S(1)}, f32[4,768]{1,0:T(4,128)S(1)}, bf16[512,768]{1,0:T(8,128)(2,1)}, f32[8,128]{1,0:T(8,128)}) custom-call(s32[3]{0:T(128)S(1)} %pad_add_fusion.refs_0_, s32[8]{0:T(128)S(1)} %get-tuple-element.135.refs_0_.refs_1_, f32[4,4608]{1,0:T(4,128)S(1)} %get-tuple-element.144.refs_2_.refs_3_.refs_4_, ...), custom_call_target="tpu_custom_call" | custom-call | flops 1 | bytes 1 | tf_op jit(solution)/shard_map/fc2_out_kernel/pallas_call | solution.py:851
  151.1 2.3 first_kernel.4
  155.1 15.6 %mid_back_kernel.1 = (bf16[512,768]{1,0:T(8,128)(2,1)S(1)}, f32[1,768]{1,0:T(1,128)S(1)}, f32[512,768]{1,0:T(8,128)}, bf16[512,768]{1,0:T(8,128)(2,1)}, bf16[32,16,768]{2,1,0:T(8,128)(2,1)}, /*index=5*/f32[8,128]{1,0:T(8,128)}) custom-call(s32[3]{0:T(128)S(1)} %pad_add_fusion.refs_0_, bf16[512,3072]{1,0:T(8,128)(2,1)S(1)} %get-tuple-element.174.refs_2_.refs_1_, ...), custom_call_target="tpu_custom_call" | custom-call | flops 1 | bytes 1 | tf_op jit(solution)/shard_map/mid_back_kernel/pallas_call | solution.py:851
  170.8 2.0 near_kernel.3
  172.8 2.4 collective-permute-start.31
  175.2 8.1 %attend_back_kernel.1 = (bf16[512,2304]{1,0:T(8,128)(2,1)S(1)}, f32[1,2304]{1,0:T(1,128)S(1)}, f32[8,128]{1,0:T(8,128)}) custom-call(bf16[512,2304]{1,0:T(8,128)(2,1)} %copy-done, f32[3072,256]{1,0:T(8,128)} %get-tuple-element.165.refs_1_, bf16[512,768]{1,0:T(8,128)(2,1)S(1)} %get-tuple-element.190.refs_2_, f32[8,128]{1,0:T(8,128)} %get-tuple-element.194.refs_3_), custom_call_target="tpu_custom_call" | custom-call | flops 1 | bytes 1 | tf_op jit(solution)/shard_map/attend_back_kernel/pallas_call | solution.py:851
  183.3 1.8 beyond_kernel.2
  185.2 2.3 second_kernel.4
  188.9 5.9 %all-to-all-start.2 = ((bf16[32,16,768]{2,1,0:T(8,128)(2,1)}), bf16[32,16,768]{2,1,0:T(8,128)(2,1)S(1)}, u32[]{:S(2)}, u32[]{:S(2)}) async-start(bf16[32,16,768]{2,1,0:T(8,128)(2,1)} %get-tuple-element.217), calls=%async_computation.2 | async-start | bytes 1572864 | tf_op jit(solution)/shard_map/all_to_all | solution.py:1376
  194.8 6.5 %wgrad_kernel.3 = (bf16[768,1536]{1,0:T(8,128)(2,1)}, bf16[768,1536]{1,0:T(8,128)(2,1)}, f32[8,128]{1,0:T(8,128)}) custom-call(s32[3]{0:T(128)S(1)} %copy-done.15, bf16[768,512]{1,0:T(8,128)(2,1)} %get-tuple-element.199.refs_1_, bf16[768,512]{1,0:T(8,128)(2,1)} %get-tuple-element.200.refs_2_, bf16[512,768]{1,0:T(8,128)(2,1)} %get-tuple-element.201.refs_3_, ...), custom_call_target="tpu_custom_call" | custom-call | flops 1 | bytes 1 | tf_op jit(solution)/shard_map/wgrad_kernel/pallas_call | solution.py:851
  201.8 3.6 %near_kernel.4 = (bf16[96,1536]{1,0:T(8,128)(2,1)}, f32[48,1536]{1,0:T(8,128)}, f32[48,1536]{1,0:T(8,128)}, f32[8,128]{1,0:T(8,128)}) custom-call(bf16[768,1536]{1,0:T(8,128)(2,1)} %get-tuple-element.183.refs_0_, bf16[768,1536]{1,0:T(8,128)(2,1)S(1)} %copy-done.6, bf16[192,1536]{1,0:T(8,128)(2,1)S(1)} %copy-done.23, bf16[192,1536]{1,0:T(8,128)(2,1)S(1)} %copy-done.25, ...), custom_call_target="tpu_custom_call" | custom-call | flops 99999997952 | bytes 1 | tf_op jit(solution)/shard_map/near_kernel/pallas_call | solution.py:851
  206.2 3.2 %first_kernel.5 = (bf16[192,1536]{1,0:T(8,128)(2,1)}, bf16[192,1536]{1,0:T(8,128)(2,1)}, f32[8,128]{1,0:T(8,128)}) custom-call(bf16[768,1536]{1,0:T(8,128)(2,1)} %get-tuple-element.210.refs_0_, bf16[768,1536]{1,0:T(8,128)(2,1)S(1)} %collective-permute-done.32.refs_1_, f32[8,128]{1,0:T(8,128)} %get-tuple-element.215.refs_2_), custom_call_target="tpu_custom_call" | custom-call | flops 1 | bytes 1 | tf_op jit(solution)/shard_map/first_kernel/pallas_call | solution.py:851
  212.1 2.1 collective-permute-start.47
  215.8 7.8 %start_back_kernel.1 = (f32[512,768]{1,0:T(8,128)}, bf16[384,768]{1,0:T(8,128)(2,1)}, bf16[32,8,768]{2,1,0:T(8,128)(2,1)}, f32[8,128]{1,0:T(8,128)}) custom-call(s32[8]{0:T(128)S(1)} %copy-done.19, bf16[512,2304]{1,0:T(8,128)(2,1)S(1)} %get-tuple-element.195.refs_4_.refs_1_, f32[4,4608]{1,0:T(4,128)S(1)} %copy-done.8, bf16[128,768]{1,0:T(8,128)(2,1)S(1)} %copy-done.12, ...), custom_call_target="tpu_custom_call" | custom-call | flops 1 | bytes 1 | tf_op jit(solution)/shard_map/start_back_kernel/pallas_call | solution.py:851
  223.6 4.3 %all-to-all-start.3 = ((bf16[32,8,768]{2,1,0:T(8,128)(2,1)}), bf16[32,8,768]{2,1,0:T(8,128)(2,1)S(1)}, u32[]{:S(2)}, u32[]{:S(2)}) async-start(bf16[32,8,768]{2,1,0:T(8,128)(2,1)} %get-tuple-element.231), calls=%async_computation.3 | async-start | bytes 786432 | tf_op jit(solution)/shard_map/all_to_all | solution.py:1435
  227.9 1.8 beyond_kernel.3
  229.7 2.3 collective-permute-start.45
  232.0 3.6 %collective-permute-start.35 = (bf16[384,768]{1,0:T(8,128)(2,1)}, bf16[384,768]{1,0:T(8,128)(2,1)}, u32[]{:S(2)}, u32[]{:S(2)}) collective-permute-start(bf16[384,768]{1,0:T(8,128)(2,1)} %get-tuple-element.218), channel_id=1, source_target_pairs={{0,1},{1,2},{2,3},{3,4},{4,5},{5,6},{6,7},{7,8},{8,9},{9,10},{10,1... | collective-permute-start | bytes 1769480 | tf_op jit(solution)/shard_map/ppermute | solution.py:1445
  235.7 2.7 second_kernel.5
  239.7 3.5 %all-to-all-done.3.refs_3_ = bf16[32,8,768]{2,1,0:T(8,128)(2,1)S(1)} async-done(((bf16[32,8,768]{2,1,0:T(8,128)(2,1)}), bf16[32,8,768]{2,1,0:T(8,128)(2,1)S(1)}, u32[]{:S(2)}, u32[]{:S(2)}) %all-to-all-start.3) | async-done | bytes 393248 | tf_op jit(solution)/shard_map/all_to_all | solution.py:1435
  243.3 4.9 %ada_kernel.1 = (f32[24,4608]{1,0:T(8,128)}, f32[1,4608]{1,0:T(1,128)S(1)}, bf16[32,32,128]{2,1,0:T(8,128)(2,1)}, f32[8,128]{1,0:T(8,128)S(1)}) custom-call(s32[3]{0:T(128)S(1)} %copy-done.16, s32[32]{0:T(128)S(1)} %get-tuple-element.230.refs_1_, bf16[32,16,768]{2,1,0:T(8,128)(2,1)S(1)} %all-to-all-done.2.refs_8_.refs_2_, ...), custom_call_target="tpu_custom_call" | custom-call | flops 1 | bytes 1 | tf_op jit(solution)/shard_map/ada_kernel/pallas_call | solution.py:851
  249.4 3.7 %all-to-all-start.4 = ((bf16[32,32,128]{2,1,0:T(8,128)(2,1)}), bf16[32,32,128]{2,1,0:T(8,128)(2,1)S(1)}, u32[]{:S(2)}, u32[]{:S(2)}) async-start(bf16[32,32,128]{2,1,0:T(8,128)(2,1)} %get-tuple-element.241), calls=%async_computation.4 | async-start | bytes 524288 | tf_op jit(solution)/shard_map/all_to_all | solution.py:1461
  254.2 2.7 near_kernel.5
  257.0 2.4 collective-permute-start.42
  259.6 5.6 %place_kernel.1 = (bf16[512,768]{1,0:T(8,128)(2,1)}, f32[512,768]{1,0:T(8,128)}, f32[8,128]{1,0:T(8,128)}) custom-call(s32[8]{0:T(128)S(1)} %copy-done.19, bf16[384,768]{1,0:T(8,128)(2,1)} %collective-permute-done.35.refs_1_, bf16[512,768]{1,0:T(8,128)(2,1)} %refs_2_.5, bf16[512,768]{1,0:T(8,128)(2,1)} %refs_3_.5, ...), custom_call_target="tpu_custom_call" | custom-call | flops 1 | bytes 1 | tf_op jit(solution)/shard_map/place_kernel/pallas_call | solution.py:851
  268.0 5.5 %collective-permute-done.43 = bf16[48,1536]{1,0:T(8,128)(2,1)S(1)} collective-permute-done((bf16[48,1536]{1,0:T(8,128)(2,1)S(1)}, bf16[48,1536]{1,0:T(8,128)(2,1)S(1)}, u32[]{:S(2)}, u32[]{:S(2)}) %collective-permute-start.43) | collective-permute-done | bytes 147488 | tf_op jit(solution)/shard_map/ppermute | solution.py:903
  275.1 1.7 convert_add_fusion
  (208 shorter events, 52.6 us)
Async XLA Ops:
  4.5 23.2 %all-to-all-start = ((bf16[32,24,144]{2,1,0:T(8,128)(2,1)}), bf16[32,24,144]{2,1,0:T(8,128)(2,1)S(1)}, u32[]{:S(2)}, u32[]{:S(2)}) async-start(bf16[32,24,144]{2,1,0:T(8,128)(2,1)} %get-tuple-element.137), calls=%async_computation | async-start | bytes 786432 | tf_op jit(solution)/shard_map/all_to_all | solution.py:1098
  11.3 33.4 %collective-permute-start.1 = (bf16[256,768]{1,0:T(8,128)(2,1)S(1)}, bf16[256,768]{1,0:T(8,128)(2,1)S(1)}, u32[]{:S(2)}, u32[]{:S(2)}) collective-permute-start(bf16[256,768]{1,0:T(8,128)(2,1)S(1)} %get-tuple-element.141), channel_id=1, source_target_pairs={{1,0},{2,1},{3,2},{4,3},{5,4},{6,5},{7,6},{8,7},{9,8},{10,9},{11,1... | collective-permute-start | bytes 1179656 | tf_op jit(solution)/shard_map/ppermute | solution.py:1096
  14.0 19.9 %collective-permute-start.4 = (bf16[48,1152]{1,0:T(8,128)(2,1)S(1)}, bf16[48,1152]{1,0:T(8,128)(2,1)S(1)}, u32[]{:S(2)}, u32[]{:S(2)}) collective-permute-start(bf16[48,1152]{1,0:T(8,128)(2,1)S(1)} %slice.84), channel_id=1, source_target_pairs={{0,24},{1,25},{2,26},{3,27},{4,28},{5,29},{6,30},{7,31},{8,16},{9,... | collective-permute-start | bytes 331784 | tf_op jit(solution)/shard_map/ppermute | solution.py:903
  15.2 18.6 %collective-permute-start.3 = (bf16[48,1152]{1,0:T(8,128)(2,1)S(1)}, bf16[48,1152]{1,0:T(8,128)(2,1)S(1)}, u32[]{:S(2)}, u32[]{:S(2)}) collective-permute-start(bf16[48,1152]{1,0:T(8,128)(2,1)S(1)} %slice.84), channel_id=1, source_target_pairs={{0,16},{1,17},{2,18},{3,19},{4,20},{5,21},{6,22},{7,23},{8,24},{9,... | collective-permute-start | bytes 331784 | tf_op jit(solution)/shard_map/ppermute | solution.py:903
  16.3 17.6 %collective-permute-start.2 = (bf16[48,1152]{1,0:T(8,128)(2,1)S(1)}, bf16[48,1152]{1,0:T(8,128)(2,1)S(1)}, u32[]{:S(2)}, u32[]{:S(2)}) collective-permute-start(bf16[48,1152]{1,0:T(8,128)(2,1)S(1)} %slice.84), channel_id=1, source_target_pairs={{0,8},{1,9},{2,10},{3,11},{4,12},{5,13},{6,14},{7,15},{8,0},{9,1},... | collective-permute-start | bytes 331784 | tf_op jit(solution)/shard_map/ppermute | solution.py:903
  29.1 15.6 %all-to-all-start.1 = ((f32[32,8,144]{2,1,0:T(8,128)}), f32[32,8,144]{2,1,0:T(8,128)S(1)}, u32[]{:S(2)}, u32[]{:S(2)}) async-start(f32[32,8,144]{2,1,0:T(8,128)} %get-tuple-element.140), calls=%async_computation.1 | async-start | bytes 524288 | tf_op jit(solution)/shard_map/all_to_all | solution.py:1122
  33.7 8.9 %collective-permute-start.5 = (bf16[48,1920]{1,0:T(8,128)(2,1)S(1)}, bf16[48,1920]{1,0:T(8,128)(2,1)S(1)}, u32[]{:S(2)}, u32[]{:S(2)}) collective-permute-start(bf16[48,1920]{1,0:T(8,128)(2,1)S(1)} %slice_select_fusion), channel_id=1, source_target_pairs={{0,8},{1,9},{2,10},{3,11},{4,12},{5,13},{6,14},{7,15},{8,0},{9,1},... | collective-permute-start | bytes 552968 | tf_op jit(solution)/shard_map/ppermute | solution.py:903
  34.0 27.2 %collective-permute-start.8 = (bf16[192,1152]{1,0:T(8,128)(2,1)S(1)}, bf16[192,1152]{1,0:T(8,128)(2,1)S(1)}, u32[]{:S(2)}, u32[]{:S(2)}) collective-permute-start(bf16[192,1152]{1,0:T(8,128)(2,1)S(1)} %maximum_select_fusion.refs_7_.refs_0_), channel_id=1, source_target_pairs={{0,6},{1,7},{2,4},{3,5},{4,2},{5,3},{6,0},{7,1},{8,14},{9,15},{10,... | collective-permute-start | bytes 1327112 | tf_op jit(solution)/shard_map/ppermute | solution.py:903
  36.3 24.9 %collective-permute-start.7 = (bf16[192,1152]{1,0:T(8,128)(2,1)S(1)}, bf16[192,1152]{1,0:T(8,128)(2,1)S(1)}, u32[]{:S(2)}, u32[]{:S(2)}) collective-permute-start(bf16[192,1152]{1,0:T(8,128)(2,1)S(1)} %maximum_select_fusion.refs_7_.refs_0_), channel_id=1, source_target_pairs={{0,4},{1,5},{2,6},{3,7},{4,0},{5,1},{6,2},{7,3},{8,12},{9,13},{10,... | collective-permute-start | bytes 1327112 | tf_op jit(solution)/shard_map/ppermute | solution.py:903
  36.6 24.6 %collective-permute-start.6 = (bf16[192,1152]{1,0:T(8,128)(2,1)S(1)}, bf16[192,1152]{1,0:T(8,128)(2,1)S(1)}, u32[]{:S(2)}, u32[]{:S(2)}) collective-permute-start(bf16[192,1152]{1,0:T(8,128)(2,1)S(1)} %maximum_select_fusion.refs_7_.refs_0_), channel_id=1, source_target_pairs={{0,2},{1,3},{2,0},{3,1},{4,6},{5,7},{6,4},{7,5},{8,10},{9,11},{10,... | collective-permute-start | bytes 1327112 | tf_op jit(solution)/shard_map/ppermute | solution.py:903
  42.6 17.5 %collective-permute-start.9 = (bf16[96,1920]{1,0:T(8,128)(2,1)S(1)}, bf16[96,1920]{1,0:T(8,128)(2,1)}, u32[]{:S(2)}, u32[]{:S(2)}) collective-permute-start(bf16[96,1920]{1,0:T(8,128)(2,1)S(1)} %pad_maximum_fusion.1.refs_8_), channel_id=1, source_target_pairs={{0,16},{1,17},{2,18},{3,19},{4,20},{5,21},{6,22},{7,23},{8,24},{9,... | collective-permute-start | bytes 1105928 | tf_op jit(solution)/shard_map/ppermute | solution.py:903
  62.3 7.0 %collective-permute-start.10 = (bf16[768,1152]{1,0:T(8,128)(2,1)S(1)}, bf16[768,1152]{1,0:T(8,128)(2,1)S(1)}, u32[]{:S(2)}, u32[]{:S(2)}) collective-permute-start(bf16[768,1152]{1,0:T(8,128)(2,1)S(1)} %get-tuple-element.147.refs_4_), channel_id=1, source_target_pairs={{0,1},{1,0},{2,3},{3,2},{4,5},{5,4},{6,7},{7,6},{8,9},{9,8},{10,11... | collective-permute-start | bytes 5308424 | tf_op jit(solution)/shard_map/ppermute | solution.py:903
  63.6 18.1 %collective-permute-start.13 = (bf16[192,1920]{1,0:T(8,128)(2,1)S(1)}, bf16[192,1920]{1,0:T(8,128)(2,1)S(1)}, u32[]{:S(2)}, u32[]{:S(2)}) collective-permute-start(bf16[192,1920]{1,0:T(8,128)(2,1)S(1)} %pad_maximum_fusion.refs_5_.refs_0_), channel_id=1, source_target_pairs={{0,4},{1,5},{2,6},{3,7},{4,0},{5,1},{6,2},{7,3},{8,12},{9,13},{10,... | collective-permute-start | bytes 2211848 | tf_op jit(solution)/shard_map/ppermute | solution.py:903
  64.9 17.7 %collective-permute-start.12 = (bf16[192,1920]{1,0:T(8,128)(2,1)S(1)}, bf16[192,1920]{1,0:T(8,128)(2,1)S(1)}, u32[]{:S(2)}, u32[]{:S(2)}) collective-permute-start(bf16[192,1920]{1,0:T(8,128)(2,1)S(1)} %pad_maximum_fusion.refs_5_.refs_0_), channel_id=1, source_target_pairs={{0,2},{1,3},{2,0},{3,1},{4,6},{5,7},{6,4},{7,5},{8,10},{9,11},{10,... | collective-permute-start | bytes 2211848 | tf_op jit(solution)/shard_map/ppermute | solution.py:903
  66.0 8.5 %collective-permute-start.11 = (bf16[96,768]{1,0:T(8,128)(2,1)S(1)}, bf16[96,768]{1,0:T(8,128)(2,1)S(1)}, u32[]{:S(2)}, u32[]{:S(2)}) collective-permute-start(bf16[96,768]{1,0:T(8,128)(2,1)S(1)} %copy-done.13), channel_id=1, source_target_pairs={{0,16},{1,17},{2,18},{3,19},{4,20},{5,21},{6,22},{7,23},{8,24},{9,... | collective-permute-start | bytes 442376 | tf_op jit(solution)/shard_map/ppermute | solution.py:903
  83.9 16.6 %collective-permute-start.16 = (bf16[576,1920]{1,0:T(8,128)(2,1)S(1)}, bf16[576,1920]{1,0:T(8,128)(2,1)S(1)}, u32[]{:S(2)}, u32[]{:S(2)}) collective-permute-start(bf16[576,1920]{1,0:T(8,128)(2,1)S(1)} %get-tuple-element.156.refs_7_), channel_id=1, source_target_pairs={{0,1},{1,0},{2,3},{3,2},{4,5},{5,4},{6,7},{7,6},{8,9},{9,8},{10,11... | collective-permute-start | bytes 6635528 | tf_op jit(solution)/shard_map/ppermute | solution.py:903
  85.1 10.2 %collective-permute-start.14 = (bf16[96,1920]{1,0:T(8,128)(2,1)S(1)}, bf16[96,1920]{1,0:T(8,128)(2,1)S(1)}, u32[]{:S(2)}, u32[]{:S(2)}) collective-permute-start(bf16[96,1920]{1,0:T(8,128)(2,1)S(1)} %get-tuple-element.157), channel_id=1, source_target_pairs={{0,2},{1,3},{2,0},{3,1},{4,6},{5,7},{6,4},{7,5},{8,10},{9,11},{10,... | collective-permute-start | bytes 1105928 | tf_op jit(solution)/shard_map/ppermute | solution.py:903
  86.3 9.8 %collective-permute-start.15 = (bf16[96,1920]{1,0:T(8,128)(2,1)S(1)}, bf16[96,1920]{1,0:T(8,128)(2,1)S(1)}, u32[]{:S(2)}, u32[]{:S(2)}) collective-permute-start(bf16[96,1920]{1,0:T(8,128)(2,1)S(1)} %get-tuple-element.158), channel_id=1, source_target_pairs={{0,4},{1,5},{2,6},{3,7},{4,0},{5,1},{6,2},{7,3},{8,12},{9,13},{10,... | collective-permute-start | bytes 1105928 | tf_op jit(solution)/shard_map/ppermute | solution.py:903
  86.6 11.2 %collective-permute-start.18 = (bf16[192,768]{1,0:T(8,128)(2,1)S(1)}, bf16[192,768]{1,0:T(8,128)(2,1)S(1)}, u32[]{:S(2)}, u32[]{:S(2)}) collective-permute-start(bf16[192,768]{1,0:T(8,128)(2,1)S(1)} %get-tuple-element.150.refs_2_), channel_id=1, source_target_pairs={{0,8},{1,9},{2,10},{3,11},{4,12},{5,13},{6,14},{7,15},{8,0},{9,1},... | collective-permute-start | bytes 884744 | tf_op jit(solution)/shard_map/ppermute | solution.py:903
  97.8 26.5 %collective-permute-start.21 = (bf16[384,768]{1,0:T(8,128)(2,1)S(1)}, bf16[384,768]{1,0:T(8,128)(2,1)S(1)}, u32[]{:S(2)}, u32[]{:S(2)}) collective-permute-start(bf16[384,768]{1,0:T(8,128)(2,1)S(1)} %constant_dynamic-update-slice_fusion.refs_0_), channel_id=1, source_target_pairs={{0,6},{1,7},{2,4},{3,5},{4,2},{5,3},{6,0},{7,1},{8,14},{9,15},{10,... | collective-permute-start | bytes 1769480 | tf_op jit(solution)/shard_map/ppermute | solution.py:903
  98.1 27.3 %collective-permute-start.20 = (bf16[384,768]{1,0:T(8,128)(2,1)S(1)}, bf16[384,768]{1,0:T(8,128)(2,1)S(1)}, u32[]{:S(2)}, u32[]{:S(2)}) collective-permute-start(bf16[384,768]{1,0:T(8,128)(2,1)S(1)} %constant_dynamic-update-slice_fusion.refs_0_), channel_id=1, source_target_pairs={{0,4},{1,5},{2,6},{3,7},{4,0},{5,1},{6,2},{7,3},{8,12},{9,13},{10,... | collective-permute-start | bytes 1769480 | tf_op jit(solution)/shard_map/ppermute | solution.py:903
  99.3 26.1 %collective-permute-start.19 = (bf16[384,768]{1,0:T(8,128)(2,1)S(1)}, bf16[384,768]{1,0:T(8,128)(2,1)S(1)}, u32[]{:S(2)}, u32[]{:S(2)}) collective-permute-start(bf16[384,768]{1,0:T(8,128)(2,1)S(1)} %constant_dynamic-update-slice_fusion.refs_0_), channel_id=1, source_target_pairs={{0,2},{1,3},{2,0},{3,1},{4,6},{5,7},{6,4},{7,5},{8,10},{9,11},{10,... | collective-permute-start | bytes 1769480 | tf_op jit(solution)/shard_map/ppermute | solution.py:903
  116.2 10.9 %collective-permute-start.23 = (bf16[1536,768]{1,0:T(8,128)(2,1)}, bf16[1536,768]{1,0:T(8,128)(2,1)S(1)}, u32[]{:S(2)}, u32[]{:S(2)}) collective-permute-start(bf16[1536,768]{1,0:T(8,128)(2,1)} %get-tuple-element.171), channel_id=1, source_target_pairs={{0,1},{1,0},{2,3},{3,2},{4,5},{5,4},{6,7},{7,6},{8,9},{9,8},{10,11... | collective-permute-start | bytes 7077896 | tf_op jit(solution)/shard_map/ppermute | solution.py:903
  128.4 20.0 %collective-permute-start.25 = (bf16[384,768]{1,0:T(8,128)(2,1)S(1)}, bf16[384,768]{1,0:T(8,128)(2,1)S(1)}, u32[]{:S(2)}, u32[]{:S(2)}) collective-permute-start(bf16[384,768]{1,0:T(8,128)(2,1)S(1)} %get-tuple-element.185), channel_id=1, source_target_pairs={{0,2},{1,3},{2,0},{3,1},{4,6},{5,7},{6,4},{7,5},{8,10},{9,11},{10,... | collective-permute-start | bytes 1769480 | tf_op jit(solution)/shard_map/ppermute | solution.py:903
  129.5 19.0 %collective-permute-start.26 = (bf16[384,768]{1,0:T(8,128)(2,1)S(1)}, bf16[384,768]{1,0:T(8,128)(2,1)S(1)}, u32[]{:S(2)}, u32[]{:S(2)}) collective-permute-start(bf16[384,768]{1,0:T(8,128)(2,1)S(1)} %get-tuple-element.186), channel_id=1, source_target_pairs={{0,4},{1,5},{2,6},{3,7},{4,0},{5,1},{6,2},{7,3},{8,12},{9,13},{10,... | collective-permute-start | bytes 1769480 | tf_op jit(solution)/shard_map/ppermute | solution.py:903
  141.3 9.8 %collective-permute-start.24 = (bf16[768,1536]{1,0:T(8,128)(2,1)}, bf16[768,1536]{1,0:T(8,128)(2,1)S(1)}, u32[]{:S(2)}, u32[]{:S(2)}) collective-permute-start(bf16[768,1536]{1,0:T(8,128)(2,1)} %get-tuple-element.184), channel_id=1, source_target_pairs={{0,1},{1,0},{2,3},{3,2},{4,5},{5,4},{6,7},{7,6},{8,9},{9,8},{10,11... | collective-permute-start | bytes 7077896 | tf_op jit(solution)/shard_map/ppermute | solution.py:903
  149.8 21.0 %collective-permute-start.27 = (bf16[192,768]{1,0:T(8,128)(2,1)S(1)}, bf16[192,768]{1,0:T(8,128)(2,1)S(1)}, u32[]{:S(2)}, u32[]{:S(2)}) collective-permute-start(bf16[192,768]{1,0:T(8,128)(2,1)S(1)} %get-tuple-element.191), channel_id=1, source_target_pairs={{0,2},{1,3},{2,0},{3,1},{4,6},{5,7},{6,4},{7,5},{8,10},{9,11},{10,... | collective-permute-start | bytes 884744 | tf_op jit(solution)/shard_map/ppermute | solution.py:903
  150.8 20.0 %collective-permute-start.28 = (bf16[192,768]{1,0:T(8,128)(2,1)S(1)}, bf16[192,768]{1,0:T(8,128)(2,1)S(1)}, u32[]{:S(2)}, u32[]{:S(2)}) collective-permute-start(bf16[192,768]{1,0:T(8,128)(2,1)S(1)} %get-tuple-element.192), channel_id=1, source_target_pairs={{0,4},{1,5},{2,6},{3,7},{4,0},{5,1},{6,2},{7,3},{8,12},{9,13},{10,... | collective-permute-start | bytes 884744 | tf_op jit(solution)/shard_map/ppermute | solution.py:903
  153.4 31.8 %collective-permute-start.29 = (bf16[192,1536]{1,0:T(8,128)(2,1)S(1)}, bf16[192,1536]{1,0:T(8,128)(2,1)S(1)}, u32[]{:S(2)}, u32[]{:S(2)}) collective-permute-start(bf16[192,1536]{1,0:T(8,128)(2,1)S(1)} %get-tuple-element.202), channel_id=1, source_target_pairs={{0,2},{1,3},{2,0},{3,1},{4,6},{5,7},{6,4},{7,5},{8,10},{9,11},{10,... | collective-permute-start | bytes 1769480 | tf_op jit(solution)/shard_map/ppermute | solution.py:903
  154.6 30.5 %collective-permute-start.30 = (bf16[192,1536]{1,0:T(8,128)(2,1)S(1)}, bf16[192,1536]{1,0:T(8,128)(2,1)S(1)}, u32[]{:S(2)}, u32[]{:S(2)}) collective-permute-start(bf16[192,1536]{1,0:T(8,128)(2,1)S(1)} %get-tuple-element.203), channel_id=1, source_target_pairs={{0,4},{1,5},{2,6},{3,7},{4,0},{5,1},{6,2},{7,3},{8,12},{9,13},{10,... | collective-permute-start | bytes 1769480 | tf_op jit(solution)/shard_map/ppermute | solution.py:903
  172.8 10.6 %collective-permute-start.31 = (bf16[192,768]{1,0:T(8,128)(2,1)S(1)}, bf16[192,768]{1,0:T(8,128)(2,1)S(1)}, u32[]{:S(2)}, u32[]{:S(2)}) collective-permute-start(bf16[192,768]{1,0:T(8,128)(2,1)S(1)} %get-tuple-element.204), channel_id=1, source_target_pairs={{0,8},{1,9},{2,10},{3,11},{4,12},{5,13},{6,14},{7,15},{8,0},{9,1},... | collective-permute-start | bytes 884744 | tf_op jit(solution)/shard_map/ppermute | solution.py:903
  187.6 14.1 %collective-permute-start.33 = (bf16[96,1536]{1,0:T(8,128)(2,1)}, bf16[96,1536]{1,0:T(8,128)(2,1)S(1)}, u32[]{:S(2)}, u32[]{:S(2)}) collective-permute-start(bf16[96,1536]{1,0:T(8,128)(2,1)} %get-tuple-element.212), channel_id=1, source_target_pairs={{0,2},{1,3},{2,0},{3,1},{4,6},{5,7},{6,4},{7,5},{8,10},{9,11},{10,... | collective-permute-start | bytes 884744 | tf_op jit(solution)/shard_map/ppermute | solution.py:903
  188.3 13.4 %collective-permute-start.34 = (bf16[96,1536]{1,0:T(8,128)(2,1)}, bf16[96,1536]{1,0:T(8,128)(2,1)}, u32[]{:S(2)}, u32[]{:S(2)}) collective-permute-start(bf16[96,1536]{1,0:T(8,128)(2,1)} %get-tuple-element.213), channel_id=1, source_target_pairs={{0,4},{1,5},{2,6},{3,7},{4,0},{5,1},{6,2},{7,3},{8,12},{9,13},{10,... | collective-permute-start | bytes 884744 | tf_op jit(solution)/shard_map/ppermute | solution.py:903
  188.9 26.0 %all-to-all-start.2 = ((bf16[32,16,768]{2,1,0:T(8,128)(2,1)}), bf16[32,16,768]{2,1,0:T(8,128)(2,1)S(1)}, u32[]{:S(2)}, u32[]{:S(2)}) async-start(bf16[32,16,768]{2,1,0:T(8,128)(2,1)} %get-tuple-element.217), calls=%async_computation.2 | async-start | bytes 1572864 | tf_op jit(solution)/shard_map/all_to_all | solution.py:1376
  209.4 26.2 %collective-permute-start.36 = (bf16[192,1536]{1,0:T(8,128)(2,1)}, bf16[192,1536]{1,0:T(8,128)(2,1)}, u32[]{:S(2)}, u32[]{:S(2)}) collective-permute-start(bf16[192,1536]{1,0:T(8,128)(2,1)} %get-tuple-element.221), channel_id=1, source_target_pairs={{0,2},{1,3},{2,0},{3,1},{4,6},{5,7},{6,4},{7,5},{8,10},{9,11},{10,... | collective-permute-start | bytes 1769480 | tf_op jit(solution)/shard_map/ppermute | solution.py:903
  210.6 25.0 %collective-permute-start.37 = (bf16[192,1536]{1,0:T(8,128)(2,1)}, bf16[192,1536]{1,0:T(8,128)(2,1)}, u32[]{:S(2)}, u32[]{:S(2)}) collective-permute-start(bf16[192,1536]{1,0:T(8,128)(2,1)} %get-tuple-element.222), channel_id=1, source_target_pairs={{0,4},{1,5},{2,6},{3,7},{4,0},{5,1},{6,2},{7,3},{8,12},{9,13},{10,... | collective-permute-start | bytes 1769480 | tf_op jit(solution)/shard_map/ppermute | solution.py:903
  211.8 16.0 %collective-permute-start.38 = (bf16[96,1536]{1,0:T(8,128)(2,1)}, bf16[96,1536]{1,0:T(8,128)(2,1)S(1)}, u32[]{:S(2)}, u32[]{:S(2)}) collective-permute-start(bf16[96,1536]{1,0:T(8,128)(2,1)} %get-tuple-element.223), channel_id=1, source_target_pairs={{0,8},{1,9},{2,10},{3,11},{4,12},{5,13},{6,14},{7,15},{8,0},{9,1},... | collective-permute-start | bytes 884744 | tf_op jit(solution)/shard_map/ppermute | solution.py:903
  212.1 63.0 %collective-permute-start.47 = (bf16[96,768]{1,0:T(8,128)(2,1)}, bf16[96,768]{1,0:T(8,128)(2,1)}, u32[]{:S(2)}, u32[]{:S(2)}) collective-permute-start(bf16[96,768]{1,0:T(8,128)(2,1)} %copy-done.26), channel_id=1, source_target_pairs={{0,16},{1,17},{2,18},{3,19},{4,20},{5,21},{6,22},{7,23},{8,24},{9,... | collective-permute-start | bytes 442376 | tf_op jit(solution)/shard_map/ppermute | solution.py:903
  223.6 19.7 %all-to-all-start.3 = ((bf16[32,8,768]{2,1,0:T(8,128)(2,1)}), bf16[32,8,768]{2,1,0:T(8,128)(2,1)S(1)}, u32[]{:S(2)}, u32[]{:S(2)}) async-start(bf16[32,8,768]{2,1,0:T(8,128)(2,1)} %get-tuple-element.231), calls=%async_computation.3 | async-start | bytes 786432 | tf_op jit(solution)/shard_map/all_to_all | solution.py:1435
  229.7 19.7 %collective-permute-start.45 = (bf16[48,1536]{1,0:T(8,128)(2,1)S(1)}, bf16[48,1536]{1,0:T(8,128)(2,1)S(1)}, u32[]{:S(2)}, u32[]{:S(2)}) collective-permute-start(bf16[48,1536]{1,0:T(8,128)(2,1)S(1)} %get-tuple-element.253), channel_id=1, source_target_pairs={{0,16},{1,17},{2,18},{3,19},{4,20},{5,21},{6,22},{7,23},{8,24},{9,... | collective-permute-start | bytes 442376 | tf_op jit(solution)/shard_map/ppermute | solution.py:903
  232.0 27.4 %collective-permute-start.35 = (bf16[384,768]{1,0:T(8,128)(2,1)}, bf16[384,768]{1,0:T(8,128)(2,1)}, u32[]{:S(2)}, u32[]{:S(2)}) collective-permute-start(bf16[384,768]{1,0:T(8,128)(2,1)} %get-tuple-element.218), channel_id=1, source_target_pairs={{0,1},{1,2},{2,3},{3,4},{4,5},{5,6},{6,7},{7,8},{8,9},{9,10},{10,1... | collective-permute-start | bytes 1769480 | tf_op jit(solution)/shard_map/ppermute | solution.py:1445
  238.4 15.8 %collective-permute-start.39 = (bf16[96,1536]{1,0:T(8,128)(2,1)S(1)}, bf16[96,1536]{1,0:T(8,128)(2,1)S(1)}, u32[]{:S(2)}, u32[]{:S(2)}) collective-permute-start(bf16[96,1536]{1,0:T(8,128)(2,1)S(1)} %get-tuple-element.228), channel_id=1, source_target_pairs={{0,2},{1,3},{2,0},{3,1},{4,6},{5,7},{6,4},{7,5},{8,10},{9,11},{10,... | collective-permute-start | bytes 884744 | tf_op jit(solution)/shard_map/ppermute | solution.py:903
  239.6 14.6 %collective-permute-start.40 = (bf16[96,1536]{1,0:T(8,128)(2,1)S(1)}, bf16[96,1536]{1,0:T(8,128)(2,1)S(1)}, u32[]{:S(2)}, u32[]{:S(2)}) collective-permute-start(bf16[96,1536]{1,0:T(8,128)(2,1)S(1)} %get-tuple-element.229), channel_id=1, source_target_pairs={{0,4},{1,5},{2,6},{3,7},{4,0},{5,1},{6,2},{7,3},{8,12},{9,13},{10,... | collective-permute-start | bytes 884744 | tf_op jit(solution)/shard_map/ppermute | solution.py:903
  249.4 16.6 %all-to-all-start.4 = ((bf16[32,32,128]{2,1,0:T(8,128)(2,1)}), bf16[32,32,128]{2,1,0:T(8,128)(2,1)S(1)}, u32[]{:S(2)}, u32[]{:S(2)}) async-start(bf16[32,32,128]{2,1,0:T(8,128)(2,1)} %get-tuple-element.241), calls=%async_computation.4 | async-start | bytes 524288 | tf_op jit(solution)/shard_map/all_to_all | solution.py:1461
  253.1 12.1 %collective-permute-start.46 = (f32[24,1536]{1,0:T(8,128)S(1)}, f32[24,1536]{1,0:T(8,128)S(1)}, u32[]{:S(2)}, u32[]{:S(2)}) collective-permute-start(f32[24,1536]{1,0:T(8,128)S(1)} %get-tuple-element.257), channel_id=1, source_target_pairs={{0,1},{1,0},{2,3},{3,2},{4,5},{5,4},{6,7},{7,6},{8,9},{9,8},{10,11... | collective-permute-start | bytes 442376 | tf_op jit(solution)/shard_map/ppermute | solution.py:903
  256.9 11.1 %collective-permute-start.41 = (bf16[48,1536]{1,0:T(8,128)(2,1)S(1)}, bf16[48,1536]{1,0:T(8,128)(2,1)S(1)}, u32[]{:S(2)}, u32[]{:S(2)}) collective-permute-start(bf16[48,1536]{1,0:T(8,128)(2,1)S(1)} %get-tuple-element.248), channel_id=1, source_target_pairs={{0,8},{1,9},{2,10},{3,11},{4,12},{5,13},{6,14},{7,15},{8,0},{9,1},... | collective-permute-start | bytes 442376 | tf_op jit(solution)/shard_map/ppermute | solution.py:903
  257.0 11.1 %collective-permute-start.42 = (bf16[48,1536]{1,0:T(8,128)(2,1)S(1)}, bf16[48,1536]{1,0:T(8,128)(2,1)S(1)}, u32[]{:S(2)}, u32[]{:S(2)}) collective-permute-start(bf16[48,1536]{1,0:T(8,128)(2,1)S(1)} %get-tuple-element.249), channel_id=1, source_target_pairs={{0,16},{1,17},{2,18},{3,19},{4,20},{5,21},{6,22},{7,23},{8,24},{9,... | collective-permute-start | bytes 442376 | tf_op jit(solution)/shard_map/ppermute | solution.py:903
  259.3 14.2 %collective-permute-start.43 = (bf16[48,1536]{1,0:T(8,128)(2,1)S(1)}, bf16[48,1536]{1,0:T(8,128)(2,1)S(1)}, u32[]{:S(2)}, u32[]{:S(2)}) collective-permute-start(bf16[48,1536]{1,0:T(8,128)(2,1)S(1)} %get-tuple-element.250), channel_id=1, source_target_pairs={{0,24},{1,25},{2,26},{3,27},{4,28},{5,29},{6,30},{7,31},{8,16},{9,... | collective-permute-start | bytes 442376 | tf_op jit(solution)/shard_map/ppermute | solution.py:903
  (43 other events, 757.6 us)
where the time goes:
time: 283 us; the launch traced here: 279 us
  Pallas kernels  136 us (48%)
  starting transfers between devices  77.6 us (27%)
  waiting for transfers between devices  49.8 us (18%)
  local copies, waits for them, and re-layouts  6.39 us (2%)
  other arithmetic  5.57 us (2%)
  between operations  3.87 us (1%)
    pallas_call x34, Pallas kernels, call(): pl.pallas_call(body, out_shape=out_shape, in_specs=list(spaces) + [ANY] *...  136 us
    ppermute x46, starting transfers between devices, swap(): lax.ppermute(array, 'wide', [(i, i ^ bits) for i in range(self.devices)])  47.8 us
    ppermute x46, waiting for transfers between devices, swap(): lax.ppermute(array, 'wide', [(i, i ^ bits) for i in range(self.devices)])  35.3 us
    all_to_all x1, waiting for transfers between devices, on_device(): ada_cols = lax.all_to_all(ada_parts, 'wide', 0, 0, tiled=True)  10.3 us
    all_to_all x1, starting transfers between devices, on_device(): ada_cols = lax.all_to_all(ada_parts, 'wide', 0, 0, tiled=True)  6.36 us
    all_to_all x1, starting transfers between devices, on_device(): early = lax.all_to_all(early, 'wide', 0, 0, tiled=True)  5.91 us
  transfers between devices with their start and end apart: 53, of which 14 were waited for; matrix products, arithmetic and copies ran while one was open for 3% of the time, Pallas kernels for 46%

commit v1 on v0

--- a/solution.py
+++ b/solution.py
@@ -1435,9 +1435,9 @@
     late = lax.all_to_all(late, "wide", 0, 0, tiled=True)
 
     if cube:
-        fc1_own, fc1_beyond, fc1_halved = links.halved_z(*fc1_near_sum, [start_ran])
-        qkv_twos, qkv_second = links.second(qkv_keep, qkv_got, qkv_ones, [fc1_halved], True)
-        before_ada = [qkv_second]
+        qkv_twos, qkv_second = links.second(qkv_keep, qkv_got, qkv_ones, [start_ran], True)
+        fc1_own, fc1_beyond, fc1_halved = links.halved_z(*fc1_near_sum, [qkv_second])
+        before_ada = [fc1_halved]
     else:
         before_ada = [start_ran]
 
@@ -1499,7 +1499,7 @@
     )
     fc1_widths, qkv_widths = [F // 2], [D // 2, 3 * D // 2]
     if cube:
-        fc2_grad = tie(fc2_own, finished) + fc2_beyond.astype(f32)
+        fc2_grad = tie(fc2_own, ada_ran) + fc2_beyond.astype(f32)
         (fc1_grad,) = links.own_rows(
             tie(fc1_own, ada_ran) + fc1_beyond.astype(f32), fc1_widths
         )

time: 283 us -> 288 us (1.018)
  waiting for transfers between devices: 49.8 us -> 52.9 us
  transfers between devices with their start and end apart: 53 -> 53, of which waited for: 14 -> 15; matrix products, arithmetic and copies ran while one was open for 3% -> 3% of each run, Pallas kernels for 46% -> 45%
where the time goes in v1:
time: 288 us; the launch traced here: 284 us
  Pallas kernels  136 us (47%)
  starting transfers between devices  77.7 us (27%)
  waiting for transfers between devices  52.9 us (18%)
  other arithmetic  6.76 us (2%)
  local copies, waits for them, and re-layouts  6.37 us (2%)
  between operations  3.83 us (1%)
    pallas_call x34, Pallas kernels, call(): pl.pallas_call(body, out_shape=out_shape, in_specs=list(spaces) + [ANY] *...  136 us
    ppermute x46, starting transfers between devices, swap(): lax.ppermute(array, 'wide', [(i, i ^ bits) for i in range(self.devices)])  47.4 us
    ppermute x46, waiting for transfers between devices, swap(): lax.ppermute(array, 'wide', [(i, i ^ bits) for i in range(self.devices)])  35.4 us
    all_to_all x1, waiting for transfers between devices, on_device(): ada_cols = lax.all_to_all(ada_parts, 'wide', 0, 0, tiled=True)  10.3 us
    all_to_all x1, starting transfers between devices, on_device(): ada_cols = lax.all_to_all(ada_parts, 'wide', 0, 0, tiled=True)  6.36 us
    all_to_all x1, starting transfers between devices, on_device(): early = lax.all_to_all(early, 'wide', 0, 0, tiled=True)  5.9 us
  transfers between devices with their start and end apart: 53, of which 15 were waited for; matrix products, arithmetic and copies ran while one was open for 3% of the time, Pallas kernels for 45%

profile of v1, /device:TPU:9, one launch (start us, length us, event | category | flops | bytes accessed | tf_op | source)
XLA Modules:
  0.0 284.0 jit_solution(14965114534784059585)
XLA Ops:
  1.5 3.0 %begin_kernel.1 = (bf16[24,3072]{1,0:T(8,128)(2,1)S(1)}, bf16[24,3072]{1,0:T(8,128)(2,1)S(1)}, bf16[256,768]{1,0:T(8,128)(2,1)S(1)}, s32[8]{0:T(128)S(1)}, s32[3...) custom-call(s32[3]{0:T(128)S(1)} %pad_add_fusion.refs_0_, ...), custom_call_target="tpu_custom_call" | custom-call | flops 1 | bytes 1 | tf_op jit(solution)/shard_map/begin_kernel/pallas_call | solution.py:851
  4.5 6.4 %all-to-all-start = ((bf16[32,24,144]{2,1,0:T(8,128)(2,1)}), bf16[32,24,144]{2,1,0:T(8,128)(2,1)S(1)}, u32[]{:S(2)}, u32[]{:S(2)}) async-start(bf16[32,24,144]{2,1,0:T(8,128)(2,1)} %get-tuple-element.137), calls=%async_computation | async-start | bytes 786432 | tf_op jit(solution)/shard_map/all_to_all | solution.py:1098
  11.3 2.0 collective-permute-start.1
  17.4 10.3 %all-to-all-done = bf16[32,24,144]{2,1,0:T(8,128)(2,1)S(1)} async-done(((bf16[32,24,144]{2,1,0:T(8,128)(2,1)}), bf16[32,24,144]{2,1,0:T(8,128)(2,1)S(1)}, u32[]{:S(2)}, u32[]{:S(2)}) %all-to-all-start) | async-done | bytes 221216 | tf_op jit(solution)/shard_map/all_to_all | solution.py:1098
  29.1 3.9 %all-to-all-start.1 = ((f32[32,8,144]{2,1,0:T(8,128)}), f32[32,8,144]{2,1,0:T(8,128)S(1)}, u32[]{:S(2)}, u32[]{:S(2)}) async-start(f32[32,8,144]{2,1,0:T(8,128)} %get-tuple-element.140), calls=%async_computation.1 | async-start | bytes 524288 | tf_op jit(solution)/shard_map/all_to_all | solution.py:1122
  34.0 2.4 collective-permute-start.8
  36.7 5.9 %collective-permute-done.5 = bf16[48,1920]{1,0:T(8,128)(2,1)S(1)} collective-permute-done((bf16[48,1920]{1,0:T(8,128)(2,1)S(1)}, bf16[48,1920]{1,0:T(8,128)(2,1)S(1)}, u32[]{:S(2)}, u32[]{:S(2)}) %collective-permute-start.5) | collective-permute-done | bytes 184352 | tf_op jit(solution)/shard_map/ppermute | solution.py:903
  42.6 2.1 collective-permute-start.9
  44.7 4.4 %prep_kernel.1 = (f32[512,768]{1,0:T(8,128)S(1)}, bf16[512,768]{1,0:T(8,128)(2,1)S(1)}, f32[4,4608]{1,0:T(4,128)S(1)}, f32[1,2304]{1,0:T(1,128)S(1)}, f32[1,768]...) custom-call(s32[8]{0:T(128)S(1)} %get-tuple-element.135.refs_0_.refs_1_, ...), custom_call_target="tpu_custom_call" | custom-call | flops 10000000000 | bytes 1 | tf_op jit(solution)/shard_map/prep_kernel/pallas_call | solution.py:851
  49.1 11.0 %collective-permute-done.9 = bf16[96,1920]{1,0:T(8,128)(2,1)} collective-permute-done((bf16[96,1920]{1,0:T(8,128)(2,1)S(1)}, bf16[96,1920]{1,0:T(8,128)(2,1)}, u32[]{:S(2)}, u32[]{:S(2)}) %collective-permute-start.9) | collective-permute-done | bytes 368672 | tf_op jit(solution)/shard_map/ppermute | solution.py:903
  66.0 3.2 %collective-permute-start.11 = (bf16[96,768]{1,0:T(8,128)(2,1)S(1)}, bf16[96,768]{1,0:T(8,128)(2,1)S(1)}, u32[]{:S(2)}, u32[]{:S(2)}) collective-permute-start(bf16[96,768]{1,0:T(8,128)(2,1)S(1)} %copy-done.13), channel_id=1, source_target_pairs={{0,16},{1,17},{2,18},{3,19},{4,20},{5,21},{6,22},{7,23},{8,24},{9,... | collective-permute-start | bytes 442376 | tf_op jit(solution)/shard_map/ppermute | solution.py:903
  69.3 4.7 %qkv_kernel.1 = (bf16[512,768]{1,0:T(8,128)(2,1)}, bf16[512,2304]{1,0:T(8,128)(2,1)S(1)}, bf16[768,2304]{1,0:T(8,128)(2,1)}, f32[8,128]{1,0:T(8,128)S(1)}) custom-call(s32[3]{0:T(128)S(1)} %pad_add_fusion.refs_0_, f32[512,768]{1,0:T(8,128)S(1)} %get-tuple-element.143.refs_1_.refs_4_, f32[4,4608]{1,0:T(4,128)S(1)} %get-tuple-element.144.refs_2_.refs_3_.refs_4_, ...), custom_call_target="tpu_custom_call" | custom-call | flops 1 | bytes 1 | tf_op jit(solution)/shard_map/qkv_kernel/pallas_call | solution.py:851
  74.9 5.1 %attend_kernel.1 = (bf16[512,768]{1,0:T(8,128)(2,1)S(1)}, bf16[512,768]{1,0:T(8,128)(2,1)}, f32[8,128]{1,0:T(8,128)S(1)}) custom-call(bf16[512,2304]{1,0:T(8,128)(2,1)S(1)} %get-tuple-element.148.refs_0_, f32[8,128]{1,0:T(8,128)} %copy-done.17, bf16[192,768]{1,0:T(8,128)(2,1)S(1)} %get-tuple-element.150.refs_2_), custom_call_target="tpu_custom_call" | custom-call | flops 1 | bytes 1 | tf_op jit(solution)/shard_map/attend_kernel/pallas_call | solution.py:851
  86.6 2.1 collective-permute-start.18
  88.7 6.6 %collective-permute-done.14.refs_0_ = bf16[96,1920]{1,0:T(8,128)(2,1)S(1)} collective-permute-done((bf16[96,1920]{1,0:T(8,128)(2,1)S(1)}, bf16[96,1920]{1,0:T(8,128)(2,1)S(1)}, u32[]{:S(2)}, u32[]{:S(2)}) %collective-permute-start.14) | collective-permute-done | bytes 368672 | tf_op jit(solution)/shard_map/ppermute | solution.py:903
  100.5 15.6 %hidden_kernel.1 = (f32[512,768]{1,0:T(8,128)S(1)}, f32[512,768]{1,0:T(8,128)S(1)}, bf16[512,768]{1,0:T(8,128)(2,1)S(1)}, bf16[512,768]{1,0:T(8,128)(2,1)S(1)}, ...) custom-call(s32[3]{0:T(128)S(1)} %pad_add_fusion.refs_0_, ...), custom_call_target="tpu_custom_call" | custom-call | flops 1 | bytes 1 | tf_op jit(solution)/shard_map/hidden_kernel/pallas_call | solution.py:851
  117.1 3.3 %flips_kernel.1 = (bf16[768,512]{1,0:T(8,128)(2,1)S(1)}, bf16[768,512]{1,0:T(8,128)(2,1)}, bf16[768,512]{1,0:T(8,128)(2,1)}, f32[8,128]{1,0:T(8,128)}) custom-call(s32[3]{0:T(128)S(1)} %pad_add_fusion.refs_0_, bf16[512,768]{1,0:T(8,128)(2,1)S(1)} %get-tuple-element.160.refs_1_, bf16[512,768]{1,0:T(8,128)(2,1)} %get-tuple-element.161.refs_2_, ...), custom_call_target="tpu_custom_call" | custom-call | flops 1 | bytes 1 | tf_op jit(solution)/shard_map/flips_kernel/pallas_call | solution.py:851
  120.4 3.9 %probs_kernel.1 = (f32[3072,256]{1,0:T(8,128)}, f32[8,128]{1,0:T(8,128)}) custom-call(bf16[512,2304]{1,0:T(8,128)(2,1)} %copy-done, f32[8,128]{1,0:T(8,128)} %get-tuple-element.164.refs_1_), custom_call_target="tpu_custom_call" | custom-call | flops 1 | bytes 1 | tf_op jit(solution)/shard_map/probs_kernel/pallas_call | solution.py:851
  129.8 1.4 collective-permute-done.22.refs_4_.refs_8_
  131.2 5.8 %fc2_back_kernel.1 = (bf16[512,3072]{1,0:T(8,128)(2,1)S(1)}, f32[1,3072]{1,0:T(1,128)S(1)}, f32[8,128]{1,0:T(8,128)}) custom-call(s32[3]{0:T(128)S(1)} %pad_add_fusion.refs_0_, bf16[512,768]{1,0:T(8,128)(2,1)S(1)} %get-tuple-element.166.refs_1_, bf16[512,3072]{1,0:T(8,128)(2,1)} %get-tuple-element.167.refs_2_, ...), custom_call_target="tpu_custom_call" | custom-call | flops 1 | bytes 1 | tf_op jit(solution)/shard_map/fc2_back_kernel/pallas_call | solution.py:851
  137.0 4.2 %wgrad_kernel.2 = (bf16[768,1536]{1,0:T(8,128)(2,1)}, bf16[768,1536]{1,0:T(8,128)(2,1)}, f32[8,128]{1,0:T(8,128)}) custom-call(s32[3]{0:T(128)S(1)} %pad_add_fusion.refs_0_, bf16[768,512]{1,0:T(8,128)(2,1)S(1)} %get-tuple-element.180.refs_1_, bf16[512,3072]{1,0:T(8,128)(2,1)S(1)} %get-tuple-element.174.refs_2_.refs_1_), custom_call_target="tpu_custom_call" | custom-call | flops 1 | bytes 1 | tf_op jit(solution)/shard_map/wgrad_kernel/pallas_call | solution.py:851
  141.7 6.7 %fc2_out_kernel.1 = (bf16[128,768]{1,0:T(8,128)(2,1)S(1)}, f32[4,768]{1,0:T(4,128)S(1)}, bf16[512,768]{1,0:T(8,128)(2,1)}, f32[8,128]{1,0:T(8,128)}) custom-call(s32[3]{0:T(128)S(1)} %pad_add_fusion.refs_0_, s32[8]{0:T(128)S(1)} %get-tuple-element.135.refs_0_.refs_1_, f32[4,4608]{1,0:T(4,128)S(1)} %get-tuple-element.144.refs_2_.refs_3_.refs_4_, ...), custom_call_target="tpu_custom_call" | custom-call | flops 1 | bytes 1 | tf_op jit(solution)/shard_map/fc2_out_kernel/pallas_call | solution.py:851
  151.1 2.3 first_kernel.4
  155.1 15.6 %mid_back_kernel.1 = (bf16[512,768]{1,0:T(8,128)(2,1)S(1)}, f32[1,768]{1,0:T(1,128)S(1)}, f32[512,768]{1,0:T(8,128)}, bf16[512,768]{1,0:T(8,128)(2,1)}, bf16[32,16,768]{2,1,0:T(8,128)(2,1)}, /*index=5*/f32[8,128]{1,0:T(8,128)}) custom-call(s32[3]{0:T(128)S(1)} %pad_add_fusion.refs_0_, bf16[512,3072]{1,0:T(8,128)(2,1)S(1)} %get-tuple-element.174.refs_2_.refs_1_, ...), custom_call_target="tpu_custom_call" | custom-call | flops 1 | bytes 1 | tf_op jit(solution)/shard_map/mid_back_kernel/pallas_call | solution.py:851
  170.8 2.0 near_kernel.3
  172.8 2.4 collective-permute-start.31
  175.2 8.1 %attend_back_kernel.1 = (bf16[512,2304]{1,0:T(8,128)(2,1)S(1)}, f32[1,2304]{1,0:T(1,128)S(1)}, f32[8,128]{1,0:T(8,128)}) custom-call(bf16[512,2304]{1,0:T(8,128)(2,1)} %copy-done, f32[3072,256]{1,0:T(8,128)} %get-tuple-element.165.refs_1_, bf16[512,768]{1,0:T(8,128)(2,1)S(1)} %get-tuple-element.190.refs_2_, f32[8,128]{1,0:T(8,128)} %get-tuple-element.194.refs_3_), custom_call_target="tpu_custom_call" | custom-call | flops 1 | bytes 1 | tf_op jit(solution)/shard_map/attend_back_kernel/pallas_call | solution.py:851
  183.4 2.5 beyond_kernel.2
  185.9 2.3 second_kernel.4
  189.5 5.9 %all-to-all-start.2 = ((bf16[32,16,768]{2,1,0:T(8,128)(2,1)}), bf16[32,16,768]{2,1,0:T(8,128)(2,1)S(1)}, u32[]{:S(2)}, u32[]{:S(2)}) async-start(bf16[32,16,768]{2,1,0:T(8,128)(2,1)} %get-tuple-element.217), calls=%async_computation.2 | async-start | bytes 1572864 | tf_op jit(solution)/shard_map/all_to_all | solution.py:1376
  195.5 6.5 %wgrad_kernel.3 = (bf16[768,1536]{1,0:T(8,128)(2,1)}, bf16[768,1536]{1,0:T(8,128)(2,1)}, f32[8,128]{1,0:T(8,128)}) custom-call(s32[3]{0:T(128)S(1)} %copy-done.15, bf16[768,512]{1,0:T(8,128)(2,1)} %get-tuple-element.199.refs_1_, bf16[768,512]{1,0:T(8,128)(2,1)} %get-tuple-element.200.refs_2_, bf16[512,768]{1,0:T(8,128)(2,1)} %get-tuple-element.201.refs_3_, ...), custom_call_target="tpu_custom_call" | custom-call | flops 1 | bytes 1 | tf_op jit(solution)/shard_map/wgrad_kernel/pallas_call | solution.py:851
  202.4 3.7 %near_kernel.4 = (bf16[96,1536]{1,0:T(8,128)(2,1)}, f32[48,1536]{1,0:T(8,128)}, f32[48,1536]{1,0:T(8,128)}, f32[8,128]{1,0:T(8,128)}) custom-call(bf16[768,1536]{1,0:T(8,128)(2,1)} %get-tuple-element.183.refs_0_, bf16[768,1536]{1,0:T(8,128)(2,1)S(1)} %copy-done.6, bf16[192,1536]{1,0:T(8,128)(2,1)S(1)} %copy-done.23, bf16[192,1536]{1,0:T(8,128)(2,1)S(1)} %copy-done.25, ...), custom_call_target="tpu_custom_call" | custom-call | flops 99999997952 | bytes 1 | tf_op jit(solution)/shard_map/near_kernel/pallas_call | solution.py:851
  206.8 3.2 %first_kernel.5 = (bf16[192,1536]{1,0:T(8,128)(2,1)}, bf16[192,1536]{1,0:T(8,128)(2,1)}, f32[8,128]{1,0:T(8,128)}) custom-call(bf16[768,1536]{1,0:T(8,128)(2,1)} %get-tuple-element.210.refs_0_, bf16[768,1536]{1,0:T(8,128)(2,1)S(1)} %collective-permute-done.32.refs_1_, f32[8,128]{1,0:T(8,128)} %get-tuple-element.215.refs_2_), custom_call_target="tpu_custom_call" | custom-call | flops 1 | bytes 1 | tf_op jit(solution)/shard_map/first_kernel/pallas_call | solution.py:851
  212.7 2.8 all-to-all-done.2.refs_8_.refs_2_
  216.4 7.8 %start_back_kernel.1 = (f32[512,768]{1,0:T(8,128)}, bf16[384,768]{1,0:T(8,128)(2,1)}, bf16[32,8,768]{2,1,0:T(8,128)(2,1)}, f32[8,128]{1,0:T(8,128)}) custom-call(s32[8]{0:T(128)S(1)} %copy-done.19, bf16[512,2304]{1,0:T(8,128)(2,1)S(1)} %get-tuple-element.195.refs_4_.refs_1_, f32[4,4608]{1,0:T(4,128)S(1)} %copy-done.8, bf16[128,768]{1,0:T(8,128)(2,1)S(1)} %copy-done.12, ...), custom_call_target="tpu_custom_call" | custom-call | flops 1 | bytes 1 | tf_op jit(solution)/shard_map/start_back_kernel/pallas_call | solution.py:851
  224.2 4.2 %all-to-all-start.3 = ((bf16[32,8,768]{2,1,0:T(8,128)(2,1)}), bf16[32,8,768]{2,1,0:T(8,128)(2,1)S(1)}, u32[]{:S(2)}, u32[]{:S(2)}) async-start(bf16[32,8,768]{2,1,0:T(8,128)(2,1)} %get-tuple-element.227), calls=%async_computation.3 | async-start | bytes 786432 | tf_op jit(solution)/shard_map/all_to_all | solution.py:1435
  228.5 2.7 second_kernel.5
  231.2 2.5 beyond_kernel.3
  233.7 2.2 collective-permute-start.45
  236.1 3.9 %collective-permute-start.35 = (bf16[384,768]{1,0:T(8,128)(2,1)}, bf16[384,768]{1,0:T(8,128)(2,1)S(1)}, u32[]{:S(2)}, u32[]{:S(2)}) collective-permute-start(bf16[384,768]{1,0:T(8,128)(2,1)} %get-tuple-element.218), channel_id=1, source_target_pairs={{0,1},{1,2},{2,3},{3,4},{4,5},{5,6},{6,7},{7,8},{8,9},{9,10},{10,1... | collective-permute-start | bytes 1769480 | tf_op jit(solution)/shard_map/ppermute | solution.py:1445
  242.4 4.4 %all-to-all-done.3.refs_3_ = bf16[32,8,768]{2,1,0:T(8,128)(2,1)S(1)} async-done(((bf16[32,8,768]{2,1,0:T(8,128)(2,1)}), bf16[32,8,768]{2,1,0:T(8,128)(2,1)S(1)}, u32[]{:S(2)}, u32[]{:S(2)}) %all-to-all-start.3) | async-done | bytes 393248 | tf_op jit(solution)/shard_map/all_to_all | solution.py:1435
  246.9 4.9 %ada_kernel.1 = (f32[24,4608]{1,0:T(8,128)}, f32[1,4608]{1,0:T(1,128)S(1)}, bf16[32,32,128]{2,1,0:T(8,128)(2,1)}, f32[8,128]{1,0:T(8,128)S(1)}) custom-call(s32[3]{0:T(128)S(1)} %copy-done.16, s32[32]{0:T(128)S(1)} %get-tuple-element.226.refs_1_, bf16[32,16,768]{2,1,0:T(8,128)(2,1)S(1)} %all-to-all-done.2.refs_8_.refs_2_, ...), custom_call_target="tpu_custom_call" | custom-call | flops 1 | bytes 1 | tf_op jit(solution)/shard_map/ada_kernel/pallas_call | solution.py:851
  252.9 4.0 %all-to-all-start.4 = ((bf16[32,32,128]{2,1,0:T(8,128)(2,1)}), bf16[32,32,128]{2,1,0:T(8,128)(2,1)S(1)}, u32[]{:S(2)}, u32[]{:S(2)}) async-start(bf16[32,32,128]{2,1,0:T(8,128)(2,1)} %get-tuple-element.241), calls=%async_computation.4 | async-start | bytes 524288 | tf_op jit(solution)/shard_map/all_to_all | solution.py:1461
  259.1 1.8 convert_add_fusion
  260.9 2.7 near_kernel.5
  263.7 2.4 collective-permute-start.42
  266.3 5.1 %place_kernel.1 = (bf16[512,768]{1,0:T(8,128)(2,1)}, f32[512,768]{1,0:T(8,128)}, f32[8,128]{1,0:T(8,128)}) custom-call(s32[8]{0:T(128)S(1)} %copy-done.19, bf16[384,768]{1,0:T(8,128)(2,1)S(1)} %collective-permute-done.35.refs_1_, bf16[512,768]{1,0:T(8,128)(2,1)} %refs_2_.5, bf16[512,768]{1,0:T(8,128)(2,1)} %refs_3_.5, ...), custom_call_target="tpu_custom_call" | custom-call | flops 1 | bytes 1 | tf_op jit(solution)/shard_map/place_kernel/pallas_call | solution.py:851
  274.2 5.1 %collective-permute-done.43 = bf16[48,1536]{1,0:T(8,128)(2,1)S(1)} collective-permute-done((bf16[48,1536]{1,0:T(8,128)(2,1)S(1)}, bf16[48,1536]{1,0:T(8,128)(2,1)S(1)}, u32[]{:S(2)}, u32[]{:S(2)}) %collective-permute-start.43) | collective-permute-done | bytes 147488 | tf_op jit(solution)/shard_map/ppermute | solution.py:903
  (202 shorter events, 55.3 us)
Async XLA Ops:
  4.5 23.2 %all-to-all-start = ((bf16[32,24,144]{2,1,0:T(8,128)(2,1)}), bf16[32,24,144]{2,1,0:T(8,128)(2,1)S(1)}, u32[]{:S(2)}, u32[]{:S(2)}) async-start(bf16[32,24,144]{2,1,0:T(8,128)(2,1)} %get-tuple-element.137), calls=%async_computation | async-start | bytes 786432 | tf_op jit(solution)/shard_map/all_to_all | solution.py:1098
  11.3 33.4 %collective-permute-start.1 = (bf16[256,768]{1,0:T(8,128)(2,1)S(1)}, bf16[256,768]{1,0:T(8,128)(2,1)S(1)}, u32[]{:S(2)}, u32[]{:S(2)}) collective-permute-start(bf16[256,768]{1,0:T(8,128)(2,1)S(1)} %get-tuple-element.141), channel_id=1, source_target_pairs={{1,0},{2,1},{3,2},{4,3},{5,4},{6,5},{7,6},{8,7},{9,8},{10,9},{11,1... | collective-permute-start | bytes 1179656 | tf_op jit(solution)/shard_map/ppermute | solution.py:1096
  14.0 19.9 %collective-permute-start.4 = (bf16[48,1152]{1,0:T(8,128)(2,1)S(1)}, bf16[48,1152]{1,0:T(8,128)(2,1)S(1)}, u32[]{:S(2)}, u32[]{:S(2)}) collective-permute-start(bf16[48,1152]{1,0:T(8,128)(2,1)S(1)} %slice.84), channel_id=1, source_target_pairs={{0,24},{1,25},{2,26},{3,27},{4,28},{5,29},{6,30},{7,31},{8,16},{9,... | collective-permute-start | bytes 331784 | tf_op jit(solution)/shard_map/ppermute | solution.py:903
  15.2 18.6 %collective-permute-start.3 = (bf16[48,1152]{1,0:T(8,128)(2,1)S(1)}, bf16[48,1152]{1,0:T(8,128)(2,1)S(1)}, u32[]{:S(2)}, u32[]{:S(2)}) collective-permute-start(bf16[48,1152]{1,0:T(8,128)(2,1)S(1)} %slice.84), channel_id=1, source_target_pairs={{0,16},{1,17},{2,18},{3,19},{4,20},{5,21},{6,22},{7,23},{8,24},{9,... | collective-permute-start | bytes 331784 | tf_op jit(solution)/shard_map/ppermute | solution.py:903
  16.3 17.6 %collective-permute-start.2 = (bf16[48,1152]{1,0:T(8,128)(2,1)S(1)}, bf16[48,1152]{1,0:T(8,128)(2,1)S(1)}, u32[]{:S(2)}, u32[]{:S(2)}) collective-permute-start(bf16[48,1152]{1,0:T(8,128)(2,1)S(1)} %slice.84), channel_id=1, source_target_pairs={{0,8},{1,9},{2,10},{3,11},{4,12},{5,13},{6,14},{7,15},{8,0},{9,1},... | collective-permute-start | bytes 331784 | tf_op jit(solution)/shard_map/ppermute | solution.py:903
  29.1 15.6 %all-to-all-start.1 = ((f32[32,8,144]{2,1,0:T(8,128)}), f32[32,8,144]{2,1,0:T(8,128)S(1)}, u32[]{:S(2)}, u32[]{:S(2)}) async-start(f32[32,8,144]{2,1,0:T(8,128)} %get-tuple-element.140), calls=%async_computation.1 | async-start | bytes 524288 | tf_op jit(solution)/shard_map/all_to_all | solution.py:1122
  33.7 8.9 %collective-permute-start.5 = (bf16[48,1920]{1,0:T(8,128)(2,1)S(1)}, bf16[48,1920]{1,0:T(8,128)(2,1)S(1)}, u32[]{:S(2)}, u32[]{:S(2)}) collective-permute-start(bf16[48,1920]{1,0:T(8,128)(2,1)S(1)} %slice_select_fusion), channel_id=1, source_target_pairs={{0,8},{1,9},{2,10},{3,11},{4,12},{5,13},{6,14},{7,15},{8,0},{9,1},... | collective-permute-start | bytes 552968 | tf_op jit(solution)/shard_map/ppermute | solution.py:903
  34.0 27.2 %collective-permute-start.8 = (bf16[192,1152]{1,0:T(8,128)(2,1)S(1)}, bf16[192,1152]{1,0:T(8,128)(2,1)S(1)}, u32[]{:S(2)}, u32[]{:S(2)}) collective-permute-start(bf16[192,1152]{1,0:T(8,128)(2,1)S(1)} %maximum_select_fusion.refs_7_.refs_0_), channel_id=1, source_target_pairs={{0,6},{1,7},{2,4},{3,5},{4,2},{5,3},{6,0},{7,1},{8,14},{9,15},{10,... | collective-permute-start | bytes 1327112 | tf_op jit(solution)/shard_map/ppermute | solution.py:903
  36.3 24.9 %collective-permute-start.7 = (bf16[192,1152]{1,0:T(8,128)(2,1)S(1)}, bf16[192,1152]{1,0:T(8,128)(2,1)S(1)}, u32[]{:S(2)}, u32[]{:S(2)}) collective-permute-start(bf16[192,1152]{1,0:T(8,128)(2,1)S(1)} %maximum_select_fusion.refs_7_.refs_0_), channel_id=1, source_target_pairs={{0,4},{1,5},{2,6},{3,7},{4,0},{5,1},{6,2},{7,3},{8,12},{9,13},{10,... | collective-permute-start | bytes 1327112 | tf_op jit(solution)/shard_map/ppermute | solution.py:903
  36.6 24.6 %collective-permute-start.6 = (bf16[192,1152]{1,0:T(8,128)(2,1)S(1)}, bf16[192,1152]{1,0:T(8,128)(2,1)S(1)}, u32[]{:S(2)}, u32[]{:S(2)}) collective-permute-start(bf16[192,1152]{1,0:T(8,128)(2,1)S(1)} %maximum_select_fusion.refs_7_.refs_0_), channel_id=1, source_target_pairs={{0,2},{1,3},{2,0},{3,1},{4,6},{5,7},{6,4},{7,5},{8,10},{9,11},{10,... | collective-permute-start | bytes 1327112 | tf_op jit(solution)/shard_map/ppermute | solution.py:903
  42.6 17.5 %collective-permute-start.9 = (bf16[96,1920]{1,0:T(8,128)(2,1)S(1)}, bf16[96,1920]{1,0:T(8,128)(2,1)}, u32[]{:S(2)}, u32[]{:S(2)}) collective-permute-start(bf16[96,1920]{1,0:T(8,128)(2,1)S(1)} %pad_maximum_fusion.1.refs_8_), channel_id=1, source_target_pairs={{0,16},{1,17},{2,18},{3,19},{4,20},{5,21},{6,22},{7,23},{8,24},{9,... | collective-permute-start | bytes 1105928 | tf_op jit(solution)/shard_map/ppermute | solution.py:903
  62.3 7.0 %collective-permute-start.10 = (bf16[768,1152]{1,0:T(8,128)(2,1)S(1)}, bf16[768,1152]{1,0:T(8,128)(2,1)S(1)}, u32[]{:S(2)}, u32[]{:S(2)}) collective-permute-start(bf16[768,1152]{1,0:T(8,128)(2,1)S(1)} %get-tuple-element.147.refs_4_), channel_id=1, source_target_pairs={{0,1},{1,0},{2,3},{3,2},{4,5},{5,4},{6,7},{7,6},{8,9},{9,8},{10,11... | collective-permute-start | bytes 5308424 | tf_op jit(solution)/shard_map/ppermute | solution.py:903
  63.6 18.1 %collective-permute-start.13 = (bf16[192,1920]{1,0:T(8,128)(2,1)S(1)}, bf16[192,1920]{1,0:T(8,128)(2,1)S(1)}, u32[]{:S(2)}, u32[]{:S(2)}) collective-permute-start(bf16[192,1920]{1,0:T(8,128)(2,1)S(1)} %pad_maximum_fusion.refs_5_.refs_0_), channel_id=1, source_target_pairs={{0,4},{1,5},{2,6},{3,7},{4,0},{5,1},{6,2},{7,3},{8,12},{9,13},{10,... | collective-permute-start | bytes 2211848 | tf_op jit(solution)/shard_map/ppermute | solution.py:903
  64.9 17.7 %collective-permute-start.12 = (bf16[192,1920]{1,0:T(8,128)(2,1)S(1)}, bf16[192,1920]{1,0:T(8,128)(2,1)S(1)}, u32[]{:S(2)}, u32[]{:S(2)}) collective-permute-start(bf16[192,1920]{1,0:T(8,128)(2,1)S(1)} %pad_maximum_fusion.refs_5_.refs_0_), channel_id=1, source_target_pairs={{0,2},{1,3},{2,0},{3,1},{4,6},{5,7},{6,4},{7,5},{8,10},{9,11},{10,... | collective-permute-start | bytes 2211848 | tf_op jit(solution)/shard_map/ppermute | solution.py:903
  66.0 8.5 %collective-permute-start.11 = (bf16[96,768]{1,0:T(8,128)(2,1)S(1)}, bf16[96,768]{1,0:T(8,128)(2,1)S(1)}, u32[]{:S(2)}, u32[]{:S(2)}) collective-permute-start(bf16[96,768]{1,0:T(8,128)(2,1)S(1)} %copy-done.13), channel_id=1, source_target_pairs={{0,16},{1,17},{2,18},{3,19},{4,20},{5,21},{6,22},{7,23},{8,24},{9,... | collective-permute-start | bytes 442376 | tf_op jit(solution)/shard_map/ppermute | solution.py:903
  83.9 16.6 %collective-permute-start.16 = (bf16[576,1920]{1,0:T(8,128)(2,1)S(1)}, bf16[576,1920]{1,0:T(8,128)(2,1)S(1)}, u32[]{:S(2)}, u32[]{:S(2)}) collective-permute-start(bf16[576,1920]{1,0:T(8,128)(2,1)S(1)} %get-tuple-element.156.refs_7_), channel_id=1, source_target_pairs={{0,1},{1,0},{2,3},{3,2},{4,5},{5,4},{6,7},{7,6},{8,9},{9,8},{10,11... | collective-permute-start | bytes 6635528 | tf_op jit(solution)/shard_map/ppermute | solution.py:903
  85.1 10.2 %collective-permute-start.14 = (bf16[96,1920]{1,0:T(8,128)(2,1)S(1)}, bf16[96,1920]{1,0:T(8,128)(2,1)S(1)}, u32[]{:S(2)}, u32[]{:S(2)}) collective-permute-start(bf16[96,1920]{1,0:T(8,128)(2,1)S(1)} %get-tuple-element.157), channel_id=1, source_target_pairs={{0,2},{1,3},{2,0},{3,1},{4,6},{5,7},{6,4},{7,5},{8,10},{9,11},{10,... | collective-permute-start | bytes 1105928 | tf_op jit(solution)/shard_map/ppermute | solution.py:903
  86.3 9.8 %collective-permute-start.15 = (bf16[96,1920]{1,0:T(8,128)(2,1)S(1)}, bf16[96,1920]{1,0:T(8,128)(2,1)S(1)}, u32[]{:S(2)}, u32[]{:S(2)}) collective-permute-start(bf16[96,1920]{1,0:T(8,128)(2,1)S(1)} %get-tuple-element.158), channel_id=1, source_target_pairs={{0,4},{1,5},{2,6},{3,7},{4,0},{5,1},{6,2},{7,3},{8,12},{9,13},{10,... | collective-permute-start | bytes 1105928 | tf_op jit(solution)/shard_map/ppermute | solution.py:903
  86.6 11.2 %collective-permute-start.18 = (bf16[192,768]{1,0:T(8,128)(2,1)S(1)}, bf16[192,768]{1,0:T(8,128)(2,1)S(1)}, u32[]{:S(2)}, u32[]{:S(2)}) collective-permute-start(bf16[192,768]{1,0:T(8,128)(2,1)S(1)} %get-tuple-element.150.refs_2_), channel_id=1, source_target_pairs={{0,8},{1,9},{2,10},{3,11},{4,12},{5,13},{6,14},{7,15},{8,0},{9,1},... | collective-permute-start | bytes 884744 | tf_op jit(solution)/shard_map/ppermute | solution.py:903
  97.8 26.4 %collective-permute-start.21 = (bf16[384,768]{1,0:T(8,128)(2,1)S(1)}, bf16[384,768]{1,0:T(8,128)(2,1)S(1)}, u32[]{:S(2)}, u32[]{:S(2)}) collective-permute-start(bf16[384,768]{1,0:T(8,128)(2,1)S(1)} %constant_dynamic-update-slice_fusion.refs_0_), channel_id=1, source_target_pairs={{0,6},{1,7},{2,4},{3,5},{4,2},{5,3},{6,0},{7,1},{8,14},{9,15},{10,... | collective-permute-start | bytes 1769480 | tf_op jit(solution)/shard_map/ppermute | solution.py:903
  98.1 27.3 %collective-permute-start.20 = (bf16[384,768]{1,0:T(8,128)(2,1)S(1)}, bf16[384,768]{1,0:T(8,128)(2,1)S(1)}, u32[]{:S(2)}, u32[]{:S(2)}) collective-permute-start(bf16[384,768]{1,0:T(8,128)(2,1)S(1)} %constant_dynamic-update-slice_fusion.refs_0_), channel_id=1, source_target_pairs={{0,4},{1,5},{2,6},{3,7},{4,0},{5,1},{6,2},{7,3},{8,12},{9,13},{10,... | collective-permute-start | bytes 1769480 | tf_op jit(solution)/shard_map/ppermute | solution.py:903
  99.3 26.1 %collective-permute-start.19 = (bf16[384,768]{1,0:T(8,128)(2,1)S(1)}, bf16[384,768]{1,0:T(8,128)(2,1)S(1)}, u32[]{:S(2)}, u32[]{:S(2)}) collective-permute-start(bf16[384,768]{1,0:T(8,128)(2,1)S(1)} %constant_dynamic-update-slice_fusion.refs_0_), channel_id=1, source_target_pairs={{0,2},{1,3},{2,0},{3,1},{4,6},{5,7},{6,4},{7,5},{8,10},{9,11},{10,... | collective-permute-start | bytes 1769480 | tf_op jit(solution)/shard_map/ppermute | solution.py:903
  116.2 10.9 %collective-permute-start.23 = (bf16[1536,768]{1,0:T(8,128)(2,1)}, bf16[1536,768]{1,0:T(8,128)(2,1)S(1)}, u32[]{:S(2)}, u32[]{:S(2)}) collective-permute-start(bf16[1536,768]{1,0:T(8,128)(2,1)} %get-tuple-element.171), channel_id=1, source_target_pairs={{0,1},{1,0},{2,3},{3,2},{4,5},{5,4},{6,7},{7,6},{8,9},{9,8},{10,11... | collective-permute-start | bytes 7077896 | tf_op jit(solution)/shard_map/ppermute | solution.py:903
  128.4 20.0 %collective-permute-start.25 = (bf16[384,768]{1,0:T(8,128)(2,1)S(1)}, bf16[384,768]{1,0:T(8,128)(2,1)S(1)}, u32[]{:S(2)}, u32[]{:S(2)}) collective-permute-start(bf16[384,768]{1,0:T(8,128)(2,1)S(1)} %get-tuple-element.185), channel_id=1, source_target_pairs={{0,2},{1,3},{2,0},{3,1},{4,6},{5,7},{6,4},{7,5},{8,10},{9,11},{10,... | collective-permute-start | bytes 1769480 | tf_op jit(solution)/shard_map/ppermute | solution.py:903
  129.5 19.0 %collective-permute-start.26 = (bf16[384,768]{1,0:T(8,128)(2,1)S(1)}, bf16[384,768]{1,0:T(8,128)(2,1)S(1)}, u32[]{:S(2)}, u32[]{:S(2)}) collective-permute-start(bf16[384,768]{1,0:T(8,128)(2,1)S(1)} %get-tuple-element.186), channel_id=1, source_target_pairs={{0,4},{1,5},{2,6},{3,7},{4,0},{5,1},{6,2},{7,3},{8,12},{9,13},{10,... | collective-permute-start | bytes 1769480 | tf_op jit(solution)/shard_map/ppermute | solution.py:903
  141.3 9.9 %collective-permute-start.24 = (bf16[768,1536]{1,0:T(8,128)(2,1)}, bf16[768,1536]{1,0:T(8,128)(2,1)S(1)}, u32[]{:S(2)}, u32[]{:S(2)}) collective-permute-start(bf16[768,1536]{1,0:T(8,128)(2,1)} %get-tuple-element.184), channel_id=1, source_target_pairs={{0,1},{1,0},{2,3},{3,2},{4,5},{5,4},{6,7},{7,6},{8,9},{9,8},{10,11... | collective-permute-start | bytes 7077896 | tf_op jit(solution)/shard_map/ppermute | solution.py:903
  149.8 21.0 %collective-permute-start.27 = (bf16[192,768]{1,0:T(8,128)(2,1)S(1)}, bf16[192,768]{1,0:T(8,128)(2,1)S(1)}, u32[]{:S(2)}, u32[]{:S(2)}) collective-permute-start(bf16[192,768]{1,0:T(8,128)(2,1)S(1)} %get-tuple-element.191), channel_id=1, source_target_pairs={{0,2},{1,3},{2,0},{3,1},{4,6},{5,7},{6,4},{7,5},{8,10},{9,11},{10,... | collective-permute-start | bytes 884744 | tf_op jit(solution)/shard_map/ppermute | solution.py:903
  150.8 20.0 %collective-permute-start.28 = (bf16[192,768]{1,0:T(8,128)(2,1)S(1)}, bf16[192,768]{1,0:T(8,128)(2,1)S(1)}, u32[]{:S(2)}, u32[]{:S(2)}) collective-permute-start(bf16[192,768]{1,0:T(8,128)(2,1)S(1)} %get-tuple-element.192), channel_id=1, source_target_pairs={{0,4},{1,5},{2,6},{3,7},{4,0},{5,1},{6,2},{7,3},{8,12},{9,13},{10,... | collective-permute-start | bytes 884744 | tf_op jit(solution)/shard_map/ppermute | solution.py:903
  153.4 32.4 %collective-permute-start.29 = (bf16[192,1536]{1,0:T(8,128)(2,1)S(1)}, bf16[192,1536]{1,0:T(8,128)(2,1)S(1)}, u32[]{:S(2)}, u32[]{:S(2)}) collective-permute-start(bf16[192,1536]{1,0:T(8,128)(2,1)S(1)} %get-tuple-element.202), channel_id=1, source_target_pairs={{0,2},{1,3},{2,0},{3,1},{4,6},{5,7},{6,4},{7,5},{8,10},{9,11},{10,... | collective-permute-start | bytes 1769480 | tf_op jit(solution)/shard_map/ppermute | solution.py:903
  154.7 31.2 %collective-permute-start.30 = (bf16[192,1536]{1,0:T(8,128)(2,1)S(1)}, bf16[192,1536]{1,0:T(8,128)(2,1)S(1)}, u32[]{:S(2)}, u32[]{:S(2)}) collective-permute-start(bf16[192,1536]{1,0:T(8,128)(2,1)S(1)} %get-tuple-element.203), channel_id=1, source_target_pairs={{0,4},{1,5},{2,6},{3,7},{4,0},{5,1},{6,2},{7,3},{8,12},{9,13},{10,... | collective-permute-start | bytes 1769480 | tf_op jit(solution)/shard_map/ppermute | solution.py:903
  172.8 10.6 %collective-permute-start.31 = (bf16[192,768]{1,0:T(8,128)(2,1)S(1)}, bf16[192,768]{1,0:T(8,128)(2,1)S(1)}, u32[]{:S(2)}, u32[]{:S(2)}) collective-permute-start(bf16[192,768]{1,0:T(8,128)(2,1)S(1)} %get-tuple-element.204), channel_id=1, source_target_pairs={{0,8},{1,9},{2,10},{3,11},{4,12},{5,13},{6,14},{7,15},{8,0},{9,1},... | collective-permute-start | bytes 884744 | tf_op jit(solution)/shard_map/ppermute | solution.py:903
  188.3 14.1 %collective-permute-start.33 = (bf16[96,1536]{1,0:T(8,128)(2,1)}, bf16[96,1536]{1,0:T(8,128)(2,1)S(1)}, u32[]{:S(2)}, u32[]{:S(2)}) collective-permute-start(bf16[96,1536]{1,0:T(8,128)(2,1)} %get-tuple-element.212), channel_id=1, source_target_pairs={{0,2},{1,3},{2,0},{3,1},{4,6},{5,7},{6,4},{7,5},{8,10},{9,11},{10,... | collective-permute-start | bytes 884744 | tf_op jit(solution)/shard_map/ppermute | solution.py:903
  189.0 13.4 %collective-permute-start.34 = (bf16[96,1536]{1,0:T(8,128)(2,1)}, bf16[96,1536]{1,0:T(8,128)(2,1)}, u32[]{:S(2)}, u32[]{:S(2)}) collective-permute-start(bf16[96,1536]{1,0:T(8,128)(2,1)} %get-tuple-element.213), channel_id=1, source_target_pairs={{0,4},{1,5},{2,6},{3,7},{4,0},{5,1},{6,2},{7,3},{8,12},{9,13},{10,... | collective-permute-start | bytes 884744 | tf_op jit(solution)/shard_map/ppermute | solution.py:903
  189.5 26.0 %all-to-all-start.2 = ((bf16[32,16,768]{2,1,0:T(8,128)(2,1)}), bf16[32,16,768]{2,1,0:T(8,128)(2,1)S(1)}, u32[]{:S(2)}, u32[]{:S(2)}) async-start(bf16[32,16,768]{2,1,0:T(8,128)(2,1)} %get-tuple-element.217), calls=%async_computation.2 | async-start | bytes 1572864 | tf_op jit(solution)/shard_map/all_to_all | solution.py:1376
  210.0 18.4 %collective-permute-start.36 = (bf16[192,1536]{1,0:T(8,128)(2,1)}, bf16[192,1536]{1,0:T(8,128)(2,1)}, u32[]{:S(2)}, u32[]{:S(2)}) collective-permute-start(bf16[192,1536]{1,0:T(8,128)(2,1)} %get-tuple-element.221), channel_id=1, source_target_pairs={{0,2},{1,3},{2,0},{3,1},{4,6},{5,7},{6,4},{7,5},{8,10},{9,11},{10,... | collective-permute-start | bytes 1769480 | tf_op jit(solution)/shard_map/ppermute | solution.py:903
  211.3 17.2 %collective-permute-start.37 = (bf16[192,1536]{1,0:T(8,128)(2,1)}, bf16[192,1536]{1,0:T(8,128)(2,1)}, u32[]{:S(2)}, u32[]{:S(2)}) collective-permute-start(bf16[192,1536]{1,0:T(8,128)(2,1)} %get-tuple-element.222), channel_id=1, source_target_pairs={{0,4},{1,5},{2,6},{3,7},{4,0},{5,1},{6,2},{7,3},{8,12},{9,13},{10,... | collective-permute-start | bytes 1769480 | tf_op jit(solution)/shard_map/ppermute | solution.py:903
  212.5 18.7 %collective-permute-start.40 = (bf16[96,1536]{1,0:T(8,128)(2,1)}, bf16[96,1536]{1,0:T(8,128)(2,1)S(1)}, u32[]{:S(2)}, u32[]{:S(2)}) collective-permute-start(bf16[96,1536]{1,0:T(8,128)(2,1)} %get-tuple-element.232), channel_id=1, source_target_pairs={{0,8},{1,9},{2,10},{3,11},{4,12},{5,13},{6,14},{7,15},{8,0},{9,1},... | collective-permute-start | bytes 884744 | tf_op jit(solution)/shard_map/ppermute | solution.py:903
  224.2 22.6 %all-to-all-start.3 = ((bf16[32,8,768]{2,1,0:T(8,128)(2,1)}), bf16[32,8,768]{2,1,0:T(8,128)(2,1)S(1)}, u32[]{:S(2)}, u32[]{:S(2)}) async-start(bf16[32,8,768]{2,1,0:T(8,128)(2,1)} %get-tuple-element.227), calls=%async_computation.3 | async-start | bytes 786432 | tf_op jit(solution)/shard_map/all_to_all | solution.py:1435
  233.7 23.3 %collective-permute-start.45 = (bf16[48,1536]{1,0:T(8,128)(2,1)}, bf16[48,1536]{1,0:T(8,128)(2,1)}, u32[]{:S(2)}, u32[]{:S(2)}) collective-permute-start(bf16[48,1536]{1,0:T(8,128)(2,1)} %get-tuple-element.253), channel_id=1, source_target_pairs={{0,16},{1,17},{2,18},{3,19},{4,20},{5,21},{6,22},{7,23},{8,24},{9,... | collective-permute-start | bytes 442376 | tf_op jit(solution)/shard_map/ppermute | solution.py:903
  235.9 23.2 %collective-permute-start.47 = (bf16[96,768]{1,0:T(8,128)(2,1)}, bf16[96,768]{1,0:T(8,128)(2,1)}, u32[]{:S(2)}, u32[]{:S(2)}) collective-permute-start(bf16[96,768]{1,0:T(8,128)(2,1)} %get-tuple-element.255), channel_id=1, source_target_pairs={{0,16},{1,17},{2,18},{3,19},{4,20},{5,21},{6,22},{7,23},{8,24},{9,... | collective-permute-start | bytes 442376 | tf_op jit(solution)/shard_map/ppermute | solution.py:903
  236.1 30.2 %collective-permute-start.35 = (bf16[384,768]{1,0:T(8,128)(2,1)}, bf16[384,768]{1,0:T(8,128)(2,1)S(1)}, u32[]{:S(2)}, u32[]{:S(2)}) collective-permute-start(bf16[384,768]{1,0:T(8,128)(2,1)} %get-tuple-element.218), channel_id=1, source_target_pairs={{0,1},{1,2},{2,3},{3,4},{4,5},{5,6},{6,7},{7,8},{8,9},{9,10},{10,1... | collective-permute-start | bytes 1769480 | tf_op jit(solution)/shard_map/ppermute | solution.py:1445
  240.0 20.9 %collective-permute-start.38 = (bf16[96,1536]{1,0:T(8,128)(2,1)S(1)}, bf16[96,1536]{1,0:T(8,128)(2,1)S(1)}, u32[]{:S(2)}, u32[]{:S(2)}) collective-permute-start(bf16[96,1536]{1,0:T(8,128)(2,1)S(1)} %get-tuple-element.224), channel_id=1, source_target_pairs={{0,2},{1,3},{2,0},{3,1},{4,6},{5,7},{6,4},{7,5},{8,10},{9,11},{10,... | collective-permute-start | bytes 884744 | tf_op jit(solution)/shard_map/ppermute | solution.py:903
  241.3 19.7 %collective-permute-start.39 = (bf16[96,1536]{1,0:T(8,128)(2,1)S(1)}, bf16[96,1536]{1,0:T(8,128)(2,1)S(1)}, u32[]{:S(2)}, u32[]{:S(2)}) collective-permute-start(bf16[96,1536]{1,0:T(8,128)(2,1)S(1)} %get-tuple-element.225), channel_id=1, source_target_pairs={{0,4},{1,5},{2,6},{3,7},{4,0},{5,1},{6,2},{7,3},{8,12},{9,13},{10,... | collective-permute-start | bytes 884744 | tf_op jit(solution)/shard_map/ppermute | solution.py:903
  252.9 19.2 %all-to-all-start.4 = ((bf16[32,32,128]{2,1,0:T(8,128)(2,1)}), bf16[32,32,128]{2,1,0:T(8,128)(2,1)S(1)}, u32[]{:S(2)}, u32[]{:S(2)}) async-start(bf16[32,32,128]{2,1,0:T(8,128)(2,1)} %get-tuple-element.241), calls=%async_computation.4 | async-start | bytes 524288 | tf_op jit(solution)/shard_map/all_to_all | solution.py:1461
  258.1 13.4 %collective-permute-start.46 = (f32[24,1536]{1,0:T(8,128)S(1)}, f32[24,1536]{1,0:T(8,128)S(1)}, u32[]{:S(2)}, u32[]{:S(2)}) collective-permute-start(f32[24,1536]{1,0:T(8,128)S(1)} %get-tuple-element.257), channel_id=1, source_target_pairs={{0,1},{1,0},{2,3},{3,2},{4,5},{5,4},{6,7},{7,6},{8,9},{9,8},{10,11... | collective-permute-start | bytes 442376 | tf_op jit(solution)/shard_map/ppermute | solution.py:903
  263.6 10.6 %collective-permute-start.41 = (bf16[48,1536]{1,0:T(8,128)(2,1)S(1)}, bf16[48,1536]{1,0:T(8,128)(2,1)S(1)}, u32[]{:S(2)}, u32[]{:S(2)}) collective-permute-start(bf16[48,1536]{1,0:T(8,128)(2,1)S(1)} %get-tuple-element.248), channel_id=1, source_target_pairs={{0,8},{1,9},{2,10},{3,11},{4,12},{5,13},{6,14},{7,15},{8,0},{9,1},... | collective-permute-start | bytes 442376 | tf_op jit(solution)/shard_map/ppermute | solution.py:903
  263.7 10.5 %collective-permute-start.42 = (bf16[48,1536]{1,0:T(8,128)(2,1)S(1)}, bf16[48,1536]{1,0:T(8,128)(2,1)S(1)}, u32[]{:S(2)}, u32[]{:S(2)}) collective-permute-start(bf16[48,1536]{1,0:T(8,128)(2,1)S(1)} %get-tuple-element.249), channel_id=1, source_target_pairs={{0,16},{1,17},{2,18},{3,19},{4,20},{5,21},{6,22},{7,23},{8,24},{9,... | collective-permute-start | bytes 442376 | tf_op jit(solution)/shard_map/ppermute | solution.py:903
  266.0 13.3 %collective-permute-start.43 = (bf16[48,1536]{1,0:T(8,128)(2,1)S(1)}, bf16[48,1536]{1,0:T(8,128)(2,1)S(1)}, u32[]{:S(2)}, u32[]{:S(2)}) collective-permute-start(bf16[48,1536]{1,0:T(8,128)(2,1)S(1)} %get-tuple-element.250), channel_id=1, source_target_pairs={{0,24},{1,25},{2,26},{3,27},{4,28},{5,29},{6,30},{7,31},{8,16},{9,... | collective-permute-start | bytes 442376 | tf_op jit(solution)/shard_map/ppermute | solution.py:903
  (40 other events, 766.8 us)

commit v2 on v0

--- a/solution.py
+++ b/solution.py
@@ -1499,7 +1499,7 @@
     )
     fc1_widths, qkv_widths = [F // 2], [D // 2, 3 * D // 2]
     if cube:
-        fc2_grad = tie(fc2_own, finished) + fc2_beyond.astype(f32)
+        fc2_grad = tie(fc2_own, ada_ran) + fc2_beyond.astype(f32)
         (fc1_grad,) = links.own_rows(
             tie(fc1_own, ada_ran) + fc1_beyond.astype(f32), fc1_widths
         )

time: 283 us -> 284 us (level)
  transfers between devices with their start and end apart: 53 -> 53, of which waited for: 14 -> 15; matrix products, arithmetic and copies ran while one was open for 3% -> 3% of each run, Pallas kernels for 46% -> 46%
where the time goes in v2:
time: 284 us; the launch traced here: 280 us
  Pallas kernels  136 us (48%)
  starting transfers between devices  78 us (27%)
  waiting for transfers between devices  49.4 us (17%)
  other arithmetic  6.5 us (2%)
  local copies, waits for them, and re-layouts  6.39 us (2%)
  between operations  3.86 us (1%)
    pallas_call x34, Pallas kernels, call(): pl.pallas_call(body, out_shape=out_shape, in_specs=list(spaces) + [ANY] *...  136 us
    ppermute x46, starting transfers between devices, swap(): lax.ppermute(array, 'wide', [(i, i ^ bits) for i in range(self.devices)])  48.3 us
    ppermute x46, waiting for transfers between devices, swap(): lax.ppermute(array, 'wide', [(i, i ^ bits) for i in range(self.devices)])  34.9 us
    all_to_all x1, waiting for transfers between devices, on_device(): ada_cols = lax.all_to_all(ada_parts, 'wide', 0, 0, tiled=True)  10.3 us
    all_to_all x1, starting transfers between devices, on_device(): ada_cols = lax.all_to_all(ada_parts, 'wide', 0, 0, tiled=True)  6.36 us
    all_to_all x1, starting transfers between devices, on_device(): early = lax.all_to_all(early, 'wide', 0, 0, tiled=True)  5.9 us
  transfers between devices with their start and end apart: 53, of which 15 were waited for; matrix products, arithmetic and copies ran while one was open for 3% of the time, Pallas kernels for 46%

profile of v2, /device:TPU:9, one launch (start us, length us, event | category | flops | bytes accessed | tf_op | source)
XLA Modules:
  0.0 279.8 jit_solution(1822428998381911473)
XLA Ops:
  1.5 3.0 %begin_kernel.1 = (bf16[24,3072]{1,0:T(8,128)(2,1)S(1)}, bf16[24,3072]{1,0:T(8,128)(2,1)S(1)}, bf16[256,768]{1,0:T(8,128)(2,1)S(1)}, s32[8]{0:T(128)S(1)}, s32[3...) custom-call(s32[3]{0:T(128)S(1)} %pad_add_fusion.refs_0_, ...), custom_call_target="tpu_custom_call" | custom-call | flops 1 | bytes 1 | tf_op jit(solution)/shard_map/begin_kernel/pallas_call | solution.py:851
  4.5 6.4 %all-to-all-start = ((bf16[32,24,144]{2,1,0:T(8,128)(2,1)}), bf16[32,24,144]{2,1,0:T(8,128)(2,1)S(1)}, u32[]{:S(2)}, u32[]{:S(2)}) async-start(bf16[32,24,144]{2,1,0:T(8,128)(2,1)} %get-tuple-element.137), calls=%async_computation | async-start | bytes 786432 | tf_op jit(solution)/shard_map/all_to_all | solution.py:1098
  11.3 2.0 collective-permute-start.1
  17.4 10.3 %all-to-all-done = bf16[32,24,144]{2,1,0:T(8,128)(2,1)S(1)} async-done(((bf16[32,24,144]{2,1,0:T(8,128)(2,1)}), bf16[32,24,144]{2,1,0:T(8,128)(2,1)S(1)}, u32[]{:S(2)}, u32[]{:S(2)}) %all-to-all-start) | async-done | bytes 221216 | tf_op jit(solution)/shard_map/all_to_all | solution.py:1098
  29.1 3.9 %all-to-all-start.1 = ((f32[32,8,144]{2,1,0:T(8,128)}), f32[32,8,144]{2,1,0:T(8,128)S(1)}, u32[]{:S(2)}, u32[]{:S(2)}) async-start(f32[32,8,144]{2,1,0:T(8,128)} %get-tuple-element.140), calls=%async_computation.1 | async-start | bytes 524288 | tf_op jit(solution)/shard_map/all_to_all | solution.py:1122
  34.0 2.4 collective-permute-start.8
  36.7 5.9 %collective-permute-done.5 = bf16[48,1920]{1,0:T(8,128)(2,1)S(1)} collective-permute-done((bf16[48,1920]{1,0:T(8,128)(2,1)S(1)}, bf16[48,1920]{1,0:T(8,128)(2,1)S(1)}, u32[]{:S(2)}, u32[]{:S(2)}) %collective-permute-start.5) | collective-permute-done | bytes 184352 | tf_op jit(solution)/shard_map/ppermute | solution.py:903
  42.6 2.1 collective-permute-start.9
  44.7 4.4 %prep_kernel.1 = (f32[512,768]{1,0:T(8,128)S(1)}, bf16[512,768]{1,0:T(8,128)(2,1)S(1)}, f32[4,4608]{1,0:T(4,128)S(1)}, f32[1,2304]{1,0:T(1,128)S(1)}, f32[1,768]...) custom-call(s32[8]{0:T(128)S(1)} %get-tuple-element.135.refs_0_.refs_1_, ...), custom_call_target="tpu_custom_call" | custom-call | flops 10000000000 | bytes 1 | tf_op jit(solution)/shard_map/prep_kernel/pallas_call | solution.py:851
  49.1 11.0 %collective-permute-done.9 = bf16[96,1920]{1,0:T(8,128)(2,1)} collective-permute-done((bf16[96,1920]{1,0:T(8,128)(2,1)S(1)}, bf16[96,1920]{1,0:T(8,128)(2,1)}, u32[]{:S(2)}, u32[]{:S(2)}) %collective-permute-start.9) | collective-permute-done | bytes 368672 | tf_op jit(solution)/shard_map/ppermute | solution.py:903
  66.0 3.2 %collective-permute-start.11 = (bf16[96,768]{1,0:T(8,128)(2,1)S(1)}, bf16[96,768]{1,0:T(8,128)(2,1)S(1)}, u32[]{:S(2)}, u32[]{:S(2)}) collective-permute-start(bf16[96,768]{1,0:T(8,128)(2,1)S(1)} %copy-done.13), channel_id=1, source_target_pairs={{0,16},{1,17},{2,18},{3,19},{4,20},{5,21},{6,22},{7,23},{8,24},{9,... | collective-permute-start | bytes 442376 | tf_op jit(solution)/shard_map/ppermute | solution.py:903
  69.3 4.7 %qkv_kernel.1 = (bf16[512,768]{1,0:T(8,128)(2,1)}, bf16[512,2304]{1,0:T(8,128)(2,1)S(1)}, bf16[768,2304]{1,0:T(8,128)(2,1)}, f32[8,128]{1,0:T(8,128)S(1)}) custom-call(s32[3]{0:T(128)S(1)} %pad_add_fusion.refs_0_, f32[512,768]{1,0:T(8,128)S(1)} %get-tuple-element.143.refs_1_.refs_4_, f32[4,4608]{1,0:T(4,128)S(1)} %get-tuple-element.144.refs_2_.refs_3_.refs_4_, ...), custom_call_target="tpu_custom_call" | custom-call | flops 1 | bytes 1 | tf_op jit(solution)/shard_map/qkv_kernel/pallas_call | solution.py:851
  74.9 5.1 %attend_kernel.1 = (bf16[512,768]{1,0:T(8,128)(2,1)S(1)}, bf16[512,768]{1,0:T(8,128)(2,1)}, f32[8,128]{1,0:T(8,128)S(1)}) custom-call(bf16[512,2304]{1,0:T(8,128)(2,1)S(1)} %get-tuple-element.148.refs_0_, f32[8,128]{1,0:T(8,128)} %copy-done.17, bf16[192,768]{1,0:T(8,128)(2,1)S(1)} %get-tuple-element.150.refs_2_), custom_call_target="tpu_custom_call" | custom-call | flops 1 | bytes 1 | tf_op jit(solution)/shard_map/attend_kernel/pallas_call | solution.py:851
  86.6 2.1 collective-permute-start.18
  88.7 6.6 %collective-permute-done.14.refs_0_ = bf16[96,1920]{1,0:T(8,128)(2,1)S(1)} collective-permute-done((bf16[96,1920]{1,0:T(8,128)(2,1)S(1)}, bf16[96,1920]{1,0:T(8,128)(2,1)S(1)}, u32[]{:S(2)}, u32[]{:S(2)}) %collective-permute-start.14) | collective-permute-done | bytes 368672 | tf_op jit(solution)/shard_map/ppermute | solution.py:903
  100.5 15.6 %hidden_kernel.1 = (f32[512,768]{1,0:T(8,128)S(1)}, f32[512,768]{1,0:T(8,128)S(1)}, bf16[512,768]{1,0:T(8,128)(2,1)S(1)}, bf16[512,768]{1,0:T(8,128)(2,1)S(1)}, ...) custom-call(s32[3]{0:T(128)S(1)} %pad_add_fusion.refs_0_, ...), custom_call_target="tpu_custom_call" | custom-call | flops 1 | bytes 1 | tf_op jit(solution)/shard_map/hidden_kernel/pallas_call | solution.py:851
  117.1 3.3 %flips_kernel.1 = (bf16[768,512]{1,0:T(8,128)(2,1)S(1)}, bf16[768,512]{1,0:T(8,128)(2,1)}, bf16[768,512]{1,0:T(8,128)(2,1)}, f32[8,128]{1,0:T(8,128)}) custom-call(s32[3]{0:T(128)S(1)} %pad_add_fusion.refs_0_, bf16[512,768]{1,0:T(8,128)(2,1)S(1)} %get-tuple-element.160.refs_1_, bf16[512,768]{1,0:T(8,128)(2,1)} %get-tuple-element.161.refs_2_, ...), custom_call_target="tpu_custom_call" | custom-call | flops 1 | bytes 1 | tf_op jit(solution)/shard_map/flips_kernel/pallas_call | solution.py:851
  120.4 3.8 %probs_kernel.1 = (f32[3072,256]{1,0:T(8,128)}, f32[8,128]{1,0:T(8,128)}) custom-call(bf16[512,2304]{1,0:T(8,128)(2,1)} %copy-done, f32[8,128]{1,0:T(8,128)} %get-tuple-element.164.refs_1_), custom_call_target="tpu_custom_call" | custom-call | flops 1 | bytes 1 | tf_op jit(solution)/shard_map/probs_kernel/pallas_call | solution.py:851
  129.8 1.4 collective-permute-done.22.refs_4_.refs_8_
  131.2 5.8 %fc2_back_kernel.1 = (bf16[512,3072]{1,0:T(8,128)(2,1)S(1)}, f32[1,3072]{1,0:T(1,128)S(1)}, f32[8,128]{1,0:T(8,128)}) custom-call(s32[3]{0:T(128)S(1)} %pad_add_fusion.refs_0_, bf16[512,768]{1,0:T(8,128)(2,1)S(1)} %get-tuple-element.166.refs_1_, bf16[512,3072]{1,0:T(8,128)(2,1)} %get-tuple-element.167.refs_2_, ...), custom_call_target="tpu_custom_call" | custom-call | flops 1 | bytes 1 | tf_op jit(solution)/shard_map/fc2_back_kernel/pallas_call | solution.py:851
  137.0 4.2 %wgrad_kernel.2 = (bf16[768,1536]{1,0:T(8,128)(2,1)}, bf16[768,1536]{1,0:T(8,128)(2,1)}, f32[8,128]{1,0:T(8,128)}) custom-call(s32[3]{0:T(128)S(1)} %pad_add_fusion.refs_0_, bf16[768,512]{1,0:T(8,128)(2,1)S(1)} %get-tuple-element.180.refs_1_, bf16[512,3072]{1,0:T(8,128)(2,1)S(1)} %get-tuple-element.174.refs_2_.refs_1_), custom_call_target="tpu_custom_call" | custom-call | flops 1 | bytes 1 | tf_op jit(solution)/shard_map/wgrad_kernel/pallas_call | solution.py:851
  141.7 6.7 %fc2_out_kernel.1 = (bf16[128,768]{1,0:T(8,128)(2,1)S(1)}, f32[4,768]{1,0:T(4,128)S(1)}, bf16[512,768]{1,0:T(8,128)(2,1)}, f32[8,128]{1,0:T(8,128)}) custom-call(s32[3]{0:T(128)S(1)} %pad_add_fusion.refs_0_, s32[8]{0:T(128)S(1)} %get-tuple-element.135.refs_0_.refs_1_, f32[4,4608]{1,0:T(4,128)S(1)} %get-tuple-element.144.refs_2_.refs_3_.refs_4_, ...), custom_call_target="tpu_custom_call" | custom-call | flops 1 | bytes 1 | tf_op jit(solution)/shard_map/fc2_out_kernel/pallas_call | solution.py:851
  151.1 2.3 first_kernel.4
  155.1 15.6 %mid_back_kernel.1 = (bf16[512,768]{1,0:T(8,128)(2,1)S(1)}, f32[1,768]{1,0:T(1,128)S(1)}, f32[512,768]{1,0:T(8,128)}, bf16[512,768]{1,0:T(8,128)(2,1)}, bf16[32,16,768]{2,1,0:T(8,128)(2,1)}, /*index=5*/f32[8,128]{1,0:T(8,128)}) custom-call(s32[3]{0:T(128)S(1)} %pad_add_fusion.refs_0_, bf16[512,3072]{1,0:T(8,128)(2,1)S(1)} %get-tuple-element.174.refs_2_.refs_1_, ...), custom_call_target="tpu_custom_call" | custom-call | flops 1 | bytes 1 | tf_op jit(solution)/shard_map/mid_back_kernel/pallas_call | solution.py:851
  170.8 2.0 near_kernel.3
  172.8 2.4 collective-permute-start.31
  175.2 8.1 %attend_back_kernel.1 = (bf16[512,2304]{1,0:T(8,128)(2,1)S(1)}, f32[1,2304]{1,0:T(1,128)S(1)}, f32[8,128]{1,0:T(8,128)}) custom-call(bf16[512,2304]{1,0:T(8,128)(2,1)} %copy-done, f32[3072,256]{1,0:T(8,128)} %get-tuple-element.165.refs_1_, bf16[512,768]{1,0:T(8,128)(2,1)S(1)} %get-tuple-element.190.refs_2_, f32[8,128]{1,0:T(8,128)} %get-tuple-element.194.refs_3_), custom_call_target="tpu_custom_call" | custom-call | flops 1 | bytes 1 | tf_op jit(solution)/shard_map/attend_back_kernel/pallas_call | solution.py:851
  183.3 1.8 beyond_kernel.2
  185.2 2.3 second_kernel.4
  188.9 5.9 %all-to-all-start.2 = ((bf16[32,16,768]{2,1,0:T(8,128)(2,1)}), bf16[32,16,768]{2,1,0:T(8,128)(2,1)S(1)}, u32[]{:S(2)}, u32[]{:S(2)}) async-start(bf16[32,16,768]{2,1,0:T(8,128)(2,1)} %get-tuple-element.217), calls=%async_computation.2 | async-start | bytes 1572864 | tf_op jit(solution)/shard_map/all_to_all | solution.py:1376
  194.8 6.5 %wgrad_kernel.3 = (bf16[768,1536]{1,0:T(8,128)(2,1)}, bf16[768,1536]{1,0:T(8,128)(2,1)}, f32[8,128]{1,0:T(8,128)}) custom-call(s32[3]{0:T(128)S(1)} %copy-done.15, bf16[768,512]{1,0:T(8,128)(2,1)} %get-tuple-element.199.refs_1_, bf16[768,512]{1,0:T(8,128)(2,1)} %get-tuple-element.200.refs_2_, bf16[512,768]{1,0:T(8,128)(2,1)} %get-tuple-element.201.refs_3_, ...), custom_call_target="tpu_custom_call" | custom-call | flops 1 | bytes 1 | tf_op jit(solution)/shard_map/wgrad_kernel/pallas_call | solution.py:851
  201.8 3.6 %near_kernel.4 = (bf16[96,1536]{1,0:T(8,128)(2,1)}, f32[48,1536]{1,0:T(8,128)}, f32[48,1536]{1,0:T(8,128)}, f32[8,128]{1,0:T(8,128)}) custom-call(bf16[768,1536]{1,0:T(8,128)(2,1)} %get-tuple-element.183.refs_0_, bf16[768,1536]{1,0:T(8,128)(2,1)S(1)} %copy-done.6, bf16[192,1536]{1,0:T(8,128)(2,1)S(1)} %copy-done.23, bf16[192,1536]{1,0:T(8,128)(2,1)S(1)} %copy-done.25, ...), custom_call_target="tpu_custom_call" | custom-call | flops 99999997952 | bytes 1 | tf_op jit(solution)/shard_map/near_kernel/pallas_call | solution.py:851
  206.2 3.2 %first_kernel.5 = (bf16[192,1536]{1,0:T(8,128)(2,1)}, bf16[192,1536]{1,0:T(8,128)(2,1)}, f32[8,128]{1,0:T(8,128)}) custom-call(bf16[768,1536]{1,0:T(8,128)(2,1)} %get-tuple-element.210.refs_0_, bf16[768,1536]{1,0:T(8,128)(2,1)S(1)} %collective-permute-done.32.refs_1_, f32[8,128]{1,0:T(8,128)} %get-tuple-element.215.refs_2_), custom_call_target="tpu_custom_call" | custom-call | flops 1 | bytes 1 | tf_op jit(solution)/shard_map/first_kernel/pallas_call | solution.py:851
  212.1 2.1 collective-permute-start.47
  215.8 7.8 %start_back_kernel.1 = (f32[512,768]{1,0:T(8,128)}, bf16[384,768]{1,0:T(8,128)(2,1)}, bf16[32,8,768]{2,1,0:T(8,128)(2,1)}, f32[8,128]{1,0:T(8,128)}) custom-call(s32[8]{0:T(128)S(1)} %copy-done.19, bf16[512,2304]{1,0:T(8,128)(2,1)S(1)} %get-tuple-element.195.refs_4_.refs_1_, f32[4,4608]{1,0:T(4,128)S(1)} %copy-done.8, bf16[128,768]{1,0:T(8,128)(2,1)S(1)} %copy-done.12, ...), custom_call_target="tpu_custom_call" | custom-call | flops 1 | bytes 1 | tf_op jit(solution)/shard_map/start_back_kernel/pallas_call | solution.py:851
  223.6 4.2 %all-to-all-start.3 = ((bf16[32,8,768]{2,1,0:T(8,128)(2,1)}), bf16[32,8,768]{2,1,0:T(8,128)(2,1)S(1)}, u32[]{:S(2)}, u32[]{:S(2)}) async-start(bf16[32,8,768]{2,1,0:T(8,128)(2,1)} %get-tuple-element.231), calls=%async_computation.3 | async-start | bytes 786432 | tf_op jit(solution)/shard_map/all_to_all | solution.py:1435
  227.9 1.8 beyond_kernel.3
  229.7 2.3 collective-permute-start.45
  232.0 3.6 %collective-permute-start.35 = (bf16[384,768]{1,0:T(8,128)(2,1)}, bf16[384,768]{1,0:T(8,128)(2,1)}, u32[]{:S(2)}, u32[]{:S(2)}) collective-permute-start(bf16[384,768]{1,0:T(8,128)(2,1)} %get-tuple-element.218), channel_id=1, source_target_pairs={{0,1},{1,2},{2,3},{3,4},{4,5},{5,6},{6,7},{7,8},{8,9},{9,10},{10,1... | collective-permute-start | bytes 1769480 | tf_op jit(solution)/shard_map/ppermute | solution.py:1445
  235.7 2.7 second_kernel.5
  239.7 3.5 %all-to-all-done.3.refs_3_ = bf16[32,8,768]{2,1,0:T(8,128)(2,1)S(1)} async-done(((bf16[32,8,768]{2,1,0:T(8,128)(2,1)}), bf16[32,8,768]{2,1,0:T(8,128)(2,1)S(1)}, u32[]{:S(2)}, u32[]{:S(2)}) %all-to-all-start.3) | async-done | bytes 393248 | tf_op jit(solution)/shard_map/all_to_all | solution.py:1435
  243.3 4.9 %ada_kernel.1 = (f32[24,4608]{1,0:T(8,128)}, f32[1,4608]{1,0:T(1,128)S(1)}, bf16[32,32,128]{2,1,0:T(8,128)(2,1)}, f32[8,128]{1,0:T(8,128)S(1)}) custom-call(s32[3]{0:T(128)S(1)} %copy-done.16, s32[32]{0:T(128)S(1)} %get-tuple-element.230.refs_1_, bf16[32,16,768]{2,1,0:T(8,128)(2,1)S(1)} %all-to-all-done.2.refs_8_.refs_2_, ...), custom_call_target="tpu_custom_call" | custom-call | flops 1 | bytes 1 | tf_op jit(solution)/shard_map/ada_kernel/pallas_call | solution.py:851
  250.4 3.7 %all-to-all-start.4 = ((bf16[32,32,128]{2,1,0:T(8,128)(2,1)}), bf16[32,32,128]{2,1,0:T(8,128)(2,1)S(1)}, u32[]{:S(2)}, u32[]{:S(2)}) async-start(bf16[32,32,128]{2,1,0:T(8,128)(2,1)} %get-tuple-element.241), calls=%async_computation.4 | async-start | bytes 524288 | tf_op jit(solution)/shard_map/all_to_all | solution.py:1461
  255.1 1.7 convert_add_fusion
  256.8 2.7 near_kernel.5
  259.5 2.4 collective-permute-start.42
  262.2 5.6 %place_kernel.1 = (bf16[512,768]{1,0:T(8,128)(2,1)}, f32[512,768]{1,0:T(8,128)}, f32[8,128]{1,0:T(8,128)}) custom-call(s32[8]{0:T(128)S(1)} %copy-done.19, bf16[384,768]{1,0:T(8,128)(2,1)} %collective-permute-done.35.refs_1_, bf16[512,768]{1,0:T(8,128)(2,1)} %refs_2_.5, bf16[512,768]{1,0:T(8,128)(2,1)} %refs_3_.5, ...), custom_call_target="tpu_custom_call" | custom-call | flops 1 | bytes 1 | tf_op jit(solution)/shard_map/place_kernel/pallas_call | solution.py:851
  270.6 4.6 %collective-permute-done.43 = bf16[48,1536]{1,0:T(8,128)(2,1)S(1)} collective-permute-done((bf16[48,1536]{1,0:T(8,128)(2,1)S(1)}, bf16[48,1536]{1,0:T(8,128)(2,1)S(1)}, u32[]{:S(2)}, u32[]{:S(2)}) %collective-permute-start.43) | collective-permute-done | bytes 147488 | tf_op jit(solution)/shard_map/ppermute | solution.py:903
  (208 shorter events, 54.5 us)
Async XLA Ops:
  4.5 23.2 %all-to-all-start = ((bf16[32,24,144]{2,1,0:T(8,128)(2,1)}), bf16[32,24,144]{2,1,0:T(8,128)(2,1)S(1)}, u32[]{:S(2)}, u32[]{:S(2)}) async-start(bf16[32,24,144]{2,1,0:T(8,128)(2,1)} %get-tuple-element.137), calls=%async_computation | async-start | bytes 786432 | tf_op jit(solution)/shard_map/all_to_all | solution.py:1098
  11.3 33.4 %collective-permute-start.1 = (bf16[256,768]{1,0:T(8,128)(2,1)S(1)}, bf16[256,768]{1,0:T(8,128)(2,1)S(1)}, u32[]{:S(2)}, u32[]{:S(2)}) collective-permute-start(bf16[256,768]{1,0:T(8,128)(2,1)S(1)} %get-tuple-element.141), channel_id=1, source_target_pairs={{1,0},{2,1},{3,2},{4,3},{5,4},{6,5},{7,6},{8,7},{9,8},{10,9},{11,1... | collective-permute-start | bytes 1179656 | tf_op jit(solution)/shard_map/ppermute | solution.py:1096
  14.0 19.9 %collective-permute-start.4 = (bf16[48,1152]{1,0:T(8,128)(2,1)S(1)}, bf16[48,1152]{1,0:T(8,128)(2,1)S(1)}, u32[]{:S(2)}, u32[]{:S(2)}) collective-permute-start(bf16[48,1152]{1,0:T(8,128)(2,1)S(1)} %slice.84), channel_id=1, source_target_pairs={{0,24},{1,25},{2,26},{3,27},{4,28},{5,29},{6,30},{7,31},{8,16},{9,... | collective-permute-start | bytes 331784 | tf_op jit(solution)/shard_map/ppermute | solution.py:903
  15.2 18.6 %collective-permute-start.3 = (bf16[48,1152]{1,0:T(8,128)(2,1)S(1)}, bf16[48,1152]{1,0:T(8,128)(2,1)S(1)}, u32[]{:S(2)}, u32[]{:S(2)}) collective-permute-start(bf16[48,1152]{1,0:T(8,128)(2,1)S(1)} %slice.84), channel_id=1, source_target_pairs={{0,16},{1,17},{2,18},{3,19},{4,20},{5,21},{6,22},{7,23},{8,24},{9,... | collective-permute-start | bytes 331784 | tf_op jit(solution)/shard_map/ppermute | solution.py:903
  16.3 17.6 %collective-permute-start.2 = (bf16[48,1152]{1,0:T(8,128)(2,1)S(1)}, bf16[48,1152]{1,0:T(8,128)(2,1)S(1)}, u32[]{:S(2)}, u32[]{:S(2)}) collective-permute-start(bf16[48,1152]{1,0:T(8,128)(2,1)S(1)} %slice.84), channel_id=1, source_target_pairs={{0,8},{1,9},{2,10},{3,11},{4,12},{5,13},{6,14},{7,15},{8,0},{9,1},... | collective-permute-start | bytes 331784 | tf_op jit(solution)/shard_map/ppermute | solution.py:903
  29.1 15.6 %all-to-all-start.1 = ((f32[32,8,144]{2,1,0:T(8,128)}), f32[32,8,144]{2,1,0:T(8,128)S(1)}, u32[]{:S(2)}, u32[]{:S(2)}) async-start(f32[32,8,144]{2,1,0:T(8,128)} %get-tuple-element.140), calls=%async_computation.1 | async-start | bytes 524288 | tf_op jit(solution)/shard_map/all_to_all | solution.py:1122
  33.7 8.9 %collective-permute-start.5 = (bf16[48,1920]{1,0:T(8,128)(2,1)S(1)}, bf16[48,1920]{1,0:T(8,128)(2,1)S(1)}, u32[]{:S(2)}, u32[]{:S(2)}) collective-permute-start(bf16[48,1920]{1,0:T(8,128)(2,1)S(1)} %slice_select_fusion), channel_id=1, source_target_pairs={{0,8},{1,9},{2,10},{3,11},{4,12},{5,13},{6,14},{7,15},{8,0},{9,1},... | collective-permute-start | bytes 552968 | tf_op jit(solution)/shard_map/ppermute | solution.py:903
  34.0 27.2 %collective-permute-start.8 = (bf16[192,1152]{1,0:T(8,128)(2,1)S(1)}, bf16[192,1152]{1,0:T(8,128)(2,1)S(1)}, u32[]{:S(2)}, u32[]{:S(2)}) collective-permute-start(bf16[192,1152]{1,0:T(8,128)(2,1)S(1)} %maximum_select_fusion.refs_7_.refs_0_), channel_id=1, source_target_pairs={{0,6},{1,7},{2,4},{3,5},{4,2},{5,3},{6,0},{7,1},{8,14},{9,15},{10,... | collective-permute-start | bytes 1327112 | tf_op jit(solution)/shard_map/ppermute | solution.py:903
  36.3 24.9 %collective-permute-start.7 = (bf16[192,1152]{1,0:T(8,128)(2,1)S(1)}, bf16[192,1152]{1,0:T(8,128)(2,1)S(1)}, u32[]{:S(2)}, u32[]{:S(2)}) collective-permute-start(bf16[192,1152]{1,0:T(8,128)(2,1)S(1)} %maximum_select_fusion.refs_7_.refs_0_), channel_id=1, source_target_pairs={{0,4},{1,5},{2,6},{3,7},{4,0},{5,1},{6,2},{7,3},{8,12},{9,13},{10,... | collective-permute-start | bytes 1327112 | tf_op jit(solution)/shard_map/ppermute | solution.py:903
  36.6 24.6 %collective-permute-start.6 = (bf16[192,1152]{1,0:T(8,128)(2,1)S(1)}, bf16[192,1152]{1,0:T(8,128)(2,1)S(1)}, u32[]{:S(2)}, u32[]{:S(2)}) collective-permute-start(bf16[192,1152]{1,0:T(8,128)(2,1)S(1)} %maximum_select_fusion.refs_7_.refs_0_), channel_id=1, source_target_pairs={{0,2},{1,3},{2,0},{3,1},{4,6},{5,7},{6,4},{7,5},{8,10},{9,11},{10,... | collective-permute-start | bytes 1327112 | tf_op jit(solution)/shard_map/ppermute | solution.py:903
  42.6 17.5 %collective-permute-start.9 = (bf16[96,1920]{1,0:T(8,128)(2,1)S(1)}, bf16[96,1920]{1,0:T(8,128)(2,1)}, u32[]{:S(2)}, u32[]{:S(2)}) collective-permute-start(bf16[96,1920]{1,0:T(8,128)(2,1)S(1)} %pad_maximum_fusion.1.refs_8_), channel_id=1, source_target_pairs={{0,16},{1,17},{2,18},{3,19},{4,20},{5,21},{6,22},{7,23},{8,24},{9,... | collective-permute-start | bytes 1105928 | tf_op jit(solution)/shard_map/ppermute | solution.py:903
  62.3 7.0 %collective-permute-start.10 = (bf16[768,1152]{1,0:T(8,128)(2,1)S(1)}, bf16[768,1152]{1,0:T(8,128)(2,1)S(1)}, u32[]{:S(2)}, u32[]{:S(2)}) collective-permute-start(bf16[768,1152]{1,0:T(8,128)(2,1)S(1)} %get-tuple-element.147.refs_4_), channel_id=1, source_target_pairs={{0,1},{1,0},{2,3},{3,2},{4,5},{5,4},{6,7},{7,6},{8,9},{9,8},{10,11... | collective-permute-start | bytes 5308424 | tf_op jit(solution)/shard_map/ppermute | solution.py:903
  63.6 18.1 %collective-permute-start.13 = (bf16[192,1920]{1,0:T(8,128)(2,1)S(1)}, bf16[192,1920]{1,0:T(8,128)(2,1)S(1)}, u32[]{:S(2)}, u32[]{:S(2)}) collective-permute-start(bf16[192,1920]{1,0:T(8,128)(2,1)S(1)} %pad_maximum_fusion.refs_5_.refs_0_), channel_id=1, source_target_pairs={{0,4},{1,5},{2,6},{3,7},{4,0},{5,1},{6,2},{7,3},{8,12},{9,13},{10,... | collective-permute-start | bytes 2211848 | tf_op jit(solution)/shard_map/ppermute | solution.py:903
  64.9 17.7 %collective-permute-start.12 = (bf16[192,1920]{1,0:T(8,128)(2,1)S(1)}, bf16[192,1920]{1,0:T(8,128)(2,1)S(1)}, u32[]{:S(2)}, u32[]{:S(2)}) collective-permute-start(bf16[192,1920]{1,0:T(8,128)(2,1)S(1)} %pad_maximum_fusion.refs_5_.refs_0_), channel_id=1, source_target_pairs={{0,2},{1,3},{2,0},{3,1},{4,6},{5,7},{6,4},{7,5},{8,10},{9,11},{10,... | collective-permute-start | bytes 2211848 | tf_op jit(solution)/shard_map/ppermute | solution.py:903
  66.0 8.5 %collective-permute-start.11 = (bf16[96,768]{1,0:T(8,128)(2,1)S(1)}, bf16[96,768]{1,0:T(8,128)(2,1)S(1)}, u32[]{:S(2)}, u32[]{:S(2)}) collective-permute-start(bf16[96,768]{1,0:T(8,128)(2,1)S(1)} %copy-done.13), channel_id=1, source_target_pairs={{0,16},{1,17},{2,18},{3,19},{4,20},{5,21},{6,22},{7,23},{8,24},{9,... | collective-permute-start | bytes 442376 | tf_op jit(solution)/shard_map/ppermute | solution.py:903
  83.9 16.6 %collective-permute-start.16 = (bf16[576,1920]{1,0:T(8,128)(2,1)S(1)}, bf16[576,1920]{1,0:T(8,128)(2,1)S(1)}, u32[]{:S(2)}, u32[]{:S(2)}) collective-permute-start(bf16[576,1920]{1,0:T(8,128)(2,1)S(1)} %get-tuple-element.156.refs_7_), channel_id=1, source_target_pairs={{0,1},{1,0},{2,3},{3,2},{4,5},{5,4},{6,7},{7,6},{8,9},{9,8},{10,11... | collective-permute-start | bytes 6635528 | tf_op jit(solution)/shard_map/ppermute | solution.py:903
  85.1 10.2 %collective-permute-start.14 = (bf16[96,1920]{1,0:T(8,128)(2,1)S(1)}, bf16[96,1920]{1,0:T(8,128)(2,1)S(1)}, u32[]{:S(2)}, u32[]{:S(2)}) collective-permute-start(bf16[96,1920]{1,0:T(8,128)(2,1)S(1)} %get-tuple-element.157), channel_id=1, source_target_pairs={{0,2},{1,3},{2,0},{3,1},{4,6},{5,7},{6,4},{7,5},{8,10},{9,11},{10,... | collective-permute-start | bytes 1105928 | tf_op jit(solution)/shard_map/ppermute | solution.py:903
  86.3 9.8 %collective-permute-start.15 = (bf16[96,1920]{1,0:T(8,128)(2,1)S(1)}, bf16[96,1920]{1,0:T(8,128)(2,1)S(1)}, u32[]{:S(2)}, u32[]{:S(2)}) collective-permute-start(bf16[96,1920]{1,0:T(8,128)(2,1)S(1)} %get-tuple-element.158), channel_id=1, source_target_pairs={{0,4},{1,5},{2,6},{3,7},{4,0},{5,1},{6,2},{7,3},{8,12},{9,13},{10,... | collective-permute-start | bytes 1105928 | tf_op jit(solution)/shard_map/ppermute | solution.py:903
  86.6 11.2 %collective-permute-start.18 = (bf16[192,768]{1,0:T(8,128)(2,1)S(1)}, bf16[192,768]{1,0:T(8,128)(2,1)S(1)}, u32[]{:S(2)}, u32[]{:S(2)}) collective-permute-start(bf16[192,768]{1,0:T(8,128)(2,1)S(1)} %get-tuple-element.150.refs_2_), channel_id=1, source_target_pairs={{0,8},{1,9},{2,10},{3,11},{4,12},{5,13},{6,14},{7,15},{8,0},{9,1},... | collective-permute-start | bytes 884744 | tf_op jit(solution)/shard_map/ppermute | solution.py:903
  97.8 26.5 %collective-permute-start.21 = (bf16[384,768]{1,0:T(8,128)(2,1)S(1)}, bf16[384,768]{1,0:T(8,128)(2,1)S(1)}, u32[]{:S(2)}, u32[]{:S(2)}) collective-permute-start(bf16[384,768]{1,0:T(8,128)(2,1)S(1)} %constant_dynamic-update-slice_fusion.refs_0_), channel_id=1, source_target_pairs={{0,6},{1,7},{2,4},{3,5},{4,2},{5,3},{6,0},{7,1},{8,14},{9,15},{10,... | collective-permute-start | bytes 1769480 | tf_op jit(solution)/shard_map/ppermute | solution.py:903
  98.1 27.3 %collective-permute-start.20 = (bf16[384,768]{1,0:T(8,128)(2,1)S(1)}, bf16[384,768]{1,0:T(8,128)(2,1)S(1)}, u32[]{:S(2)}, u32[]{:S(2)}) collective-permute-start(bf16[384,768]{1,0:T(8,128)(2,1)S(1)} %constant_dynamic-update-slice_fusion.refs_0_), channel_id=1, source_target_pairs={{0,4},{1,5},{2,6},{3,7},{4,0},{5,1},{6,2},{7,3},{8,12},{9,13},{10,... | collective-permute-start | bytes 1769480 | tf_op jit(solution)/shard_map/ppermute | solution.py:903
  99.3 26.1 %collective-permute-start.19 = (bf16[384,768]{1,0:T(8,128)(2,1)S(1)}, bf16[384,768]{1,0:T(8,128)(2,1)S(1)}, u32[]{:S(2)}, u32[]{:S(2)}) collective-permute-start(bf16[384,768]{1,0:T(8,128)(2,1)S(1)} %constant_dynamic-update-slice_fusion.refs_0_), channel_id=1, source_target_pairs={{0,2},{1,3},{2,0},{3,1},{4,6},{5,7},{6,4},{7,5},{8,10},{9,11},{10,... | collective-permute-start | bytes 1769480 | tf_op jit(solution)/shard_map/ppermute | solution.py:903
  116.2 10.9 %collective-permute-start.23 = (bf16[1536,768]{1,0:T(8,128)(2,1)}, bf16[1536,768]{1,0:T(8,128)(2,1)S(1)}, u32[]{:S(2)}, u32[]{:S(2)}) collective-permute-start(bf16[1536,768]{1,0:T(8,128)(2,1)} %get-tuple-element.171), channel_id=1, source_target_pairs={{0,1},{1,0},{2,3},{3,2},{4,5},{5,4},{6,7},{7,6},{8,9},{9,8},{10,11... | collective-permute-start | bytes 7077896 | tf_op jit(solution)/shard_map/ppermute | solution.py:903
  128.4 20.0 %collective-permute-start.25 = (bf16[384,768]{1,0:T(8,128)(2,1)S(1)}, bf16[384,768]{1,0:T(8,128)(2,1)S(1)}, u32[]{:S(2)}, u32[]{:S(2)}) collective-permute-start(bf16[384,768]{1,0:T(8,128)(2,1)S(1)} %get-tuple-element.185), channel_id=1, source_target_pairs={{0,2},{1,3},{2,0},{3,1},{4,6},{5,7},{6,4},{7,5},{8,10},{9,11},{10,... | collective-permute-start | bytes 1769480 | tf_op jit(solution)/shard_map/ppermute | solution.py:903
  129.5 19.0 %collective-permute-start.26 = (bf16[384,768]{1,0:T(8,128)(2,1)S(1)}, bf16[384,768]{1,0:T(8,128)(2,1)S(1)}, u32[]{:S(2)}, u32[]{:S(2)}) collective-permute-start(bf16[384,768]{1,0:T(8,128)(2,1)S(1)} %get-tuple-element.186), channel_id=1, source_target_pairs={{0,4},{1,5},{2,6},{3,7},{4,0},{5,1},{6,2},{7,3},{8,12},{9,13},{10,... | collective-permute-start | bytes 1769480 | tf_op jit(solution)/shard_map/ppermute | solution.py:903
  141.3 9.8 %collective-permute-start.24 = (bf16[768,1536]{1,0:T(8,128)(2,1)}, bf16[768,1536]{1,0:T(8,128)(2,1)S(1)}, u32[]{:S(2)}, u32[]{:S(2)}) collective-permute-start(bf16[768,1536]{1,0:T(8,128)(2,1)} %get-tuple-element.184), channel_id=1, source_target_pairs={{0,1},{1,0},{2,3},{3,2},{4,5},{5,4},{6,7},{7,6},{8,9},{9,8},{10,11... | collective-permute-start | bytes 7077896 | tf_op jit(solution)/shard_map/ppermute | solution.py:903
  149.8 21.0 %collective-permute-start.27 = (bf16[192,768]{1,0:T(8,128)(2,1)S(1)}, bf16[192,768]{1,0:T(8,128)(2,1)S(1)}, u32[]{:S(2)}, u32[]{:S(2)}) collective-permute-start(bf16[192,768]{1,0:T(8,128)(2,1)S(1)} %get-tuple-element.191), channel_id=1, source_target_pairs={{0,2},{1,3},{2,0},{3,1},{4,6},{5,7},{6,4},{7,5},{8,10},{9,11},{10,... | collective-permute-start | bytes 884744 | tf_op jit(solution)/shard_map/ppermute | solution.py:903
  150.8 20.0 %collective-permute-start.28 = (bf16[192,768]{1,0:T(8,128)(2,1)S(1)}, bf16[192,768]{1,0:T(8,128)(2,1)S(1)}, u32[]{:S(2)}, u32[]{:S(2)}) collective-permute-start(bf16[192,768]{1,0:T(8,128)(2,1)S(1)} %get-tuple-element.192), channel_id=1, source_target_pairs={{0,4},{1,5},{2,6},{3,7},{4,0},{5,1},{6,2},{7,3},{8,12},{9,13},{10,... | collective-permute-start | bytes 884744 | tf_op jit(solution)/shard_map/ppermute | solution.py:903
  153.4 31.8 %collective-permute-start.29 = (bf16[192,1536]{1,0:T(8,128)(2,1)S(1)}, bf16[192,1536]{1,0:T(8,128)(2,1)S(1)}, u32[]{:S(2)}, u32[]{:S(2)}) collective-permute-start(bf16[192,1536]{1,0:T(8,128)(2,1)S(1)} %get-tuple-element.202), channel_id=1, source_target_pairs={{0,2},{1,3},{2,0},{3,1},{4,6},{5,7},{6,4},{7,5},{8,10},{9,11},{10,... | collective-permute-start | bytes 1769480 | tf_op jit(solution)/shard_map/ppermute | solution.py:903
  154.6 30.6 %collective-permute-start.30 = (bf16[192,1536]{1,0:T(8,128)(2,1)S(1)}, bf16[192,1536]{1,0:T(8,128)(2,1)S(1)}, u32[]{:S(2)}, u32[]{:S(2)}) collective-permute-start(bf16[192,1536]{1,0:T(8,128)(2,1)S(1)} %get-tuple-element.203), channel_id=1, source_target_pairs={{0,4},{1,5},{2,6},{3,7},{4,0},{5,1},{6,2},{7,3},{8,12},{9,13},{10,... | collective-permute-start | bytes 1769480 | tf_op jit(solution)/shard_map/ppermute | solution.py:903
  172.8 10.6 %collective-permute-start.31 = (bf16[192,768]{1,0:T(8,128)(2,1)S(1)}, bf16[192,768]{1,0:T(8,128)(2,1)S(1)}, u32[]{:S(2)}, u32[]{:S(2)}) collective-permute-start(bf16[192,768]{1,0:T(8,128)(2,1)S(1)} %get-tuple-element.204), channel_id=1, source_target_pairs={{0,8},{1,9},{2,10},{3,11},{4,12},{5,13},{6,14},{7,15},{8,0},{9,1},... | collective-permute-start | bytes 884744 | tf_op jit(solution)/shard_map/ppermute | solution.py:903
  187.6 14.1 %collective-permute-start.33 = (bf16[96,1536]{1,0:T(8,128)(2,1)}, bf16[96,1536]{1,0:T(8,128)(2,1)S(1)}, u32[]{:S(2)}, u32[]{:S(2)}) collective-permute-start(bf16[96,1536]{1,0:T(8,128)(2,1)} %get-tuple-element.212), channel_id=1, source_target_pairs={{0,2},{1,3},{2,0},{3,1},{4,6},{5,7},{6,4},{7,5},{8,10},{9,11},{10,... | collective-permute-start | bytes 884744 | tf_op jit(solution)/shard_map/ppermute | solution.py:903
  188.3 13.4 %collective-permute-start.34 = (bf16[96,1536]{1,0:T(8,128)(2,1)}, bf16[96,1536]{1,0:T(8,128)(2,1)}, u32[]{:S(2)}, u32[]{:S(2)}) collective-permute-start(bf16[96,1536]{1,0:T(8,128)(2,1)} %get-tuple-element.213), channel_id=1, source_target_pairs={{0,4},{1,5},{2,6},{3,7},{4,0},{5,1},{6,2},{7,3},{8,12},{9,13},{10,... | collective-permute-start | bytes 884744 | tf_op jit(solution)/shard_map/ppermute | solution.py:903
  188.9 26.0 %all-to-all-start.2 = ((bf16[32,16,768]{2,1,0:T(8,128)(2,1)}), bf16[32,16,768]{2,1,0:T(8,128)(2,1)S(1)}, u32[]{:S(2)}, u32[]{:S(2)}) async-start(bf16[32,16,768]{2,1,0:T(8,128)(2,1)} %get-tuple-element.217), calls=%async_computation.2 | async-start | bytes 1572864 | tf_op jit(solution)/shard_map/all_to_all | solution.py:1376
  209.4 26.2 %collective-permute-start.36 = (bf16[192,1536]{1,0:T(8,128)(2,1)}, bf16[192,1536]{1,0:T(8,128)(2,1)}, u32[]{:S(2)}, u32[]{:S(2)}) collective-permute-start(bf16[192,1536]{1,0:T(8,128)(2,1)} %get-tuple-element.221), channel_id=1, source_target_pairs={{0,2},{1,3},{2,0},{3,1},{4,6},{5,7},{6,4},{7,5},{8,10},{9,11},{10,... | collective-permute-start | bytes 1769480 | tf_op jit(solution)/shard_map/ppermute | solution.py:903
  210.6 25.0 %collective-permute-start.37 = (bf16[192,1536]{1,0:T(8,128)(2,1)}, bf16[192,1536]{1,0:T(8,128)(2,1)}, u32[]{:S(2)}, u32[]{:S(2)}) collective-permute-start(bf16[192,1536]{1,0:T(8,128)(2,1)} %get-tuple-element.222), channel_id=1, source_target_pairs={{0,4},{1,5},{2,6},{3,7},{4,0},{5,1},{6,2},{7,3},{8,12},{9,13},{10,... | collective-permute-start | bytes 1769480 | tf_op jit(solution)/shard_map/ppermute | solution.py:903
  211.8 16.0 %collective-permute-start.38 = (bf16[96,1536]{1,0:T(8,128)(2,1)}, bf16[96,1536]{1,0:T(8,128)(2,1)S(1)}, u32[]{:S(2)}, u32[]{:S(2)}) collective-permute-start(bf16[96,1536]{1,0:T(8,128)(2,1)} %get-tuple-element.223), channel_id=1, source_target_pairs={{0,8},{1,9},{2,10},{3,11},{4,12},{5,13},{6,14},{7,15},{8,0},{9,1},... | collective-permute-start | bytes 884744 | tf_op jit(solution)/shard_map/ppermute | solution.py:903
  212.1 43.0 %collective-permute-start.47 = (bf16[96,768]{1,0:T(8,128)(2,1)}, bf16[96,768]{1,0:T(8,128)(2,1)}, u32[]{:S(2)}, u32[]{:S(2)}) collective-permute-start(bf16[96,768]{1,0:T(8,128)(2,1)} %copy-done.26), channel_id=1, source_target_pairs={{0,16},{1,17},{2,18},{3,19},{4,20},{5,21},{6,22},{7,23},{8,24},{9,... | collective-permute-start | bytes 442376 | tf_op jit(solution)/shard_map/ppermute | solution.py:903
  223.6 19.7 %all-to-all-start.3 = ((bf16[32,8,768]{2,1,0:T(8,128)(2,1)}), bf16[32,8,768]{2,1,0:T(8,128)(2,1)S(1)}, u32[]{:S(2)}, u32[]{:S(2)}) async-start(bf16[32,8,768]{2,1,0:T(8,128)(2,1)} %get-tuple-element.231), calls=%async_computation.3 | async-start | bytes 786432 | tf_op jit(solution)/shard_map/all_to_all | solution.py:1435
  229.7 19.7 %collective-permute-start.45 = (bf16[48,1536]{1,0:T(8,128)(2,1)S(1)}, bf16[48,1536]{1,0:T(8,128)(2,1)}, u32[]{:S(2)}, u32[]{:S(2)}) collective-permute-start(bf16[48,1536]{1,0:T(8,128)(2,1)S(1)} %get-tuple-element.253), channel_id=1, source_target_pairs={{0,16},{1,17},{2,18},{3,19},{4,20},{5,21},{6,22},{7,23},{8,24},{9,... | collective-permute-start | bytes 442376 | tf_op jit(solution)/shard_map/ppermute | solution.py:903
  232.0 30.2 %collective-permute-start.35 = (bf16[384,768]{1,0:T(8,128)(2,1)}, bf16[384,768]{1,0:T(8,128)(2,1)}, u32[]{:S(2)}, u32[]{:S(2)}) collective-permute-start(bf16[384,768]{1,0:T(8,128)(2,1)} %get-tuple-element.218), channel_id=1, source_target_pairs={{0,1},{1,2},{2,3},{3,4},{4,5},{5,6},{6,7},{7,8},{8,9},{9,10},{10,1... | collective-permute-start | bytes 1769480 | tf_op jit(solution)/shard_map/ppermute | solution.py:1445
  238.4 18.4 %collective-permute-start.39 = (bf16[96,1536]{1,0:T(8,128)(2,1)S(1)}, bf16[96,1536]{1,0:T(8,128)(2,1)S(1)}, u32[]{:S(2)}, u32[]{:S(2)}) collective-permute-start(bf16[96,1536]{1,0:T(8,128)(2,1)S(1)} %get-tuple-element.228), channel_id=1, source_target_pairs={{0,2},{1,3},{2,0},{3,1},{4,6},{5,7},{6,4},{7,5},{8,10},{9,11},{10,... | collective-permute-start | bytes 884744 | tf_op jit(solution)/shard_map/ppermute | solution.py:903
  239.6 17.1 %collective-permute-start.40 = (bf16[96,1536]{1,0:T(8,128)(2,1)S(1)}, bf16[96,1536]{1,0:T(8,128)(2,1)S(1)}, u32[]{:S(2)}, u32[]{:S(2)}) collective-permute-start(bf16[96,1536]{1,0:T(8,128)(2,1)S(1)} %get-tuple-element.229), channel_id=1, source_target_pairs={{0,4},{1,5},{2,6},{3,7},{4,0},{5,1},{6,2},{7,3},{8,12},{9,13},{10,... | collective-permute-start | bytes 884744 | tf_op jit(solution)/shard_map/ppermute | solution.py:903
  250.4 18.2 %all-to-all-start.4 = ((bf16[32,32,128]{2,1,0:T(8,128)(2,1)}), bf16[32,32,128]{2,1,0:T(8,128)(2,1)S(1)}, u32[]{:S(2)}, u32[]{:S(2)}) async-start(bf16[32,32,128]{2,1,0:T(8,128)(2,1)} %get-tuple-element.241), calls=%async_computation.4 | async-start | bytes 524288 | tf_op jit(solution)/shard_map/all_to_all | solution.py:1461
  254.1 13.8 %collective-permute-start.46 = (f32[24,1536]{1,0:T(8,128)S(1)}, f32[24,1536]{1,0:T(8,128)S(1)}, u32[]{:S(2)}, u32[]{:S(2)}) collective-permute-start(f32[24,1536]{1,0:T(8,128)S(1)} %get-tuple-element.257), channel_id=1, source_target_pairs={{0,1},{1,0},{2,3},{3,2},{4,5},{5,4},{6,7},{7,6},{8,9},{9,8},{10,11... | collective-permute-start | bytes 442376 | tf_op jit(solution)/shard_map/ppermute | solution.py:903
  259.5 11.1 %collective-permute-start.41 = (bf16[48,1536]{1,0:T(8,128)(2,1)S(1)}, bf16[48,1536]{1,0:T(8,128)(2,1)S(1)}, u32[]{:S(2)}, u32[]{:S(2)}) collective-permute-start(bf16[48,1536]{1,0:T(8,128)(2,1)S(1)} %get-tuple-element.248), channel_id=1, source_target_pairs={{0,8},{1,9},{2,10},{3,11},{4,12},{5,13},{6,14},{7,15},{8,0},{9,1},... | collective-permute-start | bytes 442376 | tf_op jit(solution)/shard_map/ppermute | solution.py:903
  259.5 11.0 %collective-permute-start.42 = (bf16[48,1536]{1,0:T(8,128)(2,1)S(1)}, bf16[48,1536]{1,0:T(8,128)(2,1)S(1)}, u32[]{:S(2)}, u32[]{:S(2)}) collective-permute-start(bf16[48,1536]{1,0:T(8,128)(2,1)S(1)} %get-tuple-element.249), channel_id=1, source_target_pairs={{0,16},{1,17},{2,18},{3,19},{4,20},{5,21},{6,22},{7,23},{8,24},{9,... | collective-permute-start | bytes 442376 | tf_op jit(solution)/shard_map/ppermute | solution.py:903
  261.9 13.3 %collective-permute-start.43 = (bf16[48,1536]{1,0:T(8,128)(2,1)S(1)}, bf16[48,1536]{1,0:T(8,128)(2,1)S(1)}, u32[]{:S(2)}, u32[]{:S(2)}) collective-permute-start(bf16[48,1536]{1,0:T(8,128)(2,1)S(1)} %get-tuple-element.250), channel_id=1, source_target_pairs={{0,24},{1,25},{2,26},{3,27},{4,28},{5,29},{6,30},{7,31},{8,16},{9,... | collective-permute-start | bytes 442376 | tf_op jit(solution)/shard_map/ppermute | solution.py:903
  (43 other events, 766.4 us)
